TPU v7x, 32 devices: a whole 2x2x4 slice. The times are simulated.
32 devices in a mesh: st: 2 (over x), fsdp: 16 (over z, y, core).
Axes of the slice: x: 2, y: 2, z: 4, core: 2. Of those that a mesh axis runs over, the one named last changes fastest.
Arguments:
- normed: bfloat16 [16, 512, 3072], P('fsdp')
- qkv_weight: bfloat16 [3072, 8, 384], P('fsdp', 'st'), may hold values from -0.109375 to 0.109375
- out_weight: bfloat16 [3072, 1024], P('fsdp', 'st'), may hold values from -0.1875 to 0.1875
- segment_ids: int32 [16], replicated, may hold values from 0 to 3, never falling along the last dimension, each value on 1 to 8 neighbouring positions
Outputs:
- attended: bfloat16 [16, 512, 3072], P('fsdp', 'st')
Inputs may be any that keep to these rules, and one draw needn't show every extreme that they name: `segment_ids`: segment ids never fall from one frame to the next; each clip covers 1 to 8 consecutive frames, and one covers exactly 8.
All inputs are finite; a program needn't handle non-finite values.
Results may differ from a plain program's by a relative error of at most 0.017.
Values may be sent and summed in bfloat16 or wider, within the bound.
No kernel may reach another device: no remote copies, remote signals or barrier semaphores. Data moves between devices by JAX's collectives and lax.ppermute only.
A program may use at most 64 MiB of HBM per device.

v0:
```python
import math

import jax
import jax.numpy as jnp
from jax import lax
from jax.sharding import PartitionSpec as P

HEAD = 128
HS_DEV = 2


def softmax_rows(scores):
    top = jnp.max(scores, axis=-1, keepdims=True)
    expo = jnp.exp(scores - top)
    return expo / jnp.sum(expo, axis=-1, keepdims=True)


def shards(normed, qkv_weight, out_weight, segment_ids):
    patches = normed.shape[1]
    width = normed.shape[2]
    group = qkv_weight.shape[1]
    scale = 1.0 / math.sqrt(HEAD)
    frame_rows = normed.reshape(patches, width)
    projected = jnp.einsum(
        "pd,dhc->phc",
        frame_rows,
        lax.all_gather(qkv_weight, "fsdp", axis=0, tiled=True),
        preferred_element_type=jnp.float32,
    )
    out_full = lax.all_gather(out_weight, "fsdp", axis=0, tiled=True)
    packed = projected.astype(jnp.bfloat16)
    spatial = packed[:, :HS_DEV]
    scores = (
        jnp.einsum(
            "qhc,khc->hqk",
            spatial[..., :HEAD],
            spatial[..., HEAD : 2 * HEAD],
            preferred_element_type=jnp.float32,
        )
        * scale
    )
    weights = softmax_rows(scores).astype(jnp.bfloat16)
    spatial_out = jnp.einsum(
        "hqk,khc->qhc", weights, spatial[..., 2 * HEAD :], preferred_element_type=jnp.float32
    ).astype(jnp.bfloat16)
    temporal_in = packed[:, HS_DEV:].reshape(1, patches, group - HS_DEV, 3 * HEAD)
    block = lax.all_to_all(temporal_in, "fsdp", split_axis=1, concat_axis=0, tiled=True)
    query = block[..., :HEAD]
    keys = block[..., HEAD : 2 * HEAD]
    values = block[..., 2 * HEAD :]
    all_scores = (
        jnp.einsum("tphc,uphc->phtu", query, keys, preferred_element_type=jnp.float32) * scale
    )
    same = segment_ids[:, None] == segment_ids[None, :]
    all_scores = jnp.where(same, all_scores, jnp.float32(-1e30))
    all_weights = softmax_rows(all_scores).astype(jnp.bfloat16)
    result = jnp.einsum("phtu,uphc->tphc", all_weights, values, preferred_element_type=jnp.float32)
    temporal_out = lax.all_to_all(
        result.astype(jnp.bfloat16), "fsdp", split_axis=0, concat_axis=1, tiled=True
    )
    heads_out = jnp.concatenate(
        [spatial_out, temporal_out.reshape(patches, group - HS_DEV, HEAD)], axis=1
    )
    heads_out = heads_out.reshape(patches, group * HEAD)
    summed = lax.psum_scatter(
        lax.dot_general(
            heads_out, out_full, (((1,), (1,)), ((), ())), preferred_element_type=jnp.float32
        ).astype(jnp.bfloat16),
        "st",
        scatter_dimension=0,
        tiled=True,
    ).astype(jnp.float32)
    return summed.astype(jnp.bfloat16).reshape(1, summed.shape[0], width)


def solution(mesh):
    return jax.shard_map(
        shards,
        mesh=mesh,
        in_specs=(P("fsdp", None, None), P("fsdp", "st", None), P("fsdp", "st"), P()),
        out_specs=P("fsdp", "st", None),
        check_vma=False,
    )
```

profile of v0, /device:TPU:0, one launch (start us, length us, event | category | flops | bytes accessed | tf_op | source)
XLA Modules:
  0.0 214.5 jit_solution(15877828504189771126)
XLA Ops:
  6.5 0.0 copy-start
  6.5 0.0 all-gather.3.cloned.1.call-start
  6.5 2.1 copy.30
  8.6 0.0 all-gather.3.cloned.1.call-update
  8.7 0.0 all-gather.5.cloned.1.call-start
  8.7 0.7 all-gather.5.cloned.1.call-update
  9.4 84.4 %all-gather.3.cloned.1.call-done = bf16[3072,4,384]{2,0,1:T(8,128)(2,1)} async-done(((bf16[192,4,384]{2,0,1:T(8,128)(2,1)}), bf16[3072,4,384]{2,0,1:T(8,128)(2,1)}) %all-gather.3.cloned.1.call-update) | async-done | bytes 9437200 | tf_op jit(solution)/shard_map/all_gather | solution.py:27
  93.8 0.0 copy-done
  93.9 7.8 %fusion.5 = bf16[512,4,384]{2,0,1:T(8,128)(2,1)S(1)} fusion(bf16[3072,4,384]{2,0,1:T(8,128)(2,1)} %all-gather.3.cloned.1.call-done, bf16[1,512,3072]{2,1,0:T(8,128)(2,1)S(1)} %copy-done), kind=kOutput, calls=%fused_computation.9 | convolution fusion | flops 4832624640 | bytes 14155776 | tf_op jit(solution)/shard_map/pd,dhc->phc/dot_general | solution.py:24
  101.6 0.0 copy-start.1
  101.6 1.1 copy-done.1
  102.8 0.0 copy-start.2
  102.8 0.1 slice_bitcast_fusion
  102.8 1.7 copy.33
  104.6 4.3 %all-to-all-start = ((bf16[1,512,2,384]{3,2,0,1:T(2,128)(2,1)}), bf16[1,512,2,384]{3,2,0,1:T(2,128)(2,1)}, u32[]{:S(2)}, u32[]{:S(2)}) async-start(bf16[1,512,2,384]{3,2,0,1:T(2,128)(2,1)} %copy.33), calls=%async_computation | async-start | bytes 1572864 | tf_op jit(solution)/shard_map/all_to_all | solution.py:47
  108.9 0.0 copy-done.2
  108.9 0.1 broadcast_compare_fusion
  108.9 20.0 %all-to-all-done = bf16[1,512,2,384]{3,2,0,1:T(2,128)(2,1)} async-done(((bf16[1,512,2,384]{3,2,0,1:T(2,128)(2,1)}), bf16[1,512,2,384]{3,2,0,1:T(2,128)(2,1)}, u32[]{:S(2)}, u32[]{:S(2)}) %all-to-all-start) | async-done | bytes 786464 | tf_op jit(solution)/shard_map/all_to_all | solution.py:47
  128.9 1.2 copy.34
  130.2 0.9 fusion.51
  131.0 0.3 fusion.10
  131.3 0.0 copy-start.3
  131.3 0.2 fusion.52
  131.6 0.5 copy-done.3
  132.1 1.6 fusion.11
  133.8 0.9 copy.39
  134.7 13.2 %all-to-all-start.1 = ((bf16[16,32,2,128]{3,2,1,0:T(2,128)(2,1)}), bf16[16,32,2,128]{3,2,1,0:T(2,128)(2,1)S(1)}, u32[]{:S(2)}, u32[]{:S(2)}) async-start(bf16[16,32,2,128]{3,2,1,0:T(2,128)(2,1)} %copy.39), calls=%async_computation.1 | async-start | bytes 524288 | tf_op jit(solution)/shard_map/all_to_all | solution.py:58
  147.9 0.0 reduce-scatter.2.cloned.1.call-start
  148.0 1.8 fusion.53
  149.8 2.9 %fusion.12 = bf16[512,2,128]{0,2,1:T(8,128)(2,1)} fusion(f32[2,512]{1,0:T(2,128)S(1)} %fusion.53, bf16[512,4,384]{2,0,1:T(8,128)(2,1)} %copy-done.1), kind=kOutput, calls=%fused_computation.17 | convolution fusion | flops 270665216 | bytes 1052672 | tf_op jit(solution)/shard_map/hqk,khc->qhc/dot_general | solution.py:43
  152.8 5.2 %all-to-all-done.1 = bf16[16,32,2,128]{3,2,1,0:T(2,128)(2,1)S(1)} async-done(((bf16[16,32,2,128]{3,2,1,0:T(2,128)(2,1)}), bf16[16,32,2,128]{3,2,1,0:T(2,128)(2,1)S(1)}, u32[]{:S(2)}, u32[]{:S(2)}) %all-to-all-start.1) | async-done | bytes 262176 | tf_op jit(solution)/shard_map/all_to_all | solution.py:58
  158.0 0.9 copy.41
  158.8 1.9 pad_maximum_fusion
  160.7 0.0 all-gather.5.cloned.1.call-done
  160.7 5.6 %convolution_convert_fusion = bf16[512,3072]{1,0:T(8,128)(2,1)} fusion(bf16[512,512]{0,1:T(8,128)(2,1)} %bitcast.23, bf16[3072,512]{1,0:T(8,128)(2,1)} %all-gather.5.cloned.1.call-done), kind=kOutput, calls=%fused_computation.2 | convolution fusion | flops 1612185600 | bytes 6815744 | tf_op jit(solution)/shard_map/dot_general | solution.py:66
  166.3 0.0 reduce-scatter.2.cloned.1.call-update
  166.3 41.6 %reduce-scatter.2.cloned.1.call-done = bf16[256,3072]{1,0:T(8,128)(2,1)} async-done(((bf16[512,3072]{1,0:T(8,128)(2,1)}), bf16[256,3072]{1,0:T(8,128)(2,1)}) %reduce-scatter.2.cloned.1.call-update) | async-done | bytes 1572880 | tf_op jit(solution)/shard_map/reduce_scatter | solution.py:65
Async XLA Ops:
  6.5 87.3 %copy-start = (bf16[1,512,3072]{2,1,0:T(8,128)(2,1)S(1)}, bf16[1,512,3072]{2,1,0:T(8,128)(2,1)}, u32[]{:S(2)}) copy-start(bf16[1,512,3072]{2,1,0:T(8,128)(2,1)} %param.4) | copy-start | bytes 9437188
  6.5 87.3 %all-gather.3.cloned.1.call-start = ((), (), s32[]{:S(2)}) async-start(), calls=%async_computation.3 | async-start | bytes 10027008 | tf_op jit(solution)/shard_map/all_gather | solution.py:27
  8.7 152.0 %all-gather.5.cloned.1.call-start = ((), (), s32[]{:S(2)}) async-start(), calls=%async_computation.4 | async-start | bytes 3342336 | tf_op jit(solution)/shard_map/all_gather | solution.py:30
  101.6 1.1 copy-start.1
  102.8 6.1 %copy-start.2 = (s32[16]{0:T(128)S(1)}, s32[16]{0:T(128)}, u32[]{:S(2)}) copy-start(s32[16]{0:T(128)} %param.7) | copy-start | bytes 196
  104.6 24.4 %all-to-all-start = ((bf16[1,512,2,384]{3,2,0,1:T(2,128)(2,1)}), bf16[1,512,2,384]{3,2,0,1:T(2,128)(2,1)}, u32[]{:S(2)}, u32[]{:S(2)}) async-start(bf16[1,512,2,384]{3,2,0,1:T(2,128)(2,1)} %copy.33), calls=%async_computation | async-start | bytes 1572864 | tf_op jit(solution)/shard_map/all_to_all | solution.py:47
  131.3 0.8 copy-start.3
  134.7 23.3 %all-to-all-start.1 = ((bf16[16,32,2,128]{3,2,1,0:T(2,128)(2,1)}), bf16[16,32,2,128]{3,2,1,0:T(2,128)(2,1)S(1)}, u32[]{:S(2)}, u32[]{:S(2)}) async-start(bf16[16,32,2,128]{3,2,1,0:T(2,128)(2,1)} %copy.39), calls=%async_computation.1 | async-start | bytes 524288 | tf_op jit(solution)/shard_map/all_to_all | solution.py:58
  147.9 60.0 %reduce-scatter.2.cloned.1.call-start = ((), (), s32[]{:S(2)}) async-start(), calls=%async_computation.5 | async-start | bytes 4718592 | tf_op jit(solution)/shard_map/reduce_scatter | solution.py:65
Sparse Core Ops, SparseCore 0:
  9.6 84.1 all-gather.2
  96.1 49.3 all-gather.4
  166.4 41.4 reduce-scatter.1
where the time goes:
time: 215 us; the launch traced here: 214 us
  waiting for transfers between devices  152 us (71%)
  matrix products  20.1 us (9%)
  starting transfers between devices  17.6 us (8%)
  between operations  13.2 us (6%)
  local copies, waits for them, and re-layouts  9.48 us (4%)
  other arithmetic  2.18 us (1%)
    all_gather x1, waiting for transfers between devices, shards(): lax.all_gather(qkv_weight, 'fsdp', axis=0, tiled=True)  84.4 us
    reduce_scatter x1, waiting for transfers between devices, shards(): lax.psum_scatter(lax.dot_general(heads_out, out_full, (((1,), (1,)), ((),...  41.6 us
    all_to_all x1, waiting for transfers between devices, shards(): lax.all_to_all(temporal_in, 'fsdp', split_axis=1, concat_axis=0, tiled=True)  20 us
    all_to_all x1, starting transfers between devices, shards(): lax.all_to_all(result.astype(jnp.bfloat16), 'fsdp', split_axis=0, concat_...  13.2 us
    dot_general x1, matrix products, shards(): jnp.einsum('pd,dhc->phc', frame_rows, lax.all_gather(qkv_weight, 'fsdp',...  7.75 us
    dot_general x1, matrix products, shards(): lax.dot_general(heads_out, out_full, (((1,), (1,)), ((), ())), preferred_...  5.58 us
    all_to_all x1, waiting for transfers between devices, shards(): lax.all_to_all(result.astype(jnp.bfloat16), 'fsdp', split_axis=0, concat_...  5.22 us
  transfers between devices with their start and end apart: 5, of which 4 were waited for; matrix products, arithmetic and copies ran while one was open for 10% of the time, Pallas kernels for 0%

commit v1 on v0

v1 whole, which is shorter than its diff:
```python
import functools
import math

import jax
import jax.numpy as jnp
from jax import lax
from jax.experimental import pallas as pl
from jax.experimental.pallas import tpu as pltpu
from jax.sharding import PartitionSpec as P

HEAD = 128
HS_DEV = 2
SCALE = 1.0 / math.sqrt(HEAD)
VMEM_LIMIT = 40 * 1024 * 1024


def vmem_call(body, out_shape, args, flops, name):
    bytes_moved = sum(a.size * a.dtype.itemsize for a in args)
    return pl.pallas_call(
        body,
        out_shape=out_shape,
        in_specs=[
            pl.BlockSpec(memory_space=pltpu.SMEM if a.dtype == jnp.int32 else pltpu.VMEM)
            for a in args
        ],
        out_specs=pl.BlockSpec(memory_space=pltpu.VMEM),
        compiler_params=pltpu.CompilerParams(vmem_limit_bytes=VMEM_LIMIT),
        cost_estimate=pl.CostEstimate(flops=flops, bytes_accessed=bytes_moved, transcendentals=0),
        name=name,
    )(*args)


def spatial_body(qkv_ref, out_ref):
    patches = qkv_ref.shape[0] // 2
    for frame in range(2):
        rows = pl.ds(frame * patches, patches)
        query = qkv_ref[rows, :HEAD]
        keys = qkv_ref[rows, HEAD : 2 * HEAD]
        values = qkv_ref[rows, 2 * HEAD :]
        scores = lax.dot_general(
            query, keys, (((1,), (1,)), ((), ())), preferred_element_type=jnp.float32
        )
        scores = scores * SCALE
        expo = jnp.exp(scores - jnp.max(scores, axis=-1, keepdims=True))
        total = jnp.sum(expo, axis=-1, keepdims=True)
        result = jnp.dot(expo.astype(jnp.bfloat16), values, preferred_element_type=jnp.float32)
        out_ref[rows, :] = (result / total).astype(jnp.bfloat16)


def temporal_body(tile, meta_ref, qkv_ref, out_ref):
    frames, rows = qkv_ref.shape[0], qkv_ref.shape[1]
    flip = meta_ref[frames]
    size = frames * tile
    row_at = lax.broadcasted_iota(jnp.int32, (size, size), 0)
    col_at = lax.broadcasted_iota(jnp.int32, (size, size), 1)
    row_seg = jnp.zeros((size, 1), jnp.int32)
    col_seg = jnp.zeros((1, size), jnp.int32)
    row_frame = lax.broadcasted_iota(jnp.int32, (size, 1), 0) // tile
    col_frame = lax.broadcasted_iota(jnp.int32, (1, size), 1) // tile
    for frame in range(frames):
        clip = meta_ref[frame]
        row_seg = jnp.where(row_frame == frame, clip, row_seg)
        col_seg = jnp.where(col_frame == frame, clip, col_seg)
    keep = (row_at % tile == col_at % tile) & (row_seg == col_seg)
    for start in range(0, rows, tile):
        block = qkv_ref[:, start : start + tile, :].reshape(size, 3 * HEAD)
        scores = lax.dot_general(
            block[:, :HEAD],
            block[:, HEAD : 2 * HEAD],
            (((1,), (1,)), ((), ())),
            preferred_element_type=jnp.float32,
        )
        scores = jnp.where(keep, scores * SCALE, jnp.float32(-1e30))
        expo = jnp.exp(scores - jnp.max(scores, axis=-1, keepdims=True))
        total = jnp.sum(expo, axis=-1, keepdims=True)
        result = jnp.dot(
            expo.astype(jnp.bfloat16), block[:, 2 * HEAD :], preferred_element_type=jnp.float32
        )
        result = (result / total).astype(jnp.bfloat16).reshape(frames, tile, HEAD)
        for pair in range(frames // 2):
            out_ref[2 * pair + flip, start : start + tile, :] = result[2 * pair]
            out_ref[2 * pair + 1 - flip, start : start + tile, :] = result[2 * pair + 1]


def shards(n_st, n_fsdp, normed, qkv_weight, out_weight, segment_ids):
    patches, width = normed.shape[1], normed.shape[2]
    frames = n_fsdp
    depth = qkv_weight.shape[0]
    chips = n_fsdp // 2
    ring = list(range(0, chips, 2)) + list(range(chips - 1, 0, -2))
    place = [ring.index(chip) for chip in range(chips)]
    me = lax.axis_index("fsdp")
    st = lax.axis_index("st")
    chip, core = me // 2, me % 2
    spot = jnp.array(place, jnp.int32)[chip]
    ring_table = jnp.array(ring, jnp.int32)

    swap = [(i, i ^ 1) for i in range(n_fsdp)]
    forward = [
        (2 * ring[i] + c, 2 * ring[(i + 1) % chips] + c) for i in range(chips) for c in range(2)
    ]
    backward = [(b, a) for a, b in forward]

    def to_core(x):
        return lax.ppermute(x, "fsdp", swap)

    def by_core(mine, other, axis):
        return jnp.where(
            core == 0,
            jnp.concatenate([mine, other], axis=axis),
            jnp.concatenate([other, mine], axis=axis),
        )

    def st_exchange(x):
        if n_st != 2:
            return lax.all_to_all(x, "st", split_axis=0, concat_axis=0, tiled=True)
        mine = lax.dynamic_slice_in_dim(x, st, 1, 0)
        other = lax.dynamic_slice_in_dim(x, 1 - st, 1, 0)
        other = lax.ppermute(other, "st", [(0, 1), (1, 0)])
        return jnp.where(
            st == 0, jnp.concatenate([mine, other]), jnp.concatenate([other, mine])
        )

    def st_gather(x):
        if n_st != 2:
            return lax.all_gather(x, "st", axis=1, tiled=True)
        other = lax.ppermute(x, "st", [(0, 1), (1, 0)])
        return jnp.where(
            st == 0,
            jnp.concatenate([x, other], axis=1),
            jnp.concatenate([other, x], axis=1),
        )

    def ring_gather(piece):
        groups = [[piece]]
        ahead = behind = piece
        for _ in range(chips // 2 - 1):
            ahead = lax.ppermute(ahead, "fsdp", forward)
            behind = lax.ppermute(behind, "fsdp", backward)
            groups.append([ahead, behind])
        half = piece.shape[0] // 2
        ahead = lax.ppermute(ahead[:half], "fsdp", forward)
        behind = lax.ppermute(behind[half:], "fsdp", backward)
        groups.append([jnp.concatenate([ahead, behind])])
        return groups

    offsets = [0]
    for d in range(1, chips // 2):
        offsets += [chips - d, d]
    offsets.append(chips // 2)
    sources = [ring_table[(spot + d) % chips] for d in offsets]

    def take_head(first):
        mine = lax.dynamic_slice_in_dim(qkv_weight, first + core, 1, 1)[:, 0]
        other = lax.dynamic_slice_in_dim(qkv_weight, first + 1 - core, 1, 1)[:, 0]
        return by_core(mine, to_core(other), 1)

    temporal_piece = take_head(HS_DEV)
    own = normed.reshape(patches, width)
    rows = jnp.concatenate([own, to_core(own)])
    spatial_piece = take_head(0)
    chip_width = 2 * depth
    rows = jnp.concatenate(
        [lax.dynamic_slice_in_dim(rows, s * chip_width, chip_width, 1) for s in sources], axis=1
    )

    def project(pieces):
        weight = jnp.concatenate(
            [p[:, k * 3 * HEAD : (k + 1) * 3 * HEAD] for p in pieces for k in range(2)]
        )
        return jnp.dot(rows, weight, preferred_element_type=jnp.float32).astype(jnp.bfloat16)

    groups = ring_gather(temporal_piece)
    temporal = project([p for g in groups for p in g])
    part = patches // (n_st * chips)
    temporal = temporal.reshape(2, n_st, chips, part, 3 * HEAD).transpose(2, 0, 1, 3, 4)
    same_core = [[2 * i + c for i in range(chips)] for c in range(2)]
    temporal = lax.all_to_all(
        temporal,
        "fsdp",
        split_axis=0,
        concat_axis=0,
        tiled=True,
        axis_index_groups=same_core,
    ).reshape(frames, n_st * part, 3 * HEAD)
    pairs = segment_ids.reshape(chips, 2)
    pairs = jnp.where(core == 0, pairs, pairs[:, ::-1]).reshape(frames)
    meta = jnp.concatenate([pairs, core.reshape(1)]).astype(jnp.int32)
    tile = max(1, 256 // frames)
    tile = min(n_st * part, max(16, tile))
    result = vmem_call(
        functools.partial(temporal_body, tile),
        jax.ShapeDtypeStruct((frames, n_st * part, HEAD), jnp.bfloat16),
        [meta, temporal],
        4 * frames * frames * n_st * part * tile * HEAD,
        "temporal_attention",
    )
    result = result.reshape(frames, n_st, part, HEAD).transpose(1, 0, 2, 3)
    result = lax.all_to_all(
        result.reshape(n_st * frames, part, HEAD),
        ("st", "fsdp"),
        split_axis=0,
        concat_axis=0,
        tiled=True,
    )
    result = result.reshape(n_st, chips, 2, part, HEAD).transpose(1, 3, 0, 2, 4)
    temporal_heads = result.reshape(patches // n_st, n_st, 2, HEAD)

    groups = ring_gather(jnp.concatenate([spatial_piece, out_weight], axis=1))
    split = spatial_piece.shape[1]
    out_pieces = [
        st_gather(jnp.concatenate([p[:, split:] for p in g]) if len(g) > 1 else g[0][:, split:])
        for g in groups
    ]
    out_mine = jnp.concatenate(out_pieces)
    out_other = to_core(out_mine)
    spatial = project([p[:, :split] for g in groups for p in g])
    spatial = vmem_call(
        spatial_body,
        jax.ShapeDtypeStruct((2 * patches, HEAD), jnp.bfloat16),
        [spatial],
        8 * patches * patches * HEAD,
        "spatial_attention",
    )
    spatial = spatial.reshape(2, n_st, patches // n_st, HEAD).transpose(1, 0, 2, 3)
    spatial = st_exchange(spatial)
    mine, other = spatial[:, 0], to_core(spatial[:, 1])
    spatial_heads = by_core(mine[:, :, None], other[:, :, None], 2).transpose(1, 0, 2, 3)

    heads = jnp.concatenate([spatial_heads, temporal_heads], axis=2)
    heads = heads.reshape(patches // n_st, n_st * 4 * HEAD)
    out_all = by_core(
        out_mine.reshape(chips, 1, depth, -1), out_other.reshape(chips, 1, depth, -1), 1
    )
    out_all = out_all.reshape(width, -1)
    attended = lax.dot_general(
        heads, out_all, (((1,), (1,)), ((), ())), preferred_element_type=jnp.float32
    ).astype(jnp.bfloat16)
    home = [offsets.index(d) for d in range(chips)]
    home_table = jnp.array(home, jnp.int32)
    place_table = jnp.array(place, jnp.int32)
    blocks = []
    for q in range(chips):
        at = home_table[(place_table[q] - spot + chips) % chips]
        blocks.append(lax.dynamic_slice_in_dim(attended, at * chip_width, chip_width, 1))
    attended = jnp.concatenate(blocks, axis=1)
    return attended.reshape(1, patches // n_st, width)


def solution(mesh):
    return jax.shard_map(
        functools.partial(shards, mesh.shape["st"], mesh.shape["fsdp"]),
        mesh=mesh,
        in_specs=(P("fsdp", None, None), P("fsdp", "st", None), P("fsdp", "st"), P()),
        out_specs=P("fsdp", "st", None),
        check_vma=False,
    )
```

time: 215 us -> 172 us (0.80)
  waiting for transfers between devices: 152 us -> 66.5 us
  starting transfers between devices: 17.6 us -> 35.4 us
  other arithmetic: 2.18 us -> 17.3 us
  between operations: 13.2 us -> 22.2 us
  matrix products: 20.1 us -> 12.2 us
  local copies, waits for them, and re-layouts: 9.48 us -> 15.1 us
  Pallas kernels: 0 us -> 2.49 us
    all_gather x2 -> x0, waiting for transfers between devices: 84.4 us -> none  [the longest x1 84.4 us: shards(): lax.all_gather(qkv_weight, 'fsdp', axis=0, tiled=True)]
    ppermute x0 -> x27, waiting for transfers between devices: none -> 51.3 us  [the longest x6 19.9 us: ring_gather(): ahead = lax.ppermute(ahead, 'fsdp', forward)]
    reduce_scatter x1 -> x0, waiting for transfers between devices: 41.6 us -> none  [shards(): lax.psum_scatter(lax.dot_general(heads_out, out_full, (((1,), (1,)), ((),...]
    ppermute x0 -> x27, starting transfers between devices: none -> 27.1 us  [the longest x6 9.61 us: ring_gather(): ahead = lax.ppermute(ahead, 'fsdp', forward)]
    all_to_all x2, waiting for transfers between devices: 25.2 us -> 15.2 us  [the longest x1 10.4 us: shards(): lax.all_to_all(temporal, 'fsdp', split_axis=0, concat_axis=0, tiled=True,...]
    all_to_all x2, starting transfers between devices: 17.5 us -> 8.3 us  [the longest x1 5.57 us: shards(): lax.all_to_all(temporal, 'fsdp', split_axis=0, concat_axis=0, tiled=True,...]
    select_n x0 -> x5, other arithmetic: none -> 7.9 us  [the longest x3 7.87 us: by_core(): jnp.where(core == 0, jnp.concatenate([mine, other], axis=axis), jnp.conca...]
    unnamed x0 -> x11, other arithmetic: none -> 7.06 us
  transfers between devices with their start and end apart: 5 -> 29, of which waited for: 4 -> 13; matrix products, arithmetic and copies ran while one was open for 10% -> 18% of each run, Pallas kernels for 0% -> 1%
where the time goes in v1:
time: 172 us; the launch traced here: 171 us
  waiting for transfers between devices  66.5 us (39%)
  starting transfers between devices  35.4 us (21%)
  between operations  22.2 us (13%)
  other arithmetic  17.3 us (10%)
  local copies, waits for them, and re-layouts  15.1 us (9%)
  matrix products  12.2 us (7%)
  Pallas kernels  2.49 us (1%)
    ppermute x6, waiting for transfers between devices, ring_gather(): ahead = lax.ppermute(ahead, 'fsdp', forward)  19.9 us
    ppermute x6, waiting for transfers between devices, ring_gather(): behind = lax.ppermute(behind, 'fsdp', backward)  19.2 us
    all_to_all x1, waiting for transfers between devices, shards(): lax.all_to_all(temporal, 'fsdp', split_axis=0, concat_axis=0, tiled=True,...  10.4 us
    dot_general x2, matrix products, project(): jnp.dot(rows, weight, preferred_element_type=jnp.float32)  10.3 us
    ppermute x6, starting transfers between devices, ring_gather(): ahead = lax.ppermute(ahead, 'fsdp', forward)  9.61 us
    ppermute x5, waiting for transfers between devices, st_gather(): other = lax.ppermute(x, 'st', [(0, 1), (1, 0)])  8.81 us
    select_n x3, other arithmetic, by_core(): jnp.where(core == 0, jnp.concatenate([mine, other], axis=axis), jnp.conca...  7.87 us
    ppermute x5, starting transfers between devices, st_gather(): other = lax.ppermute(x, 'st', [(0, 1), (1, 0)])  7.2 us
  transfers between devices with their start and end apart: 29, of which 13 were waited for; matrix products, arithmetic and copies ran while one was open for 18% of the time, Pallas kernels for 1%

profile of v1, /device:TPU:0, one launch (start us, length us, event | category | flops | bytes accessed | tf_op | source)
XLA Modules:
  0.0 171.1 jit_solution(3760178028099097455)
XLA Ops:
  0.0 3.7 %constant_dynamic-slice_fusion.3 = (bf16[192,1,384]{2,1,0:T(2,128)(2,1)S(1)}, bf16[192,1,384]{2,1,0:T(2,128)(2,1)}, bf16[192,1,384]{2,1,0:T(2,128)(2,1)S(1)}, bf16[192,1,384]{2,1,0:T(2,128)(2,1)S(1)}) fusion(bf16[192,4,384]{2,1,0:T(4,128)(2,1)} %param.9, s32[]{:T(128)S(6)} %select_n.304, s32[]{:T(128)S(6)} %select_n.313, s32[]{:T(128)S(6)} %select_n.305, ...), kind=kLoop, calls=%fused_computation.112 | loop fusion | bytes 1179664 | tf_op jit(solution)/shard_map/dynamic_slice | solution.py:154
  3.7 0.7 copy.45
  4.4 0.5 collective-permute-start.12
  4.9 0.7 copy.47
  5.6 0.5 collective-permute-start.1
  6.0 2.5 %collective-permute-start.21 = (bf16[192,512]{1,0:T(8,128)(2,1)}, bf16[192,512]{1,0:T(8,128)(2,1)}, u32[]{:S(2)}, u32[]{:S(2)}) collective-permute-start(bf16[192,512]{1,0:T(8,128)(2,1)} %param.10), channel_id=1, source_target_pairs={{0,16},{16,0},{1,17},{17,1},{2,18},{18,2},{3,19},{19,3},{4,20},{20... | collective-permute-start | bytes 589832 | tf_op jit(solution)/shard_map/ppermute | solution.py:127
  8.5 0.6 dynamic_slice.117
  20.6 0.8 fusion.22
  26.5 1.6 copy.46
  28.1 0.7 copy.48
  28.8 1.2 maximum_select_fusion.7
  30.0 1.6 collective-permute-start.13
  31.6 0.4 collective-permute-start.14
  32.1 1.2 maximum_select_fusion.6
  33.3 1.0 pad_maximum_fusion.1
  34.3 1.6 collective-permute-start.2
  36.0 0.5 collective-permute-start.3
  36.5 2.1 %fusion.19 = bf16[1536,1024]{1,0:T(8,128)(2,1)} fusion(bf16[192,512]{1,0:T(8,128)(2,1)} %collective-permute-done.21, bf16[192,512]{1,0:T(8,128)(2,1)} %param.10, pred[]{:T(512)S(6)} %eq.34), kind=kLoop, calls=%fused_computation.46 | loop fusion | flops 1769471 | bytes 786433
  38.6 1.3 collective-permute-done.13
  39.9 1.6 collective-permute-start.15
  41.6 0.5 collective-permute-start.16
  42.1 9.9 %collective-permute-done.3 = bf16[192,1280]{1,0:T(8,128)(2,1)S(1)} collective-permute-done((bf16[192,1280]{1,0:T(8,128)(2,1)S(1)}, bf16[192,1280]{1,0:T(8,128)(2,1)S(1)}, u32[]{:S(2)}, u32[]{:S(2)}) %collective-permute-start.3) | collective-permute-done | bytes 491552 | tf_op jit(solution)/shard_map/ppermute | solution.py:139
  52.1 0.6 collective-permute-start.22
  52.7 1.6 collective-permute-start.4
  54.4 2.3 %collective-permute-done.15 = bf16[192,768]{1,0:T(8,128)(2,1)S(1)} collective-permute-done((bf16[192,768]{1,0:T(8,128)(2,1)S(1)}, bf16[192,768]{1,0:T(8,128)(2,1)S(1)}, u32[]{:S(2)}, u32[]{:S(2)}) %collective-permute-start.15) | collective-permute-done | bytes 294944 | tf_op jit(solution)/shard_map/ppermute | solution.py:138
  56.8 1.6 collective-permute-start.17
  58.4 0.5 collective-permute-start.18
  59.0 13.9 %collective-permute-done.17 = bf16[192,768]{1,0:T(8,128)(2,1)S(1)} collective-permute-done((bf16[192,768]{1,0:T(8,128)(2,1)S(1)}, bf16[192,768]{1,0:T(8,128)(2,1)S(1)}, u32[]{:S(2)}, u32[]{:S(2)}) %collective-permute-start.17) | collective-permute-done | bytes 294944 | tf_op jit(solution)/shard_map/ppermute | solution.py:138
  72.9 1.5 collective-permute-start.5
  74.5 0.6 collective-permute-start.19
  75.1 1.6 collective-permute-start.20
  76.7 1.1 fusion.16
  77.8 9.2 %collective-permute-done.5 = bf16[192,1280]{1,0:T(8,128)(2,1)S(1)} collective-permute-done((bf16[192,1280]{1,0:T(8,128)(2,1)S(1)}, bf16[192,1280]{1,0:T(8,128)(2,1)S(1)}, u32[]{:S(2)}, u32[]{:S(2)}) %collective-permute-start.5) | collective-permute-done | bytes 491552 | tf_op jit(solution)/shard_map/ppermute | solution.py:139
  87.2 1.6 collective-permute-start.6
  89.0 0.5 collective-permute-start.7
  89.6 5.5 %collective-permute-done.23 = bf16[384,512]{1,0:T(8,128)(2,1)S(1)} collective-permute-done((bf16[384,512]{1,0:T(8,128)(2,1)S(1)}, bf16[384,512]{1,0:T(8,128)(2,1)S(1)}, u32[]{:S(2)}, u32[]{:S(2)}) %collective-permute-start.23) | collective-permute-done | bytes 393248 | tf_op jit(solution)/shard_map/ppermute | solution.py:127
  95.1 1.1 fusion.17
  96.2 2.4 %collective-permute-done.6 = bf16[192,1280]{1,0:T(8,128)(2,1)S(1)} collective-permute-done((bf16[192,1280]{1,0:T(8,128)(2,1)S(1)}, bf16[192,1280]{1,0:T(8,128)(2,1)S(1)}, u32[]{:S(2)}, u32[]{:S(2)}) %collective-permute-start.6) | collective-permute-done | bytes 491552 | tf_op jit(solution)/shard_map/ppermute | solution.py:138
  98.6 1.6 collective-permute-start.8
  100.2 0.6 collective-permute-start.9
  100.9 2.0 %collective-permute-start.24 = (bf16[384,512]{1,0:T(8,128)(2,1)S(1)}, bf16[384,512]{1,0:T(8,128)(2,1)S(1)}, u32[]{:S(2)}, u32[]{:S(2)}) collective-permute-start(bf16[384,512]{1,0:T(8,128)(2,1)S(1)} %pad_maximum_fusion.4), channel_id=1, source_target_pairs={{0,16},{16,0},{1,17},{17,1},{2,18},{18,2},{3,19},{19,3},{4,20},{20... | collective-permute-start | bytes 1179656 | tf_op jit(solution)/shard_map/ppermute | solution.py:127
  103.1 1.7 %collective-permute-done.8 = bf16[96,1280]{1,0:T(8,128)(2,1)S(1)} collective-permute-done((bf16[96,1280]{1,0:T(8,128)(2,1)S(1)}, bf16[96,1280]{1,0:T(8,128)(2,1)S(1)}, u32[]{:S(2)}, u32[]{:S(2)}) %collective-permute-start.8) | collective-permute-done | bytes 245792 | tf_op jit(solution)/shard_map/ppermute | solution.py:142
  104.8 1.6 collective-permute-done.9
  106.5 2.0 %collective-permute-start.25 = (bf16[192,512]{1,0:T(8,128)(2,1)S(1)}, bf16[192,512]{1,0:T(8,128)(2,1)S(1)}, u32[]{:S(2)}, u32[]{:S(2)}) collective-permute-start(bf16[192,512]{1,0:T(8,128)(2,1)S(1)} %slice.277), channel_id=1, source_target_pairs={{0,16},{16,0},{1,17},{17,1},{2,18},{18,2},{3,19},{19,3},{4,20},{20... | collective-permute-start | bytes 589832 | tf_op jit(solution)/shard_map/ppermute | solution.py:127
  108.6 2.3 %collective-permute-done.24 = bf16[384,512]{1,0:T(8,128)(2,1)S(1)} collective-permute-done((bf16[384,512]{1,0:T(8,128)(2,1)S(1)}, bf16[384,512]{1,0:T(8,128)(2,1)S(1)}, u32[]{:S(2)}, u32[]{:S(2)}) %collective-permute-start.24) | collective-permute-done | bytes 393248 | tf_op jit(solution)/shard_map/ppermute | solution.py:127
  110.9 1.1 fusion.18
  112.0 1.0 collective-permute-done.25
  113.0 0.9 fusion.20
  115.9 3.4 %convolution_convert_fusion.1 = bf16[1024,384]{1,0:T(8,128)(2,1)S(1)} fusion(bf16[1024,3072]{1,0:T(8,128)(2,1)S(1)} %fusion.8, bf16[3072,384]{1,0:T(8,128)(2,1)S(1)} %slice_dynamic-update-slice_fusion), kind=kOutput, calls=%fused_computation.18 | convolution fusion | flops 2416312320 | bytes 9437184 | tf_op jit(solution)/shard_map/dot_general | solution.py:171
  119.3 1.0 copy.44
  120.3 5.6 %all-to-all-start = ((bf16[8,2,2,32,384]{4,3,2,1,0:T(8,128)(2,1)}), bf16[8,2,2,32,384]{4,3,2,1,0:T(8,128)(2,1)S(1)}, u32[]{:S(2)}, u32[]{:S(2)}) async-start(bf16[8,2,2,32,384]{4,3,2,1,0:T(8,128)(2,1)} %bitcast.68), calls=%async_computation | async-start | bytes 1572864 | tf_op jit(solution)/shard_map/all_to_all | solution.py:178
  125.9 1.6 slice_dynamic-update-slice_fusion.16
  127.5 6.9 %convolution_convert_fusion.2.qkv_ref = bf16[1024,384]{1,0:T(8,128)(2,1)S(1)} fusion(bf16[1024,3072]{1,0:T(8,128)(2,1)} %copy-done.3, bf16[3072,384]{1,0:T(8,128)(2,1)} %slice_dynamic-update-slice_fusion.16), kind=kOutput, calls=%fused_computation.19 | convolution fusion | flops 2416312320 | bytes 9437184 | tf_op jit(solution)/shard_map/dot_general | solution.py:171
  134.4 1.1 spatial_attention.1
  135.6 0.6 collective-permute-start.10
  136.3 10.4 %all-to-all-done = bf16[8,2,2,32,384]{4,3,2,1,0:T(8,128)(2,1)S(1)} async-done(((bf16[8,2,2,32,384]{4,3,2,1,0:T(8,128)(2,1)}), bf16[8,2,2,32,384]{4,3,2,1,0:T(8,128)(2,1)S(1)}, u32[]{:S(2)}, u32[]{:S(2)}) %all-to-all-start) | async-done | bytes 786464 | tf_op jit(solution)/shard_map/all_to_all | solution.py:178
  146.7 1.4 temporal_attention.1
  148.1 0.7 copy.28
  148.8 2.7 %all-to-all-start.1 = ((bf16[32,32,128]{2,1,0:T(8,128)(2,1)}), bf16[32,32,128]{2,1,0:T(8,128)(2,1)S(1)}, u32[]{:S(2)}, u32[]{:S(2)}) async-start(bf16[32,32,128]{2,1,0:T(8,128)(2,1)} %bitcast.27), calls=%async_computation.1 | async-start | bytes 524288 | tf_op jit(solution)/shard_map/all_to_all | solution.py:199
  151.6 0.3 collective-permute-start.11
  157.0 4.8 %all-to-all-done.1 = bf16[32,32,128]{2,1,0:T(8,128)(2,1)S(1)} async-done(((bf16[32,32,128]{2,1,0:T(8,128)(2,1)}), bf16[32,32,128]{2,1,0:T(8,128)(2,1)S(1)}, u32[]{:S(2)}, u32[]{:S(2)}) %all-to-all-start.1) | async-done | bytes 262176 | tf_op jit(solution)/shard_map/all_to_all | solution.py:199
  162.2 5.5 %maximum_select_fusion = bf16[8,2,192,1024]{3,2,1,0:T(8,128)(2,1)S(1)} fusion(bf16[8,1,192,1024]{3,2,1,0:T(8,128)(2,1)} %bitcast.35, bf16[8,1,192,1024]{3,2,1,0:T(8,128)(2,1)} %bitcast.33, pred[]{:T(512)S(6)} %eq.33), kind=kLoop, calls=%fused_computation.16 | loop fusion | flops 9437184 | bytes 12582913 | tf_op jit(solution)/shard_map/jit(_where)/select_n | solution.py:108
  167.6 1.9 %convolution_convert_fusion = bf16[256,3072]{1,0:T(8,128)(2,1)S(1)} fusion(bf16[256,1024]{0,1:T(8,128)(2,1)S(1)} %bitcast.91, bf16[3072,1024]{1,0:T(8,128)(2,1)S(1)} %bitcast.85), kind=kOutput, calls=%fused_computation.17 | convolution fusion | flops 1611399168 | bytes 8388608 | tf_op jit(solution)/shard_map/dot_general | solution.py:236
  170.0 1.1 copy-done.4
  (111 shorter events, 4.2 us)
Async XLA Ops:
  0.0 8.5 %copy-start.7 = (s32[8]{0:T(128)S(1)}, s32[8]{0:T(128)}, u32[]{:S(2)}) copy-start(s32[8]{0:T(128)} %constant.142.clone) | copy-start | bytes 100
  0.0 20.6 %copy-start.2 = (s32[8]{0:T(128)S(1)}, s32[8]{0:T(128)}, u32[]{:S(2)}) copy-start(s32[8]{0:T(128)} %constant.143.clone) | copy-start | bytes 100
  0.0 26.3 %copy-start.6 = (s32[16]{0:T(128)S(1)}, s32[16]{0:T(128)}, u32[]{:S(2)}) copy-start(s32[16]{0:T(128)} %param.11) | copy-start | bytes 196
  4.4 24.5 %collective-permute-start.12 = (bf16[192,384]{1,0:T(8,128)(2,1)}, bf16[192,384]{1,0:T(8,128)(2,1)}, u32[]{:S(2)}, u32[]{:S(2)}) collective-permute-start(bf16[192,384]{1,0:T(8,128)(2,1)} %bitcast.69), channel_id=1, source_target_pairs={{0,1},{1,0},{2,3},{3,2},{4,5},{5,4},{6,7},{7,6},{8,9},{9,8},{10,11... | collective-permute-start | bytes 442376 | tf_op jit(solution)/shard_map/ppermute | solution.py:105
  4.8 109.0 %collective-permute-start = (bf16[512,3072]{1,0:T(8,128)(2,1)}, bf16[512,3072]{1,0:T(8,128)(2,1)S(1)}, u32[]{:S(2)}, u32[]{:S(2)}) collective-permute-start(bf16[512,3072]{1,0:T(8,128)(2,1)} %bitcast.76), channel_id=1, source_target_pairs={{0,1},{1,0},{2,3},{3,2},{4,5},{5,4},{6,7},{7,6},{8,9},{9,8},{10,11... | collective-permute-start | bytes 9437192 | tf_op jit(solution)/shard_map/ppermute | solution.py:105
  5.6 26.6 %collective-permute-start.1 = (bf16[192,384]{1,0:T(8,128)(2,1)}, bf16[192,384]{1,0:T(8,128)(2,1)}, u32[]{:S(2)}, u32[]{:S(2)}) collective-permute-start(bf16[192,384]{1,0:T(8,128)(2,1)} %bitcast.71), channel_id=1, source_target_pairs={{0,1},{1,0},{2,3},{3,2},{4,5},{5,4},{6,7},{7,6},{8,9},{9,8},{10,11... | collective-permute-start | bytes 442376 | tf_op jit(solution)/shard_map/ppermute | solution.py:105
  6.0 30.0 %collective-permute-start.21 = (bf16[192,512]{1,0:T(8,128)(2,1)}, bf16[192,512]{1,0:T(8,128)(2,1)}, u32[]{:S(2)}, u32[]{:S(2)}) collective-permute-start(bf16[192,512]{1,0:T(8,128)(2,1)} %param.10), channel_id=1, source_target_pairs={{0,16},{16,0},{1,17},{17,1},{2,18},{18,2},{3,19},{19,3},{4,20},{20... | collective-permute-start | bytes 589832 | tf_op jit(solution)/shard_map/ppermute | solution.py:127
  30.0 9.9 %collective-permute-start.13 = (bf16[192,768]{1,0:T(8,128)(2,1)S(1)}, bf16[192,768]{1,0:T(8,128)(2,1)S(1)}, u32[]{:S(2)}, u32[]{:S(2)}) collective-permute-start(bf16[192,768]{1,0:T(8,128)(2,1)S(1)} %maximum_select_fusion.7), channel_id=1, source_target_pairs={{0,4},{1,5},{4,8},{5,9},{8,12},{9,13},{12,14},{13,15},{14,10},{15,... | collective-permute-start | bytes 884744 | tf_op jit(solution)/shard_map/ppermute | solution.py:138
  31.6 9.9 %collective-permute-start.14 = (bf16[192,768]{1,0:T(8,128)(2,1)S(1)}, bf16[192,768]{1,0:T(8,128)(2,1)S(1)}, u32[]{:S(2)}, u32[]{:S(2)}) collective-permute-start(bf16[192,768]{1,0:T(8,128)(2,1)S(1)} %maximum_select_fusion.7), channel_id=1, source_target_pairs={{4,0},{5,1},{8,4},{9,5},{12,8},{13,9},{14,12},{15,13},{10,14},{11,... | collective-permute-start | bytes 884744 | tf_op jit(solution)/shard_map/ppermute | solution.py:139
  34.3 17.7 %collective-permute-start.2 = (bf16[192,1280]{1,0:T(8,128)(2,1)S(1)}, bf16[192,1280]{1,0:T(8,128)(2,1)S(1)}, u32[]{:S(2)}, u32[]{:S(2)}) collective-permute-start(bf16[192,1280]{1,0:T(8,128)(2,1)S(1)} %pad_maximum_fusion.1), channel_id=1, source_target_pairs={{0,4},{1,5},{4,8},{5,9},{8,12},{9,13},{12,14},{13,15},{14,10},{15,... | collective-permute-start | bytes 1474568 | tf_op jit(solution)/shard_map/ppermute | solution.py:138
  36.0 16.0 %collective-permute-start.3 = (bf16[192,1280]{1,0:T(8,128)(2,1)S(1)}, bf16[192,1280]{1,0:T(8,128)(2,1)S(1)}, u32[]{:S(2)}, u32[]{:S(2)}) collective-permute-start(bf16[192,1280]{1,0:T(8,128)(2,1)S(1)} %pad_maximum_fusion.1), channel_id=1, source_target_pairs={{4,0},{5,1},{8,4},{9,5},{12,8},{13,9},{14,12},{15,13},{10,14},{11,... | collective-permute-start | bytes 1474568 | tf_op jit(solution)/shard_map/ppermute | solution.py:139
  39.9 16.9 %collective-permute-start.15 = (bf16[192,768]{1,0:T(8,128)(2,1)S(1)}, bf16[192,768]{1,0:T(8,128)(2,1)S(1)}, u32[]{:S(2)}, u32[]{:S(2)}) collective-permute-start(bf16[192,768]{1,0:T(8,128)(2,1)S(1)} %collective-permute-done.13), channel_id=1, source_target_pairs={{0,4},{1,5},{4,8},{5,9},{8,12},{9,13},{12,14},{13,15},{14,10},{15,... | collective-permute-start | bytes 884744 | tf_op jit(solution)/shard_map/ppermute | solution.py:138
  41.6 16.8 %collective-permute-start.16 = (bf16[192,768]{1,0:T(8,128)(2,1)S(1)}, bf16[192,768]{1,0:T(8,128)(2,1)S(1)}, u32[]{:S(2)}, u32[]{:S(2)}) collective-permute-start(bf16[192,768]{1,0:T(8,128)(2,1)S(1)} %collective-permute-done.14), channel_id=1, source_target_pairs={{4,0},{5,1},{8,4},{9,5},{12,8},{13,9},{14,12},{15,13},{10,14},{11,... | collective-permute-start | bytes 884744 | tf_op jit(solution)/shard_map/ppermute | solution.py:139
  52.1 23.0 %collective-permute-start.22 = (bf16[384,512]{1,0:T(8,128)(2,1)S(1)}, bf16[384,512]{1,0:T(8,128)(2,1)S(1)}, u32[]{:S(2)}, u32[]{:S(2)}) collective-permute-start(bf16[384,512]{1,0:T(8,128)(2,1)S(1)} %pad_maximum_fusion.2), channel_id=1, source_target_pairs={{0,16},{16,0},{1,17},{17,1},{2,18},{18,2},{3,19},{19,3},{4,20},{20... | collective-permute-start | bytes 1179656 | tf_op jit(solution)/shard_map/ppermute | solution.py:127
  52.7 34.3 %collective-permute-start.4 = (bf16[192,1280]{1,0:T(8,128)(2,1)S(1)}, bf16[192,1280]{1,0:T(8,128)(2,1)S(1)}, u32[]{:S(2)}, u32[]{:S(2)}) collective-permute-start(bf16[192,1280]{1,0:T(8,128)(2,1)S(1)} %collective-permute-done.2), channel_id=1, source_target_pairs={{0,4},{1,5},{4,8},{5,9},{8,12},{9,13},{12,14},{13,15},{14,10},{15,... | collective-permute-start | bytes 1474568 | tf_op jit(solution)/shard_map/ppermute | solution.py:138
  56.8 16.2 %collective-permute-start.17 = (bf16[192,768]{1,0:T(8,128)(2,1)S(1)}, bf16[192,768]{1,0:T(8,128)(2,1)S(1)}, u32[]{:S(2)}, u32[]{:S(2)}) collective-permute-start(bf16[192,768]{1,0:T(8,128)(2,1)S(1)} %collective-permute-done.15), channel_id=1, source_target_pairs={{0,4},{1,5},{4,8},{5,9},{8,12},{9,13},{12,14},{13,15},{14,10},{15,... | collective-permute-start | bytes 884744 | tf_op jit(solution)/shard_map/ppermute | solution.py:138
  58.4 16.0 %collective-permute-start.18 = (bf16[192,768]{1,0:T(8,128)(2,1)S(1)}, bf16[192,768]{1,0:T(8,128)(2,1)S(1)}, u32[]{:S(2)}, u32[]{:S(2)}) collective-permute-start(bf16[192,768]{1,0:T(8,128)(2,1)S(1)} %collective-permute-done.16), channel_id=1, source_target_pairs={{4,0},{5,1},{8,4},{9,5},{12,8},{13,9},{14,12},{15,13},{10,14},{11,... | collective-permute-start | bytes 884744 | tf_op jit(solution)/shard_map/ppermute | solution.py:139
  72.9 14.1 %collective-permute-start.5 = (bf16[192,1280]{1,0:T(8,128)(2,1)S(1)}, bf16[192,1280]{1,0:T(8,128)(2,1)S(1)}, u32[]{:S(2)}, u32[]{:S(2)}) collective-permute-start(bf16[192,1280]{1,0:T(8,128)(2,1)S(1)} %collective-permute-done.3), channel_id=1, source_target_pairs={{4,0},{5,1},{8,4},{9,5},{12,8},{13,9},{14,12},{15,13},{10,14},{11,... | collective-permute-start | bytes 1474568 | tf_op jit(solution)/shard_map/ppermute | solution.py:139
  74.5 14.5 %collective-permute-start.19 = (bf16[96,768]{1,0:T(8,128)(2,1)S(1)}, bf16[96,768]{1,0:T(8,128)(2,1)S(1)}, u32[]{:S(2)}, u32[]{:S(2)}) collective-permute-start(bf16[96,768]{1,0:T(8,128)(2,1)S(1)} %slice.267), channel_id=1, source_target_pairs={{0,4},{1,5},{4,8},{5,9},{8,12},{9,13},{12,14},{13,15},{14,10},{15,... | collective-permute-start | bytes 442376 | tf_op jit(solution)/shard_map/ppermute | solution.py:142
  75.1 14.4 %collective-permute-start.20 = (bf16[96,768]{1,0:T(8,128)(2,1)S(1)}, bf16[96,768]{1,0:T(8,128)(2,1)S(1)}, u32[]{:S(2)}, u32[]{:S(2)}) collective-permute-start(bf16[96,768]{1,0:T(8,128)(2,1)S(1)} %slice.268), channel_id=1, source_target_pairs={{4,0},{5,1},{8,4},{9,5},{12,8},{13,9},{14,12},{15,13},{10,14},{11,... | collective-permute-start | bytes 442376 | tf_op jit(solution)/shard_map/ppermute | solution.py:143
  87.1 8.0 %collective-permute-start.23 = (bf16[384,512]{1,0:T(8,128)(2,1)S(1)}, bf16[384,512]{1,0:T(8,128)(2,1)S(1)}, u32[]{:S(2)}, u32[]{:S(2)}) collective-permute-start(bf16[384,512]{1,0:T(8,128)(2,1)S(1)} %pad_maximum_fusion.3), channel_id=1, source_target_pairs={{0,16},{16,0},{1,17},{17,1},{2,18},{18,2},{3,19},{19,3},{4,20},{20... | collective-permute-start | bytes 1179656 | tf_op jit(solution)/shard_map/ppermute | solution.py:127
  87.2 11.4 %collective-permute-start.6 = (bf16[192,1280]{1,0:T(8,128)(2,1)S(1)}, bf16[192,1280]{1,0:T(8,128)(2,1)S(1)}, u32[]{:S(2)}, u32[]{:S(2)}) collective-permute-start(bf16[192,1280]{1,0:T(8,128)(2,1)S(1)} %collective-permute-done.4), channel_id=1, source_target_pairs={{0,4},{1,5},{4,8},{5,9},{8,12},{9,13},{12,14},{13,15},{14,10},{15,... | collective-permute-start | bytes 1474568 | tf_op jit(solution)/shard_map/ppermute | solution.py:138
  89.0 11.3 %collective-permute-start.7 = (bf16[192,1280]{1,0:T(8,128)(2,1)S(1)}, bf16[192,1280]{1,0:T(8,128)(2,1)S(1)}, u32[]{:S(2)}, u32[]{:S(2)}) collective-permute-start(bf16[192,1280]{1,0:T(8,128)(2,1)S(1)} %collective-permute-done.5), channel_id=1, source_target_pairs={{4,0},{5,1},{8,4},{9,5},{12,8},{13,9},{14,12},{15,13},{10,14},{11,... | collective-permute-start | bytes 1474568 | tf_op jit(solution)/shard_map/ppermute | solution.py:139
  98.6 6.2 %collective-permute-start.8 = (bf16[96,1280]{1,0:T(8,128)(2,1)S(1)}, bf16[96,1280]{1,0:T(8,128)(2,1)S(1)}, u32[]{:S(2)}, u32[]{:S(2)}) collective-permute-start(bf16[96,1280]{1,0:T(8,128)(2,1)S(1)} %slice.247), channel_id=1, source_target_pairs={{0,4},{1,5},{4,8},{5,9},{8,12},{9,13},{12,14},{13,15},{14,10},{15,... | collective-permute-start | bytes 737288 | tf_op jit(solution)/shard_map/ppermute | solution.py:142
  100.2 6.2 %collective-permute-start.9 = (bf16[96,1280]{1,0:T(8,128)(2,1)S(1)}, bf16[96,1280]{1,0:T(8,128)(2,1)S(1)}, u32[]{:S(2)}, u32[]{:S(2)}) collective-permute-start(bf16[96,1280]{1,0:T(8,128)(2,1)S(1)} %slice.248), channel_id=1, source_target_pairs={{4,0},{5,1},{8,4},{9,5},{12,8},{13,9},{14,12},{15,13},{10,14},{11,... | collective-permute-start | bytes 737288 | tf_op jit(solution)/shard_map/ppermute | solution.py:143
  100.9 9.9 %collective-permute-start.24 = (bf16[384,512]{1,0:T(8,128)(2,1)S(1)}, bf16[384,512]{1,0:T(8,128)(2,1)S(1)}, u32[]{:S(2)}, u32[]{:S(2)}) collective-permute-start(bf16[384,512]{1,0:T(8,128)(2,1)S(1)} %pad_maximum_fusion.4), channel_id=1, source_target_pairs={{0,16},{16,0},{1,17},{17,1},{2,18},{18,2},{3,19},{19,3},{4,20},{20... | collective-permute-start | bytes 1179656 | tf_op jit(solution)/shard_map/ppermute | solution.py:127
  103.0 10.8 %copy-start = (bf16[1,512,3072]{2,1,0:T(8,128)(2,1)S(1)}, bf16[1,512,3072]{2,1,0:T(8,128)(2,1)}, u32[]{:S(2)}) copy-start(bf16[1,512,3072]{2,1,0:T(8,128)(2,1)} %param.8) | copy-start | bytes 9437188
  106.5 2.0 %copy-start.1 = (bf16[192,1280]{1,0:T(8,128)(2,1)}, bf16[192,1280]{1,0:T(8,128)(2,1)S(1)}, u32[]{:S(2)}) copy-start(bf16[192,1280]{1,0:T(8,128)(2,1)S(1)} %constant_dynamic-update-slice_fusion) | copy-start | bytes 1474564
  106.5 6.4 %collective-permute-start.25 = (bf16[192,512]{1,0:T(8,128)(2,1)S(1)}, bf16[192,512]{1,0:T(8,128)(2,1)S(1)}, u32[]{:S(2)}, u32[]{:S(2)}) collective-permute-start(bf16[192,512]{1,0:T(8,128)(2,1)S(1)} %slice.277), channel_id=1, source_target_pairs={{0,16},{16,0},{1,17},{17,1},{2,18},{18,2},{3,19},{19,3},{4,20},{20... | collective-permute-start | bytes 589832 | tf_op jit(solution)/shard_map/ppermute | solution.py:127
  108.6 5.3 %copy-start.5 = (bf16[3072,384]{1,0:T(8,128)(2,1)}, bf16[3072,384]{1,0:T(8,128)(2,1)S(1)}, u32[]{:S(2)}) copy-start(bf16[3072,384]{1,0:T(8,128)(2,1)S(1)} %slice_dynamic-update-slice_fusion.17) | copy-start | bytes 7077892
  113.8 48.3 %collective-permute-start.26 = (bf16[1536,1024]{1,0:T(8,128)(2,1)}, bf16[1536,1024]{1,0:T(8,128)(2,1)}, u32[]{:S(2)}, u32[]{:S(2)}) collective-permute-start(bf16[1536,1024]{1,0:T(8,128)(2,1)} %fusion.20), channel_id=1, source_target_pairs={{0,1},{1,0},{2,3},{3,2},{4,5},{5,4},{6,7},{7,6},{8,9},{9,8},{10,11... | collective-permute-start | bytes 9437192 | tf_op jit(solution)/shard_map/ppermute | solution.py:105
  115.9 3.4 %copy-start.3 = (bf16[1024,3072]{1,0:T(8,128)(2,1)}, bf16[1024,3072]{1,0:T(8,128)(2,1)S(1)}, u32[]{:S(2)}) copy-start(bf16[1024,3072]{1,0:T(8,128)(2,1)S(1)} %fusion.8) | copy-start | bytes 18874372
  120.3 26.4 %all-to-all-start = ((bf16[8,2,2,32,384]{4,3,2,1,0:T(8,128)(2,1)}), bf16[8,2,2,32,384]{4,3,2,1,0:T(8,128)(2,1)S(1)}, u32[]{:S(2)}, u32[]{:S(2)}) async-start(bf16[8,2,2,32,384]{4,3,2,1,0:T(8,128)(2,1)} %bitcast.68), calls=%async_computation | async-start | bytes 1572864 | tf_op jit(solution)/shard_map/all_to_all | solution.py:178
  135.6 16.0 %collective-permute-start.10 = (bf16[1,2,256,128]{3,2,0,1:T(8,128)(2,1)S(1)}, bf16[1,2,256,128]{3,2,0,1:T(8,128)(2,1)S(1)}, u32[]{:S(2)}, u32[]{:S(2)}) collective-permute-start(bf16[1,2,256,128]{3,2,0,1:T(8,128)(2,1)S(1)} %get-tuple-element.12), channel_id=1, source_target_pairs={{0,16},{16,0},{1,17},{17,1},{2,18},{18,2},{3,19},{19,3},{4,20},{20... | collective-permute-start | bytes 393224 | tf_op jit(solution)/shard_map/ppermute | solution.py:119
  148.8 13.0 %all-to-all-start.1 = ((bf16[32,32,128]{2,1,0:T(8,128)(2,1)}), bf16[32,32,128]{2,1,0:T(8,128)(2,1)S(1)}, u32[]{:S(2)}, u32[]{:S(2)}) async-start(bf16[32,32,128]{2,1,0:T(8,128)(2,1)} %bitcast.27), calls=%async_computation.1 | async-start | bytes 524288 | tf_op jit(solution)/shard_map/all_to_all | solution.py:199
  151.6 5.4 %collective-permute-start.11 = (bf16[2,256,128]{2,1,0:T(8,128)(2,1)S(1)}, bf16[2,256,128]{2,1,0:T(8,128)(2,1)S(1)}, u32[]{:S(2)}, u32[]{:S(2)}) collective-permute-start(bf16[2,256,128]{2,1,0:T(8,128)(2,1)S(1)} %get-tuple-element.10), channel_id=1, source_target_pairs={{0,1},{1,0},{2,3},{3,2},{4,5},{5,4},{6,7},{7,6},{8,9},{9,8},{10,11... | collective-permute-start | bytes 393224 | tf_op jit(solution)/shard_map/ppermute | solution.py:105
  170.0 1.1 copy-start.4

commit v2 on v1

v2 whole, which is shorter than its diff:
```python
import functools
import math

import jax
import jax.numpy as jnp
from jax import lax
from jax.experimental import pallas as pl
from jax.experimental.pallas import tpu as pltpu
from jax.sharding import PartitionSpec as P

HEAD = 128
HS_DEV = 2
SCALE = 1.0 / math.sqrt(HEAD)
VMEM_LIMIT = 32 * 1024 * 1024


def vmem_call(body, out_shape, args, flops, name, scratch=()):
    bytes_moved = sum(a.size * a.dtype.itemsize for a in args)
    return pl.pallas_call(
        body,
        out_shape=out_shape,
        in_specs=[
            pl.BlockSpec(memory_space=pltpu.SMEM if a.dtype == jnp.int32 else pltpu.VMEM)
            for a in args
        ],
        out_specs=pl.BlockSpec(memory_space=pltpu.VMEM),
        scratch_shapes=list(scratch),
        compiler_params=pltpu.CompilerParams(vmem_limit_bytes=VMEM_LIMIT),
        cost_estimate=pl.CostEstimate(flops=flops, bytes_accessed=bytes_moved, transcendentals=0),
        name=name,
    )(*args)


def place_weight(meta_ref, piece_refs, weight):
    depth = piece_refs[0].shape[0]
    core = meta_ref[0]
    columns = weight.shape[1]
    slot, first = 0, 0
    for ref in piece_refs:
        rows = ref.shape[0]
        chip = meta_ref[2 + slot]
        for k in range(2):
            at = (chip * 2 + (core if k == 0 else 1 - core)) * depth + first
            weight[pl.ds(pl.multiple_of(at, 16), rows), :] = ref[
                :, k * columns : (k + 1) * columns
            ]
        first += rows
        if first == depth:
            slot, first = slot + 1, 0


def project_body(chips, n_st, direct, meta_ref, own_ref, other_ref, *refs):
    *piece_refs, out_ref, weight = refs
    place_weight(meta_ref, piece_refs, weight)
    patches = own_ref.shape[0]
    part = patches // (n_st * chips)
    half = patches // 2
    for frame, ref in enumerate((own_ref, other_ref)):
        for first in range(0, patches, half):
            result = jnp.dot(
                ref[first : first + half, :], weight[...], preferred_element_type=jnp.float32
            ).astype(jnp.bfloat16)
            if not direct:
                out_ref[frame * patches + first : frame * patches + first + half, :] = result
                continue
            for at in range(first, first + half, part):
                block = at // part
                out_ref[block % chips, frame, block // chips] = result[
                    at - first : at - first + part
                ]


def spatial_body(n_st, meta_ref, own_ref, other_ref, *refs):
    *piece_refs, out_ref, weight, packed = refs
    place_weight(meta_ref, piece_refs, weight)
    patches = own_ref.shape[0]
    part = patches // n_st
    half = patches // 2
    for frame, ref in enumerate((own_ref, other_ref)):
        for first in range(0, patches, half):
            packed[first : first + half, :] = jnp.dot(
                ref[first : first + half, :], weight[...], preferred_element_type=jnp.float32
            ).astype(jnp.bfloat16)
        for group in range(n_st):
            rows = slice(group * part, (group + 1) * part)
            scores = lax.dot_general(
                packed[rows, :HEAD],
                packed[:, HEAD : 2 * HEAD],
                (((1,), (1,)), ((), ())),
                preferred_element_type=jnp.float32,
            )
            scores = scores * SCALE
            expo = jnp.exp(scores - jnp.max(scores, axis=-1, keepdims=True))
            total = jnp.sum(expo, axis=-1, keepdims=True)
            result = jnp.dot(
                expo.astype(jnp.bfloat16),
                packed[:, 2 * HEAD :],
                preferred_element_type=jnp.float32,
            )
            result = (result / total).astype(jnp.bfloat16)
            place = (group + meta_ref[1]) % 2 if n_st == 2 else group
            out_ref[place, frame] = result


def temporal_body(tile, meta_ref, qkv_ref, out_ref):
    frames, rows = qkv_ref.shape[0], qkv_ref.shape[1]
    part = out_ref.shape[2]
    flip = meta_ref[frames]
    size = frames * tile
    row_at = lax.broadcasted_iota(jnp.int32, (size, size), 0)
    col_at = lax.broadcasted_iota(jnp.int32, (size, size), 1)
    row_seg = jnp.zeros((size, 1), jnp.int32)
    col_seg = jnp.zeros((1, size), jnp.int32)
    row_frame = lax.broadcasted_iota(jnp.int32, (size, 1), 0) // tile
    col_frame = lax.broadcasted_iota(jnp.int32, (1, size), 1) // tile
    for frame in range(frames):
        clip = meta_ref[frame]
        row_seg = jnp.where(row_frame == frame, clip, row_seg)
        col_seg = jnp.where(col_frame == frame, clip, col_seg)
    keep = (row_at % tile == col_at % tile) & (row_seg == col_seg)
    for start in range(0, rows, tile):
        block = qkv_ref[:, start : start + tile, :].reshape(size, 3 * HEAD)
        scores = lax.dot_general(
            block[:, :HEAD],
            block[:, HEAD : 2 * HEAD],
            (((1,), (1,)), ((), ())),
            preferred_element_type=jnp.float32,
        )
        scores = jnp.where(keep, scores * SCALE, jnp.float32(-1e30))
        expo = jnp.exp(scores - jnp.max(scores, axis=-1, keepdims=True))
        total = jnp.sum(expo, axis=-1, keepdims=True)
        result = jnp.dot(
            expo.astype(jnp.bfloat16), block[:, 2 * HEAD :], preferred_element_type=jnp.float32
        )
        result = (result / total).astype(jnp.bfloat16).reshape(frames, tile, HEAD)
        for pair in range(frames // 2):
            for k in range(2):
                at = 2 * pair + (flip if k == 0 else 1 - flip)
                if part % tile:
                    out_ref[0, at, start : start + tile, :] = result[2 * pair + k]
                else:
                    low = start % part
                    out_ref[start // part, at, low : low + tile, :] = result[2 * pair + k]


def place_out_body(depth, meta_ref, *refs):
    *piece_refs, weight = refs
    core, st = meta_ref[0], meta_ref[1]
    columns = piece_refs[0].shape[1]
    count = len(piece_refs) // 4
    for kind in range(4):
        group = st if kind < 2 else 1 - st
        side = core if kind % 2 == 0 else 1 - core
        slot = 0
        for ref in piece_refs[kind * count : (kind + 1) * count]:
            for first in range(0, ref.shape[0], depth):
                at = (meta_ref[2 + slot] * 2 + side) * depth
                weight[
                    pl.ds(pl.multiple_of(at, 16), depth),
                    pl.ds(pl.multiple_of(group * columns, 128), columns),
                ] = ref[first : first + depth, :]
                slot += 1


def out_body(meta_ref, mine_ref, peer_ref, core_ref, temporal_ref, weight_ref, out_ref, heads):
    core, st = meta_ref[0], meta_ref[1]
    n_st, chips, _, part, _ = temporal_ref.shape
    group = heads.shape[1] // n_st

    def columns(which, head):
        return pl.ds(pl.multiple_of(which * group + head * HEAD, 128), HEAD)

    heads[:, columns(st, core)] = mine_ref[0]
    heads[:, columns(1 - st, core)] = peer_ref[0]
    heads[:, columns(st, 1 - core)] = core_ref[0]
    heads[:, columns(1 - st, 1 - core)] = core_ref[1]
    for which in range(n_st):
        for chip in range(chips):
            for k in range(2):
                heads[
                    chip * part : (chip + 1) * part,
                    which * group + (HS_DEV + k) * HEAD : which * group + (HS_DEV + k + 1) * HEAD,
                ] = temporal_ref[which, chip, k]
    width = weight_ref.shape[0]
    step = 768 if width % 768 == 0 else width
    for at in range(0, width, step):
        out_ref[:, at : at + step] = lax.dot_general(
            heads[...],
            weight_ref[at : at + step, :],
            (((1,), (1,)), ((), ())),
            preferred_element_type=jnp.float32,
        ).astype(jnp.bfloat16)


def shards(n_st, n_fsdp, normed, qkv_weight, out_weight, segment_ids):
    patches, width = normed.shape[1], normed.shape[2]
    frames = n_fsdp
    depth = qkv_weight.shape[0]
    chips = n_fsdp // 2
    part = patches // (n_st * chips)
    rows = patches // n_st
    direct = part % 16 == 0
    ring = list(range(0, chips, 2)) + list(range(chips - 1, 0, -2))
    place = [ring.index(chip) for chip in range(chips)]
    me = lax.axis_index("fsdp")
    st = lax.axis_index("st")
    chip, core = me // 2, me % 2
    spot = jnp.array(place, jnp.int32)[chip]

    swap = [(i, i ^ 1) for i in range(n_fsdp)]
    forward = [
        (2 * ring[i] + c, 2 * ring[(i + 1) % chips] + c) for i in range(chips) for c in range(2)
    ]
    backward = [(b, a) for a, b in forward]

    def to_core(x):
        return lax.ppermute(x, "fsdp", swap)

    def to_peer(x):
        return lax.ppermute(x, "st", [(0, 1), (1, 0)])

    def ring_gather(piece, after=None):
        groups = [[piece]]
        ahead = behind = piece
        for _ in range(chips // 2 - 1):
            ahead = lax.ppermute(ahead, "fsdp", forward)
            behind = lax.ppermute(behind, "fsdp", backward)
            groups.append([ahead, behind])
        half = piece.shape[0] // 2
        ahead = lax.ppermute(ahead[:half], "fsdp", forward)
        behind = lax.ppermute(behind[half:], "fsdp", backward)
        groups.append([ahead, behind])
        return groups

    def pieces_of(groups, columns):
        pieces = [p[:, columns] for g in groups[:-1] for p in g]
        last = [p[:, columns] for p in groups[-1]]
        if last[0].shape[0] % 16:
            last = [jnp.concatenate(last)]
        return pieces + last

    offsets = [0]
    for d in range(1, chips // 2):
        offsets += [chips - d, d]
    offsets.append(chips // 2)
    sources = jnp.array(ring, jnp.int32)[(spot + jnp.array(offsets, jnp.int32)) % chips]
    meta = jnp.concatenate([core.reshape(1), st.reshape(1), sources]).astype(jnp.int32)

    by_head = qkv_weight.transpose(1, 0, 2)

    def take_head(heads):
        mine = lax.dynamic_index_in_dim(heads, core, 0, keepdims=False)
        other = lax.dynamic_index_in_dim(heads, 1 - core, 0, keepdims=False)
        return jnp.concatenate([mine, to_core(other)], axis=1)

    temporal_piece = take_head(lax.optimization_barrier(by_head[HS_DEV:]))
    own = normed.reshape(patches, width)

    groups = ring_gather(temporal_piece)
    first_step = groups[1]
    own, later_head, later_out, _ = lax.optimization_barrier(
        (own, by_head[:HS_DEV], out_weight, temporal_piece)
    )
    other = to_core(own)
    spatial_piece = take_head(later_head)
    head_flops = 4 * patches * width * 3 * HEAD
    weight_scratch = pltpu.VMEM((width, 3 * HEAD), jnp.bfloat16)
    shape = (chips, 2, n_st, part, 3 * HEAD) if direct else (2 * patches, 3 * HEAD)
    temporal = vmem_call(
        functools.partial(project_body, chips, n_st, direct),
        jax.ShapeDtypeStruct(shape, jnp.bfloat16),
        [meta, own, other, *pieces_of(groups, slice(None))],
        head_flops,
        "temporal_projection",
        [weight_scratch],
    )
    if not direct:
        temporal = temporal.reshape(2, n_st, chips, part, 3 * HEAD).transpose(2, 0, 1, 3, 4)
    same_core = [[2 * i + c for i in range(chips)] for c in range(2)]
    temporal = lax.all_to_all(
        temporal,
        "fsdp",
        split_axis=0,
        concat_axis=0,
        tiled=True,
        axis_index_groups=same_core,
    ).reshape(frames, n_st * part, 3 * HEAD)
    pairs = segment_ids.reshape(chips, 2)
    pairs = jnp.where(core == 0, pairs, pairs[:, ::-1]).reshape(frames)
    clips = jnp.concatenate([pairs, core.reshape(1)]).astype(jnp.int32)
    tile = min(n_st * part, max(16, 256 // frames))
    if part % tile == 0:
        shape = (n_st, frames, part, HEAD)
    else:
        shape = (1, frames, n_st * part, HEAD)
    result = vmem_call(
        functools.partial(temporal_body, tile),
        jax.ShapeDtypeStruct(shape, jnp.bfloat16),
        [clips, temporal],
        4 * frames * frames * n_st * part * tile * HEAD,
        "temporal_attention",
    )
    if part % tile:
        result = result.reshape(frames, n_st, part, HEAD).transpose(1, 0, 2, 3)
    result = lax.all_to_all(
        result.reshape(n_st * frames, part, HEAD),
        ("st", "fsdp"),
        split_axis=0,
        concat_axis=0,
        tiled=True,
    )
    temporal_heads = result.reshape(n_st, chips, 2, part, HEAD)

    split = spatial_piece.shape[1]
    both = jnp.concatenate([spatial_piece, later_out], axis=1)
    both, _ = lax.optimization_barrier((both, groups[-2]))
    groups = ring_gather(both)
    spatial = vmem_call(
        functools.partial(spatial_body, n_st),
        jax.ShapeDtypeStruct((n_st, 2, rows, HEAD), jnp.bfloat16),
        [meta, own, other, *pieces_of(groups, slice(0, split))],
        head_flops + 8 * patches * patches * HEAD,
        "spatial_heads",
        [weight_scratch, pltpu.VMEM((patches, 3 * HEAD), jnp.bfloat16)],
    )
    out_groups = [jnp.concatenate([p[:, split:] for p in g]) for g in groups]

    if n_st == 2 and direct:
        peer = to_peer(spatial[1])
        core_heads = to_core(jnp.stack([spatial[0, 1], peer[1]]))
        peer_groups = [to_peer(g) for g in out_groups]
        mine_all, peer_all = jnp.concatenate(out_groups), jnp.concatenate(peer_groups)
        weight = vmem_call(
            functools.partial(place_out_body, depth),
            jax.ShapeDtypeStruct((width, 2 * out_weight.shape[1]), jnp.bfloat16),
            [meta, mine_all, to_core(mine_all), peer_all, to_core(peer_all)],
            0,
            "place_out_weight",
        )
        attended = vmem_call(
            out_body,
            jax.ShapeDtypeStruct((rows, width), jnp.bfloat16),
            [meta, spatial[0], peer, core_heads, temporal_heads, weight],
            4 * rows * width * out_weight.shape[1],
            "out_projection",
            [pltpu.VMEM((rows, 2 * out_weight.shape[1]), jnp.bfloat16)],
        )
        return attended.reshape(1, rows, width)

    def by_core(mine, other, axis):
        return jnp.where(
            core == 0,
            jnp.concatenate([mine, other], axis=axis),
            jnp.concatenate([other, mine], axis=axis),
        )

    if n_st == 2:
        spatial = jnp.where(st == 0, spatial, spatial[::-1])
    spatial = lax.all_to_all(spatial, "st", split_axis=0, concat_axis=0, tiled=True)
    spatial = by_core(spatial[:, 0, :, None], to_core(spatial[:, 1])[:, :, None], 2)
    heads = jnp.concatenate(
        [
            spatial.transpose(1, 0, 2, 3),
            temporal_heads.transpose(1, 3, 0, 2, 4).reshape(rows, n_st, 2, HEAD),
        ],
        axis=2,
    ).reshape(rows, -1)
    weight = lax.all_gather(jnp.concatenate(out_groups), "st", axis=1, tiled=True)
    weight = by_core(
        weight.reshape(chips, 1, depth, -1), to_core(weight).reshape(chips, 1, depth, -1), 1
    )
    order = jnp.zeros((chips,), jnp.int32).at[sources].set(jnp.arange(chips, dtype=jnp.int32))
    weight = weight[order].reshape(width, -1)
    attended = lax.dot_general(
        heads, weight, (((1,), (1,)), ((), ())), preferred_element_type=jnp.float32
    ).astype(jnp.bfloat16)
    return attended.reshape(1, rows, width)


def solution(mesh):
    return jax.shard_map(
        functools.partial(shards, mesh.shape["st"], mesh.shape["fsdp"]),
        mesh=mesh,
        in_specs=(P("fsdp", None, None), P("fsdp", "st", None), P("fsdp", "st"), P()),
        out_specs=P("fsdp", "st", None),
        check_vma=False,
    )
```

time: 172 us -> 152 us (0.88)
  between operations: 22.2 us -> 0.47 us
  local copies, waits for them, and re-layouts: 15.1 us -> 35.5 us
  Pallas kernels: 2.49 us -> 22.1 us
  waiting for transfers between devices: 66.5 us -> 52.9 us
  other arithmetic: 17.3 us -> 5.02 us
  matrix products: 12.2 us -> 0 us
    slice x7 -> x20, local copies, waits for them, and re-layouts: 0.1 us -> 19.7 us  [the longest x9 11.8 us: shards(): out_groups = [jnp.concatenate([p[:, split:] for p in g]) for g in groups]]
    pallas_call x2 -> x5, Pallas kernels: 2.49 us -> 22.1 us  [vmem_call(): pl.pallas_call(body, out_shape=out_shape, in_specs=[pl.BlockSpec(memory_s...]
    ppermute x6, waiting for transfers between devices: 19.2 us -> 4.86 us  [ring_gather(): behind = lax.ppermute(behind, 'fsdp', backward)]
    dot_general x3 -> x0, matrix products: 12.2 us -> none  [the longest x2 10.3 us: project(): jnp.dot(rows, weight, preferred_element_type=jnp.float32)]
    all_to_all x1, waiting for transfers between devices: 10.4 us -> 0.01 us  [shards(): lax.all_to_all(temporal, 'fsdp', split_axis=0, concat_axis=0, tiled=True,...]
    ppermute x6, waiting for transfers between devices: 19.9 us -> 28.5 us  [ring_gather(): ahead = lax.ppermute(ahead, 'fsdp', forward)]
    ppermute x6, waiting for transfers between devices: 8.82 us -> 16.8 us  [to_peer(): return lax.ppermute(x, 'st', [(0, 1), (1, 0)])]
    select_n x4 -> x1, other arithmetic: 7.9 us -> 0.68 us  [shards(): jnp.array(ring, jnp.int32)[(spot + jnp.array(offsets, jnp.int32)) % chips]]
  transfers between devices with their start and end apart: 29 -> 30, of which waited for: 13 -> 13; matrix products, arithmetic and copies ran while one was open for 18% -> 22% of each run, Pallas kernels for 1% -> 12%
where the time goes in v2:
time: 152 us; the launch traced here: 151 us
  waiting for transfers between devices  52.9 us (35%)
  local copies, waits for them, and re-layouts  35.5 us (23%)
  starting transfers between devices  35.3 us (23%)
  Pallas kernels  22.1 us (15%)
  other arithmetic  5.02 us (3%)
    ppermute x6, waiting for transfers between devices, ring_gather(): ahead = lax.ppermute(ahead, 'fsdp', forward)  28.5 us
    pallas_call x5, Pallas kernels, vmem_call(): pl.pallas_call(body, out_shape=out_shape, in_specs=[pl.BlockSpec(memory_s...  22.1 us
    ppermute x6, waiting for transfers between devices, to_peer(): return lax.ppermute(x, 'st', [(0, 1), (1, 0)])  16.8 us
    slice x9, local copies, waits for them, and re-layouts, shards(): out_groups = [jnp.concatenate([p[:, split:] for p in g]) for g in groups]  11.8 us
    ppermute x6, starting transfers between devices, ring_gather(): ahead = lax.ppermute(ahead, 'fsdp', forward)  11 us
    unnamed x57, local copies, waits for them, and re-layouts  10.7 us
    ppermute x6, starting transfers between devices, to_peer(): return lax.ppermute(x, 'st', [(0, 1), (1, 0)])  7.51 us
    slice x7, local copies, waits for them, and re-layouts, pieces_of(): pieces = [p[:, columns] for g in groups[:-1] for p in g]  6.14 us
  transfers between devices with their start and end apart: 30, of which 13 were waited for; matrix products, arithmetic and copies ran while one was open for 22% of the time, Pallas kernels for 12%

profile of v2, /device:TPU:0, one launch (start us, length us, event | category | flops | bytes accessed | tf_op | source)
XLA Modules:
  0.0 151.3 jit_solution(3335176114893151442)
XLA Ops:
  0.0 1.1 copy.10
  1.2 0.8 fusion.1
  2.5 1.0 collective-permute-done
  3.5 3.0 %collective-permute-start.3 = (bf16[192,768]{1,0:T(8,128)(2,1)S(1)}, bf16[192,768]{1,0:T(8,128)(2,1)S(1)}, u32[]{:S(2)}, u32[]{:S(2)}) collective-permute-start(bf16[192,768]{1,0:T(8,128)(2,1)S(1)} %pad_maximum_fusion.4.refs_0_), channel_id=1, source_target_pairs={{0,4},{1,5},{4,8},{5,9},{8,12},{9,13},{12,14},{13,15},{14,10},{15,... | collective-permute-start | bytes 884744 | tf_op jit(solution)/shard_map/ppermute | solution.py:226
  6.5 7.3 %collective-permute-done.3.refs_1_ = bf16[192,768]{1,0:T(8,128)(2,1)S(1)} collective-permute-done((bf16[192,768]{1,0:T(8,128)(2,1)S(1)}, bf16[192,768]{1,0:T(8,128)(2,1)S(1)}, u32[]{:S(2)}, u32[]{:S(2)}) %collective-permute-start.3) | collective-permute-done | bytes 294944 | tf_op jit(solution)/shard_map/ppermute | solution.py:226
  13.8 1.8 %collective-permute-start.4 = (bf16[192,768]{1,0:T(8,128)(2,1)S(1)}, bf16[192,768]{1,0:T(8,128)(2,1)S(1)}, u32[]{:S(2)}, u32[]{:S(2)}) collective-permute-start(bf16[192,768]{1,0:T(8,128)(2,1)S(1)} %collective-permute-done.3.refs_1_), channel_id=1, source_target_pairs={{0,4},{1,5},{4,8},{5,9},{8,12},{9,13},{12,14},{13,15},{14,10},{15,... | collective-permute-start | bytes 884744 | tf_op jit(solution)/shard_map/ppermute | solution.py:226
  15.8 1.0 dynamic-slice_bitcast_fusion.1
  16.9 5.4 %collective-permute-done.4.refs_3_ = bf16[192,768]{1,0:T(8,128)(2,1)S(1)} collective-permute-done((bf16[192,768]{1,0:T(8,128)(2,1)S(1)}, bf16[192,768]{1,0:T(8,128)(2,1)S(1)}, u32[]{:S(2)}, u32[]{:S(2)}) %collective-permute-start.4) | collective-permute-done | bytes 294944 | tf_op jit(solution)/shard_map/ppermute | solution.py:226
  22.3 1.5 collective-permute-start.5
  24.4 1.8 %pad_maximum_fusion = bf16[192,1280]{1,0:T(8,128)(2,1)} fusion(bf16[192,512]{1,0:T(8,128)(2,1)} %param.9, bf16[192,384]{1,0:T(8,128)(2,1)S(1)} %collective-permute-done.2, bf16[192,384]{1,0:T(8,128)(2,1)S(1)} %get-tuple-element.29), kind=kLoop, calls=%fused_computation.2 | loop fusion | flops 1474560 | bytes 983040 | tf_op jit(solution)/shard_map/concatenate | solution.py:315
  26.2 3.8 %collective-permute-done.5.refs_5_ = bf16[192,768]{1,0:T(8,128)(2,1)S(1)} collective-permute-done((bf16[192,768]{1,0:T(8,128)(2,1)S(1)}, bf16[192,768]{1,0:T(8,128)(2,1)S(1)}, u32[]{:S(2)}, u32[]{:S(2)}) %collective-permute-start.5) | collective-permute-done | bytes 294944 | tf_op jit(solution)/shard_map/ppermute | solution.py:226
  30.0 0.9 collective-permute-done.8.refs_6_
  30.9 1.6 %collective-permute-start.9 = (bf16[192,1280]{1,0:T(8,128)(2,1)}, bf16[192,1280]{1,0:T(8,128)(2,1)}, u32[]{:S(2)}, u32[]{:S(2)}) collective-permute-start(bf16[192,1280]{1,0:T(8,128)(2,1)} %pad_maximum_fusion), channel_id=1, source_target_pairs={{0,4},{1,5},{4,8},{5,9},{8,12},{9,13},{12,14},{13,15},{14,10},{15,... | collective-permute-start | bytes 1474568 | tf_op jit(solution)/shard_map/ppermute | solution.py:226
  33.7 1.7 %fusion.8 = (bf16[192,512]{1,0:T(8,128)(2,1)}, bf16[1536,512]{1,0:T(8,128)(2,1)}) fusion(bf16[192,1280]{1,0:T(8,128)(2,1)} %pad_maximum_fusion), kind=kLoop, calls=%fused_computation.46 | loop fusion | bytes 589824 | tf_op jit(solution)/shard_map/slice | solution.py:326
  35.4 6.6 %collective-permute-done.9 = bf16[192,1280]{1,0:T(8,128)(2,1)} collective-permute-done((bf16[192,1280]{1,0:T(8,128)(2,1)}, bf16[192,1280]{1,0:T(8,128)(2,1)}, u32[]{:S(2)}, u32[]{:S(2)}) %collective-permute-start.9) | collective-permute-done | bytes 491552 | tf_op jit(solution)/shard_map/ppermute | solution.py:226
  42.0 1.6 %fusion.6 = (bf16[192,512]{1,0:T(8,128)(2,1)S(1)}, bf16[1536,512]{1,0:T(8,128)(2,1)}) fusion(bf16[192,1280]{1,0:T(8,128)(2,1)} %collective-permute-done.9, bf16[1536,512]{1,0:T(8,128)(2,1)} %get-tuple-element.28), kind=kLoop, calls=%fused_computation.44 | loop fusion | bytes 589824 | tf_op jit(solution)/shard_map/slice | solution.py:326
  43.6 2.9 %collective-permute-done.10 = bf16[192,1280]{1,0:T(8,128)(2,1)} collective-permute-done((bf16[192,1280]{1,0:T(8,128)(2,1)}, bf16[192,1280]{1,0:T(8,128)(2,1)}, u32[]{:S(2)}, u32[]{:S(2)}) %collective-permute-start.10) | collective-permute-done | bytes 491552 | tf_op jit(solution)/shard_map/ppermute | solution.py:227
  46.4 1.6 %fusion.7 = (bf16[192,512]{1,0:T(8,128)(2,1)S(1)}, bf16[1536,512]{1,0:T(8,128)(2,1)}) fusion(bf16[192,1280]{1,0:T(8,128)(2,1)} %collective-permute-done.10, bf16[1536,512]{1,0:T(8,128)(2,1)} %get-tuple-element.24), kind=kLoop, calls=%fused_computation.45 | loop fusion | bytes 589824 | tf_op jit(solution)/shard_map/slice | solution.py:326
  48.1 0.8 pad_maximum_fusion.1
  48.9 1.5 collective-permute-start.23
  50.4 1.6 %collective-permute-start.11 = (bf16[192,1280]{1,0:T(8,128)(2,1)}, bf16[192,1280]{1,0:T(8,128)(2,1)}, u32[]{:S(2)}, u32[]{:S(2)}) collective-permute-start(bf16[192,1280]{1,0:T(8,128)(2,1)} %collective-permute-done.9), channel_id=1, source_target_pairs={{0,4},{1,5},{4,8},{5,9},{8,12},{9,13},{12,14},{13,15},{14,10},{15,... | collective-permute-start | bytes 1474568 | tf_op jit(solution)/shard_map/ppermute | solution.py:226
  52.4 0.7 compare_select_fusion
  54.4 0.9 slice.130
  55.3 0.9 slice.131
  56.3 7.8 %collective-permute-done.22 = bf16[192,512]{1,0:T(8,128)(2,1)} collective-permute-done((bf16[192,512]{1,0:T(8,128)(2,1)}, bf16[192,512]{1,0:T(8,128)(2,1)}, u32[]{:S(2)}, u32[]{:S(2)}) %collective-permute-start.22) | collective-permute-done | bytes 196640 | tf_op jit(solution)/shard_map/ppermute | solution.py:220
  64.1 1.6 %collective-permute-start.19 = (bf16[96,768]{1,0:T(8,128)(2,1)S(1)}, bf16[96,768]{1,0:T(8,128)(2,1)S(1)}, u32[]{:S(2)}, u32[]{:S(2)}) collective-permute-start(bf16[96,768]{1,0:T(8,128)(2,1)S(1)} %slice.130), channel_id=1, source_target_pairs={{0,4},{1,5},{4,8},{5,9},{8,12},{9,13},{12,14},{13,15},{14,10},{15,... | collective-permute-start | bytes 442376 | tf_op jit(solution)/shard_map/ppermute | solution.py:230
  65.6 0.9 constant_dynamic-update-slice_fusion.13
  67.1 1.0 constant_dynamic-update-slice_fusion.12
  68.1 1.6 %collective-permute-start.13 = (bf16[192,1280]{1,0:T(8,128)(2,1)}, bf16[192,1280]{1,0:T(8,128)(2,1)S(1)}, u32[]{:S(2)}, u32[]{:S(2)}) collective-permute-start(bf16[192,1280]{1,0:T(8,128)(2,1)} %collective-permute-done.11), channel_id=1, source_target_pairs={{0,4},{1,5},{4,8},{5,9},{8,12},{9,13},{12,14},{13,15},{14,10},{15,... | collective-permute-start | bytes 1474568 | tf_op jit(solution)/shard_map/ppermute | solution.py:226
  70.2 1.6 %fusion.4 = (bf16[192,512]{1,0:T(8,128)(2,1)S(1)}, bf16[1536,512]{1,0:T(8,128)(2,1)}) fusion(bf16[192,1280]{1,0:T(8,128)(2,1)} %collective-permute-done.11, bf16[1536,512]{1,0:T(8,128)(2,1)} %get-tuple-element.26), kind=kLoop, calls=%fused_computation.42 | loop fusion | bytes 589824 | tf_op jit(solution)/shard_map/slice | solution.py:326
  71.8 1.6 %fusion.5 = (bf16[192,512]{1,0:T(8,128)(2,1)S(1)}, bf16[1536,512]{1,0:T(8,128)(2,1)}) fusion(bf16[192,1280]{1,0:T(8,128)(2,1)} %collective-permute-done.12, bf16[1536,512]{1,0:T(8,128)(2,1)} %get-tuple-element.20), kind=kLoop, calls=%fused_computation.43 | loop fusion | bytes 589824 | tf_op jit(solution)/shard_map/slice | solution.py:326
  73.5 0.8 pad_maximum_fusion.2
  74.3 5.4 %collective-permute-done.13 = bf16[192,1280]{1,0:T(8,128)(2,1)S(1)} collective-permute-done((bf16[192,1280]{1,0:T(8,128)(2,1)}, bf16[192,1280]{1,0:T(8,128)(2,1)S(1)}, u32[]{:S(2)}, u32[]{:S(2)}) %collective-permute-start.13) | collective-permute-done | bytes 491552 | tf_op jit(solution)/shard_map/ppermute | solution.py:226
  79.7 1.5 collective-permute-start.24
  81.3 1.1 collective-permute-done.14
  82.3 1.5 %collective-permute-start.15 = (bf16[96,1280]{1,0:T(8,128)(2,1)S(1)}, bf16[96,1280]{1,0:T(8,128)(2,1)S(1)}, u32[]{:S(2)}, u32[]{:S(2)}) collective-permute-start(bf16[96,1280]{1,0:T(8,128)(2,1)S(1)} %slice.122), channel_id=1, source_target_pairs={{0,4},{1,5},{4,8},{5,9},{8,12},{9,13},{12,14},{13,15},{14,10},{15,... | collective-permute-start | bytes 737288 | tf_op jit(solution)/shard_map/ppermute | solution.py:230
  83.8 0.7 slice.124
  84.6 0.7 fusion.2
  85.3 0.7 fusion.3
  86.0 0.8 pad_maximum_fusion.3
  86.8 1.8 %collective-permute-done.15 = bf16[96,1280]{1,0:T(8,128)(2,1)S(1)} collective-permute-done((bf16[96,1280]{1,0:T(8,128)(2,1)S(1)}, bf16[96,1280]{1,0:T(8,128)(2,1)S(1)}, u32[]{:S(2)}, u32[]{:S(2)}) %collective-permute-start.15) | collective-permute-done | bytes 245792 | tf_op jit(solution)/shard_map/ppermute | solution.py:230
  89.6 1.5 collective-permute-start.25
  91.2 6.5 %temporal_projection.1 = bf16[8,2,2,32,384]{4,3,2,1,0:T(8,128)(2,1)} custom-call(s32[10]{0:T(128)S(1)} %pad_add_fusion.meta_ref, bf16[512,3072]{1,0:T(8,128)(2,1)S(1)} %bitcast.27, bf16[512,3072]{1,0:T(8,128)(2,1)} %collective-permute-done.1.other_ref, bf16[192,768]{1,0:T(8,128)(2,1)S(1)} %pad_maximum_fusion.4.refs_0_, bf16[192,768]{1,0:T(8,128)(2,1)S(1)} %copy-done.11, ...), custom_call_target="tpu_custom_call" | custom-call | flops 2415919104 | bytes 8650792 | tf_op jit(solution)/shard_map/temporal_projection/pallas_call | solution.py:19
  97.7 4.5 %all-to-all-start = ((bf16[8,2,2,32,384]{4,3,2,1,0:T(8,128)(2,1)}), bf16[8,2,2,32,384]{4,3,2,1,0:T(8,128)(2,1)S(1)}, u32[]{:S(2)}, u32[]{:S(2)}) async-start(bf16[8,2,2,32,384]{4,3,2,1,0:T(8,128)(2,1)} %temporal_projection.1), calls=%async_computation | async-start | bytes 1572864 | tf_op jit(solution)/shard_map/all_to_all | solution.py:280
  102.2 1.6 %fusion.10 = (bf16[96,512]{1,0:T(8,128)(2,1)S(1)}, bf16[1536,512]{1,0:T(8,128)(2,1)}) fusion(bf16[96,1280]{1,0:T(8,128)(2,1)} %collective-permute-done.16, bf16[1536,512]{1,0:T(8,128)(2,1)} %get-tuple-element.36), kind=kLoop, calls=%fused_computation.48 | loop fusion | bytes 294912 | tf_op jit(solution)/shard_map/slice | solution.py:326
  104.3 1.0 constant_dynamic-update-slice_fusion.11
  105.5 1.0 constant_dynamic-update-slice_fusion.10
  106.5 3.0 %collective-permute-done.26 = bf16[192,512]{1,0:T(8,128)(2,1)S(1)} collective-permute-done((bf16[192,512]{1,0:T(8,128)(2,1)S(1)}, bf16[192,512]{1,0:T(8,128)(2,1)S(1)}, u32[]{:S(2)}, u32[]{:S(2)}) %collective-permute-start.26) | collective-permute-done | bytes 196640 | tf_op jit(solution)/shard_map/ppermute | solution.py:220
  109.9 1.0 slice.86.refs_0_
  110.9 1.1 slice.116.refs_1_
  112.0 1.1 slice.117.refs_2_
  113.1 1.0 slice.118.refs_3_
  114.1 1.0 slice.119.refs_4_
  115.1 1.0 slice.120.refs_5_
  116.1 0.9 slice.125.refs_8_
  117.1 7.1 %spatial_heads.1 = bf16[2,2,256,128]{3,2,1,0:T(8,128)(2,1)S(1)} custom-call(s32[10]{0:T(128)S(1)} %pad_add_fusion.meta_ref, bf16[512,3072]{1,0:T(8,128)(2,1)S(1)} %bitcast.28, bf16[512,3072]{1,0:T(8,128)(2,1)} %collective-permute-done.1.other_ref, bf16[192,768]{1,0:T(8,128)(2,1)S(1)} %slice.86.refs_0_, bf16[192,768]{1,0:T(8,128)(2,1)S(1)} %slice.116.refs_1_, ...), custom_call_target="tpu_custom_call" | custom-call | flops 2684354560 | bytes 8650792 | tf_op jit(solution)/shard_map/spatial_heads/pallas_call | solution.py:19
  124.2 2.1 %temporal_attention.1 = bf16[2,16,32,128]{3,2,1,0:T(8,128)(2,1)} custom-call(s32[17]{0:T(128)S(1)} %pad_add_fusion.1.meta_ref, bf16[16,64,384]{2,1,0:T(8,128)(2,1)S(1)} %bitcast.25), custom_call_target="tpu_custom_call" | custom-call | flops 134217728 | bytes 786500 | tf_op jit(solution)/shard_map/temporal_attention/pallas_call | solution.py:19
  126.2 5.2 %all-to-all-start.1 = ((bf16[32,32,128]{2,1,0:T(8,128)(2,1)}), bf16[32,32,128]{2,1,0:T(8,128)(2,1)S(1)}, u32[]{:S(2)}, u32[]{:S(2)}) async-start(bf16[32,32,128]{2,1,0:T(8,128)(2,1)} %bitcast.13), calls=%async_computation.1 | async-start | bytes 524288 | tf_op jit(solution)/shard_map/all_to_all | solution.py:305
  131.4 1.8 %collective-permute-start.17 = (bf16[2,256,128]{2,1,0:T(8,128)(2,1)S(1)}, bf16[2,256,128]{2,1,0:T(8,128)(2,1)S(1)}, u32[]{:S(2)}, u32[]{:S(2)}) collective-permute-start(bf16[2,256,128]{2,1,0:T(8,128)(2,1)S(1)} %get-tuple-element.33), channel_id=1, source_target_pairs={{0,16},{16,0},{1,17},{17,1},{2,18},{18,2},{3,19},{19,3},{4,20},{20... | collective-permute-start | bytes 393224 | tf_op jit(solution)/shard_map/ppermute | solution.py:220
  133.3 6.0 %collective-permute-done.17.peer_ref = bf16[2,256,128]{2,1,0:T(8,128)(2,1)S(1)} collective-permute-done((bf16[2,256,128]{2,1,0:T(8,128)(2,1)S(1)}, bf16[2,256,128]{2,1,0:T(8,128)(2,1)S(1)}, u32[]{:S(2)}, u32[]{:S(2)}) %collective-permute-start.17) | collective-permute-done | bytes 131104 | tf_op jit(solution)/shard_map/ppermute | solution.py:220
  139.4 2.9 %place_out_weight.1.weight_ref = bf16[3072,1024]{1,0:T(8,128)(2,1)S(1)} custom-call(s32[10]{0:T(128)S(1)} %pad_add_fusion.meta_ref, bf16[1536,512]{1,0:T(8,128)(2,1)} %get-tuple-element.38.refs_0_, bf16[1536,512]{1,0:T(8,128)(2,1)} %collective-permute-done.21.refs_1_, bf16[1536,512]{1,0:T(8,128)(2,1)S(1)} %constant_dynamic-update-slice_fusion.9.refs_2_, ...), custom_call_target="tpu_custom_call" | custom-call | bytes 6291496 | tf_op jit(solution)/shard_map/place_out_weight/pallas_call | solution.py:19
  142.3 2.6 %copy-done = bf16[3072,1024]{1,0:T(8,128)(2,1)} copy-done((bf16[3072,1024]{1,0:T(8,128)(2,1)}, bf16[3072,1024]{1,0:T(8,128)(2,1)S(1)}, u32[]{:S(2)}) %copy-start) | copy-done | bytes 6291480
  145.0 2.8 %copy-done.1 = bf16[3072,1024]{1,0:T(8,128)(2,1)S(1)} copy-done((bf16[3072,1024]{1,0:T(8,128)(2,1)S(1)}, bf16[3072,1024]{1,0:T(8,128)(2,1)}, u32[]{:S(2)}) %copy-start.1) | copy-done | bytes 6291480
  147.8 3.5 %out_projection.1 = bf16[256,3072]{1,0:T(8,128)(2,1)} custom-call(s32[10]{0:T(128)S(1)} %pad_add_fusion.meta_ref, bf16[2,256,128]{2,1,0:T(8,128)(2,1)S(1)} %get-tuple-element.34.mine_ref, bf16[2,256,128]{2,1,0:T(8,128)(2,1)S(1)} %collective-permute-done.17.peer_ref, bf16[2,256,128]{2,1,0:T(8,128)(2,1)S(1)} %collective-permute-done.18.core_ref, ...), custom_call_target="tpu_custom_call" | custom-call | flops 1610612736 | bytes 6946856 | tf_op jit(solution)/shard_map/out_projection/pallas_call | solution.py:19
  (104 shorter events, 7.9 us)
Async XLA Ops:
  1.1 31.3 %copy-start.2 = (bf16[1,512,3072]{2,1,0:T(8,128)(2,1)S(1)}, bf16[1,512,3072]{2,1,0:T(8,128)(2,1)}, u32[]{:S(2)}) copy-start(bf16[1,512,3072]{2,1,0:T(8,128)(2,1)} %param.7) | copy-start | bytes 9437188
  1.9 31.1 %copy-start.25 = (s32[8]{0:T(128)S(1)}, s32[8]{0:T(128)}, u32[]{:S(2)}) copy-start(s32[8]{0:T(128)} %constant.67.clone) | copy-start | bytes 100
  2.0 1.5 %collective-permute-start = (bf16[192,384]{1,0:T(8,128)(2,1)S(1)}, bf16[192,384]{1,0:T(8,128)(2,1)S(1)}, u32[]{:S(2)}, u32[]{:S(2)}) collective-permute-start(bf16[192,384]{1,0:T(8,128)(2,1)S(1)} %get-tuple-element.32), channel_id=1, source_target_pairs={{0,1},{1,0},{2,3},{3,2},{4,5},{5,4},{6,7},{7,6},{8,9},{9,8},{10,11... | collective-permute-start | bytes 442376 | tf_op jit(solution)/shard_map/ppermute | solution.py:217
  3.5 10.2 %collective-permute-start.3 = (bf16[192,768]{1,0:T(8,128)(2,1)S(1)}, bf16[192,768]{1,0:T(8,128)(2,1)S(1)}, u32[]{:S(2)}, u32[]{:S(2)}) collective-permute-start(bf16[192,768]{1,0:T(8,128)(2,1)S(1)} %pad_maximum_fusion.4.refs_0_), channel_id=1, source_target_pairs={{0,4},{1,5},{4,8},{5,9},{8,12},{9,13},{12,14},{13,15},{14,10},{15,... | collective-permute-start | bytes 884744 | tf_op jit(solution)/shard_map/ppermute | solution.py:226
  6.5 9.1 %collective-permute-start.6 = (bf16[192,768]{1,0:T(8,128)(2,1)S(1)}, bf16[192,768]{1,0:T(8,128)(2,1)S(1)}, u32[]{:S(2)}, u32[]{:S(2)}) collective-permute-start(bf16[192,768]{1,0:T(8,128)(2,1)S(1)} %pad_maximum_fusion.4.refs_0_), channel_id=1, source_target_pairs={{4,0},{5,1},{8,4},{9,5},{12,8},{13,9},{14,12},{15,13},{10,14},{11,... | collective-permute-start | bytes 884744 | tf_op jit(solution)/shard_map/ppermute | solution.py:227
  13.8 10.0 %copy-start.10 = (bf16[192,768]{1,0:T(8,128)(2,1)}, bf16[192,768]{1,0:T(8,128)(2,1)S(1)}, u32[]{:S(2)}) copy-start(bf16[192,768]{1,0:T(8,128)(2,1)S(1)} %collective-permute-done.3.refs_1_) | copy-start | bytes 884740
  13.8 8.5 %collective-permute-start.4 = (bf16[192,768]{1,0:T(8,128)(2,1)S(1)}, bf16[192,768]{1,0:T(8,128)(2,1)S(1)}, u32[]{:S(2)}, u32[]{:S(2)}) collective-permute-start(bf16[192,768]{1,0:T(8,128)(2,1)S(1)} %collective-permute-done.3.refs_1_), channel_id=1, source_target_pairs={{0,4},{1,5},{4,8},{5,9},{8,12},{9,13},{12,14},{13,15},{14,10},{15,... | collective-permute-start | bytes 884744 | tf_op jit(solution)/shard_map/ppermute | solution.py:226
  15.6 8.2 %copy-start.12 = (bf16[192,768]{1,0:T(8,128)(2,1)}, bf16[192,768]{1,0:T(8,128)(2,1)S(1)}, u32[]{:S(2)}) copy-start(bf16[192,768]{1,0:T(8,128)(2,1)S(1)} %collective-permute-done.6.refs_2_) | copy-start | bytes 884740
  15.6 8.2 %collective-permute-start.7 = (bf16[192,768]{1,0:T(8,128)(2,1)S(1)}, bf16[192,768]{1,0:T(8,128)(2,1)S(1)}, u32[]{:S(2)}, u32[]{:S(2)}) collective-permute-start(bf16[192,768]{1,0:T(8,128)(2,1)S(1)} %collective-permute-done.6.refs_2_), channel_id=1, source_target_pairs={{4,0},{5,1},{8,4},{9,5},{12,8},{13,9},{14,12},{15,13},{10,14},{11,... | collective-permute-start | bytes 884744 | tf_op jit(solution)/shard_map/ppermute | solution.py:227
  16.8 7.6 %collective-permute-start.2 = (bf16[192,384]{1,0:T(8,128)(2,1)S(1)}, bf16[192,384]{1,0:T(8,128)(2,1)S(1)}, u32[]{:S(2)}, u32[]{:S(2)}) collective-permute-start(bf16[192,384]{1,0:T(8,128)(2,1)S(1)} %get-tuple-element.30), channel_id=1, source_target_pairs={{0,1},{1,0},{2,3},{3,2},{4,5},{5,4},{6,7},{7,6},{8,9},{9,8},{10,11... | collective-permute-start | bytes 442376 | tf_op jit(solution)/shard_map/ppermute | solution.py:217
  22.3 10.2 %copy-start.14 = (bf16[192,768]{1,0:T(8,128)(2,1)}, bf16[192,768]{1,0:T(8,128)(2,1)S(1)}, u32[]{:S(2)}) copy-start(bf16[192,768]{1,0:T(8,128)(2,1)S(1)} %collective-permute-done.4.refs_3_) | copy-start | bytes 884740
  22.3 7.6 %collective-permute-start.5 = (bf16[192,768]{1,0:T(8,128)(2,1)S(1)}, bf16[192,768]{1,0:T(8,128)(2,1)S(1)}, u32[]{:S(2)}, u32[]{:S(2)}) collective-permute-start(bf16[192,768]{1,0:T(8,128)(2,1)S(1)} %collective-permute-done.4.refs_3_), channel_id=1, source_target_pairs={{0,4},{1,5},{4,8},{5,9},{8,12},{9,13},{12,14},{13,15},{14,10},{15,... | collective-permute-start | bytes 884744 | tf_op jit(solution)/shard_map/ppermute | solution.py:226
  23.8 8.7 %copy-start.16 = (bf16[192,768]{1,0:T(8,128)(2,1)}, bf16[192,768]{1,0:T(8,128)(2,1)S(1)}, u32[]{:S(2)}) copy-start(bf16[192,768]{1,0:T(8,128)(2,1)S(1)} %collective-permute-done.7.refs_4_) | copy-start | bytes 884740
  23.8 7.1 %collective-permute-start.8 = (bf16[192,768]{1,0:T(8,128)(2,1)S(1)}, bf16[192,768]{1,0:T(8,128)(2,1)S(1)}, u32[]{:S(2)}, u32[]{:S(2)}) collective-permute-start(bf16[192,768]{1,0:T(8,128)(2,1)S(1)} %collective-permute-done.7.refs_4_), channel_id=1, source_target_pairs={{4,0},{5,1},{8,4},{9,5},{12,8},{13,9},{14,12},{15,13},{10,14},{11,... | collective-permute-start | bytes 884744 | tf_op jit(solution)/shard_map/ppermute | solution.py:227
  24.4 29.3 %copy-start.18 = (s32[8]{0:T(128)S(1)}, s32[8]{0:T(128)}, u32[]{:S(2)}) copy-start(s32[8]{0:T(128)} %constant.68.clone) | copy-start | bytes 100
  30.0 0.9 copy-start.6
  30.9 1.6 %copy-start.8 = (bf16[192,768]{1,0:T(8,128)(2,1)}, bf16[192,768]{1,0:T(8,128)(2,1)S(1)}, u32[]{:S(2)}) copy-start(bf16[192,768]{1,0:T(8,128)(2,1)S(1)} %collective-permute-done.8.refs_6_) | copy-start | bytes 884740
  30.9 11.1 %collective-permute-start.9 = (bf16[192,1280]{1,0:T(8,128)(2,1)}, bf16[192,1280]{1,0:T(8,128)(2,1)}, u32[]{:S(2)}, u32[]{:S(2)}) collective-permute-start(bf16[192,1280]{1,0:T(8,128)(2,1)} %pad_maximum_fusion), channel_id=1, source_target_pairs={{0,4},{1,5},{4,8},{5,9},{8,12},{9,13},{12,14},{13,15},{14,10},{15,... | collective-permute-start | bytes 1474568 | tf_op jit(solution)/shard_map/ppermute | solution.py:226
  32.5 58.7 %collective-permute-start.1 = (bf16[512,3072]{1,0:T(8,128)(2,1)S(1)}, bf16[512,3072]{1,0:T(8,128)(2,1)}, u32[]{:S(2)}, u32[]{:S(2)}) collective-permute-start(bf16[512,3072]{1,0:T(8,128)(2,1)S(1)} %bitcast.26), channel_id=1, source_target_pairs={{0,1},{1,0},{2,3},{3,2},{4,5},{5,4},{6,7},{7,6},{8,9},{9,8},{10,11... | collective-permute-start | bytes 9437192 | tf_op jit(solution)/shard_map/ppermute | solution.py:217
  32.5 13.9 %collective-permute-start.10 = (bf16[192,1280]{1,0:T(8,128)(2,1)}, bf16[192,1280]{1,0:T(8,128)(2,1)}, u32[]{:S(2)}, u32[]{:S(2)}) collective-permute-start(bf16[192,1280]{1,0:T(8,128)(2,1)} %pad_maximum_fusion), channel_id=1, source_target_pairs={{4,0},{5,1},{8,4},{9,5},{12,8},{13,9},{14,12},{15,13},{10,14},{11,... | collective-permute-start | bytes 1474568 | tf_op jit(solution)/shard_map/ppermute | solution.py:227
  48.9 17.7 %collective-permute-start.23 = (bf16[384,512]{1,0:T(8,128)(2,1)}, bf16[384,512]{1,0:T(8,128)(2,1)}, u32[]{:S(2)}, u32[]{:S(2)}) collective-permute-start(bf16[384,512]{1,0:T(8,128)(2,1)} %pad_maximum_fusion.1), channel_id=1, source_target_pairs={{0,16},{16,0},{1,17},{17,1},{2,18},{18,2},{3,19},{19,3},{4,20},{20... | collective-permute-start | bytes 1179656 | tf_op jit(solution)/shard_map/ppermute | solution.py:220
  50.4 17.8 %collective-permute-start.11 = (bf16[192,1280]{1,0:T(8,128)(2,1)}, bf16[192,1280]{1,0:T(8,128)(2,1)}, u32[]{:S(2)}, u32[]{:S(2)}) collective-permute-start(bf16[192,1280]{1,0:T(8,128)(2,1)} %collective-permute-done.9), channel_id=1, source_target_pairs={{0,4},{1,5},{4,8},{5,9},{8,12},{9,13},{12,14},{13,15},{14,10},{15,... | collective-permute-start | bytes 1474568 | tf_op jit(solution)/shard_map/ppermute | solution.py:226
  51.9 17.8 %collective-permute-start.12 = (bf16[192,1280]{1,0:T(8,128)(2,1)}, bf16[192,1280]{1,0:T(8,128)(2,1)}, u32[]{:S(2)}, u32[]{:S(2)}) collective-permute-start(bf16[192,1280]{1,0:T(8,128)(2,1)} %collective-permute-done.10), channel_id=1, source_target_pairs={{4,0},{5,1},{8,4},{9,5},{12,8},{13,9},{14,12},{15,13},{10,14},{11,... | collective-permute-start | bytes 1474568 | tf_op jit(solution)/shard_map/ppermute | solution.py:227
  53.1 11.0 %collective-permute-start.22 = (bf16[192,512]{1,0:T(8,128)(2,1)}, bf16[192,512]{1,0:T(8,128)(2,1)}, u32[]{:S(2)}, u32[]{:S(2)}) collective-permute-start(bf16[192,512]{1,0:T(8,128)(2,1)} %get-tuple-element.27), channel_id=1, source_target_pairs={{0,16},{16,0},{1,17},{17,1},{2,18},{18,2},{3,19},{19,3},{4,20},{20... | collective-permute-start | bytes 589832 | tf_op jit(solution)/shard_map/ppermute | solution.py:220
  64.1 25.6 %collective-permute-start.19 = (bf16[96,768]{1,0:T(8,128)(2,1)S(1)}, bf16[96,768]{1,0:T(8,128)(2,1)S(1)}, u32[]{:S(2)}, u32[]{:S(2)}) collective-permute-start(bf16[96,768]{1,0:T(8,128)(2,1)S(1)} %slice.130), channel_id=1, source_target_pairs={{0,4},{1,5},{4,8},{5,9},{8,12},{9,13},{12,14},{13,15},{14,10},{15,... | collective-permute-start | bytes 442376 | tf_op jit(solution)/shard_map/ppermute | solution.py:230
  66.6 24.5 %collective-permute-start.20 = (bf16[96,768]{1,0:T(8,128)(2,1)S(1)}, bf16[96,768]{1,0:T(8,128)(2,1)S(1)}, u32[]{:S(2)}, u32[]{:S(2)}) collective-permute-start(bf16[96,768]{1,0:T(8,128)(2,1)S(1)} %slice.131), channel_id=1, source_target_pairs={{4,0},{5,1},{8,4},{9,5},{12,8},{13,9},{14,12},{15,13},{10,14},{11,... | collective-permute-start | bytes 442376 | tf_op jit(solution)/shard_map/ppermute | solution.py:231
  68.1 17.2 %copy-start.4 = (bf16[1536,512]{1,0:T(8,128)(2,1)}, bf16[1536,512]{1,0:T(8,128)(2,1)S(1)}, u32[]{:S(2)}) copy-start(bf16[1536,512]{1,0:T(8,128)(2,1)S(1)} %constant_dynamic-update-slice_fusion.12) | copy-start | bytes 4718596
  68.1 11.6 %collective-permute-start.13 = (bf16[192,1280]{1,0:T(8,128)(2,1)}, bf16[192,1280]{1,0:T(8,128)(2,1)S(1)}, u32[]{:S(2)}, u32[]{:S(2)}) collective-permute-start(bf16[192,1280]{1,0:T(8,128)(2,1)} %collective-permute-done.11), channel_id=1, source_target_pairs={{0,4},{1,5},{4,8},{5,9},{8,12},{9,13},{12,14},{13,15},{14,10},{15,... | collective-permute-start | bytes 1474568 | tf_op jit(solution)/shard_map/ppermute | solution.py:226
  69.8 12.5 %collective-permute-start.14 = (bf16[192,1280]{1,0:T(8,128)(2,1)}, bf16[192,1280]{1,0:T(8,128)(2,1)S(1)}, u32[]{:S(2)}, u32[]{:S(2)}) collective-permute-start(bf16[192,1280]{1,0:T(8,128)(2,1)} %collective-permute-done.12), channel_id=1, source_target_pairs={{4,0},{5,1},{8,4},{9,5},{12,8},{13,9},{14,12},{15,13},{10,14},{11,... | collective-permute-start | bytes 1474568 | tf_op jit(solution)/shard_map/ppermute | solution.py:227
  74.3 16.9 %copy-start.7 = (bf16[192,768]{1,0:T(8,128)(2,1)S(1)}, bf16[192,768]{1,0:T(8,128)(2,1)}, u32[]{:S(2)}) copy-start(bf16[192,768]{1,0:T(8,128)(2,1)} %copy-done.6) | copy-start | bytes 884740
  74.3 16.9 %copy-start.9 = (bf16[192,768]{1,0:T(8,128)(2,1)S(1)}, bf16[192,768]{1,0:T(8,128)(2,1)}, u32[]{:S(2)}) copy-start(bf16[192,768]{1,0:T(8,128)(2,1)} %copy-done.8) | copy-start | bytes 884740
  74.3 16.9 %copy-start.11 = (bf16[192,768]{1,0:T(8,128)(2,1)S(1)}, bf16[192,768]{1,0:T(8,128)(2,1)}, u32[]{:S(2)}) copy-start(bf16[192,768]{1,0:T(8,128)(2,1)} %copy-done.10) | copy-start | bytes 884740
  74.3 16.9 %copy-start.13 = (bf16[192,768]{1,0:T(8,128)(2,1)S(1)}, bf16[192,768]{1,0:T(8,128)(2,1)}, u32[]{:S(2)}) copy-start(bf16[192,768]{1,0:T(8,128)(2,1)} %copy-done.12) | copy-start | bytes 884740
  74.3 16.9 %copy-start.15 = (bf16[192,768]{1,0:T(8,128)(2,1)S(1)}, bf16[192,768]{1,0:T(8,128)(2,1)}, u32[]{:S(2)}) copy-start(bf16[192,768]{1,0:T(8,128)(2,1)} %copy-done.14) | copy-start | bytes 884740
  74.3 16.9 %copy-start.17 = (bf16[192,768]{1,0:T(8,128)(2,1)S(1)}, bf16[192,768]{1,0:T(8,128)(2,1)}, u32[]{:S(2)}) copy-start(bf16[192,768]{1,0:T(8,128)(2,1)} %copy-done.16) | copy-start | bytes 884740
  79.7 9.9 %copy-start.19 = (bf16[192,1280]{1,0:T(8,128)(2,1)}, bf16[192,1280]{1,0:T(8,128)(2,1)S(1)}, u32[]{:S(2)}) copy-start(bf16[192,1280]{1,0:T(8,128)(2,1)S(1)} %collective-permute-done.13) | copy-start | bytes 1474564
  79.7 24.6 %collective-permute-start.24 = (bf16[384,512]{1,0:T(8,128)(2,1)}, bf16[384,512]{1,0:T(8,128)(2,1)}, u32[]{:S(2)}, u32[]{:S(2)}) collective-permute-start(bf16[384,512]{1,0:T(8,128)(2,1)} %pad_maximum_fusion.2), channel_id=1, source_target_pairs={{0,16},{16,0},{1,17},{17,1},{2,18},{18,2},{3,19},{19,3},{4,20},{20... | collective-permute-start | bytes 1179656 | tf_op jit(solution)/shard_map/ppermute | solution.py:220
  82.3 8.8 %copy-start.20 = (bf16[192,1280]{1,0:T(8,128)(2,1)}, bf16[192,1280]{1,0:T(8,128)(2,1)S(1)}, u32[]{:S(2)}) copy-start(bf16[192,1280]{1,0:T(8,128)(2,1)S(1)} %collective-permute-done.14) | copy-start | bytes 1474564
  82.3 6.2 %collective-permute-start.15 = (bf16[96,1280]{1,0:T(8,128)(2,1)S(1)}, bf16[96,1280]{1,0:T(8,128)(2,1)S(1)}, u32[]{:S(2)}, u32[]{:S(2)}) collective-permute-start(bf16[96,1280]{1,0:T(8,128)(2,1)S(1)} %slice.122), channel_id=1, source_target_pairs={{0,4},{1,5},{4,8},{5,9},{8,12},{9,13},{12,14},{13,15},{14,10},{15,... | collective-permute-start | bytes 737288 | tf_op jit(solution)/shard_map/ppermute | solution.py:230
  88.5 2.6 %copy-start.22 = (bf16[96,1280]{1,0:T(8,128)(2,1)}, bf16[96,1280]{1,0:T(8,128)(2,1)S(1)}, u32[]{:S(2)}) copy-start(bf16[96,1280]{1,0:T(8,128)(2,1)S(1)} %collective-permute-done.15) | copy-start | bytes 737284
  88.5 13.6 %collective-permute-start.16 = (bf16[96,1280]{1,0:T(8,128)(2,1)}, bf16[96,1280]{1,0:T(8,128)(2,1)}, u32[]{:S(2)}, u32[]{:S(2)}) collective-permute-start(bf16[96,1280]{1,0:T(8,128)(2,1)} %slice.124), channel_id=1, source_target_pairs={{4,0},{5,1},{8,4},{9,5},{12,8},{13,9},{14,12},{15,13},{10,14},{11,... | collective-permute-start | bytes 737288 | tf_op jit(solution)/shard_map/ppermute | solution.py:231
  89.6 15.8 %collective-permute-start.25 = (bf16[384,512]{1,0:T(8,128)(2,1)}, bf16[384,512]{1,0:T(8,128)(2,1)}, u32[]{:S(2)}, u32[]{:S(2)}) collective-permute-start(bf16[384,512]{1,0:T(8,128)(2,1)} %pad_maximum_fusion.3), channel_id=1, source_target_pairs={{0,16},{16,0},{1,17},{17,1},{2,18},{18,2},{3,19},{19,3},{4,20},{20... | collective-permute-start | bytes 1179656 | tf_op jit(solution)/shard_map/ppermute | solution.py:220
  97.7 6.7 %copy-start.5 = (bf16[1536,512]{1,0:T(8,128)(2,1)S(1)}, bf16[1536,512]{1,0:T(8,128)(2,1)}, u32[]{:S(2)}) copy-start(bf16[1536,512]{1,0:T(8,128)(2,1)} %copy-done.4) | copy-start | bytes 4718596
  97.7 26.5 %all-to-all-start = ((bf16[8,2,2,32,384]{4,3,2,1,0:T(8,128)(2,1)}), bf16[8,2,2,32,384]{4,3,2,1,0:T(8,128)(2,1)S(1)}, u32[]{:S(2)}, u32[]{:S(2)}) async-start(bf16[8,2,2,32,384]{4,3,2,1,0:T(8,128)(2,1)} %temporal_projection.1), calls=%async_computation | async-start | bytes 1572864 | tf_op jit(solution)/shard_map/all_to_all | solution.py:280
  102.1 7.4 %copy-start.24 = (s32[16]{0:T(128)S(1)}, s32[16]{0:T(128)}, u32[]{:S(2)}) copy-start(s32[16]{0:T(128)} %param.10) | copy-start | bytes 196
  103.7 5.7 %collective-permute-start.26 = (bf16[192,512]{1,0:T(8,128)(2,1)S(1)}, bf16[192,512]{1,0:T(8,128)(2,1)S(1)}, u32[]{:S(2)}, u32[]{:S(2)}) collective-permute-start(bf16[192,512]{1,0:T(8,128)(2,1)S(1)} %pad_maximum_fusion.5), channel_id=1, source_target_pairs={{0,16},{16,0},{1,17},{17,1},{2,18},{18,2},{3,19},{19,3},{4,20},{20... | collective-permute-start | bytes 589832 | tf_op jit(solution)/shard_map/ppermute | solution.py:220
  105.4 34.0 %collective-permute-start.21 = (bf16[1536,512]{1,0:T(8,128)(2,1)}, bf16[1536,512]{1,0:T(8,128)(2,1)}, u32[]{:S(2)}, u32[]{:S(2)}) collective-permute-start(bf16[1536,512]{1,0:T(8,128)(2,1)} %get-tuple-element.38.refs_0_), channel_id=1, source_target_pairs={{0,1},{1,0},{2,3},{3,2},{4,5},{5,4},{6,7},{7,6},{8,9},{9,8},{10,11... | collective-permute-start | bytes 4718600 | tf_op jit(solution)/shard_map/ppermute | solution.py:217
  109.5 29.9 %collective-permute-start.27 = (bf16[1536,512]{1,0:T(8,128)(2,1)S(1)}, bf16[1536,512]{1,0:T(8,128)(2,1)}, u32[]{:S(2)}, u32[]{:S(2)}) collective-permute-start(bf16[1536,512]{1,0:T(8,128)(2,1)S(1)} %constant_dynamic-update-slice_fusion.9.refs_2_), channel_id=1, source_target_pairs={{0,1},{1,0},{2,3},{3,2},{4,5},{5,4},{6,7},{7,6},{8,9},{9,8},{10,11... | collective-permute-start | bytes 4718600 | tf_op jit(solution)/shard_map/ppermute | solution.py:217
  110.9 5.2 %copy-start.21 = (bf16[192,1280]{1,0:T(8,128)(2,1)S(1)}, bf16[192,1280]{1,0:T(8,128)(2,1)}, u32[]{:S(2)}) copy-start(bf16[192,1280]{1,0:T(8,128)(2,1)} %copy-done.20) | copy-start | bytes 1474564
  110.9 5.2 %copy-start.23 = (bf16[96,1280]{1,0:T(8,128)(2,1)S(1)}, bf16[96,1280]{1,0:T(8,128)(2,1)}, u32[]{:S(2)}) copy-start(bf16[96,1280]{1,0:T(8,128)(2,1)} %copy-done.22) | copy-start | bytes 737284
  112.0 5.1 %copy-start.3 = (bf16[1,512,3072]{2,1,0:T(8,128)(2,1)S(1)}, bf16[1,512,3072]{2,1,0:T(8,128)(2,1)}, u32[]{:S(2)}) copy-start(bf16[1,512,3072]{2,1,0:T(8,128)(2,1)} %param.7) | copy-start | bytes 9437188
  126.2 18.7 %all-to-all-start.1 = ((bf16[32,32,128]{2,1,0:T(8,128)(2,1)}), bf16[32,32,128]{2,1,0:T(8,128)(2,1)S(1)}, u32[]{:S(2)}, u32[]{:S(2)}) async-start(bf16[32,32,128]{2,1,0:T(8,128)(2,1)} %bitcast.13), calls=%async_computation.1 | async-start | bytes 524288 | tf_op jit(solution)/shard_map/all_to_all | solution.py:305
  131.4 7.8 %collective-permute-start.17 = (bf16[2,256,128]{2,1,0:T(8,128)(2,1)S(1)}, bf16[2,256,128]{2,1,0:T(8,128)(2,1)S(1)}, u32[]{:S(2)}, u32[]{:S(2)}) collective-permute-start(bf16[2,256,128]{2,1,0:T(8,128)(2,1)S(1)} %get-tuple-element.33), channel_id=1, source_target_pairs={{0,16},{16,0},{1,17},{17,1},{2,18},{18,2},{3,19},{19,3},{4,20},{20... | collective-permute-start | bytes 393224 | tf_op jit(solution)/shard_map/ppermute | solution.py:220
  139.3 5.7 %collective-permute-start.18 = (bf16[2,256,128]{2,1,0:T(8,128)(2,1)S(1)}, bf16[2,256,128]{2,1,0:T(8,128)(2,1)S(1)}, u32[]{:S(2)}, u32[]{:S(2)}) collective-permute-start(bf16[2,256,128]{2,1,0:T(8,128)(2,1)S(1)} %pad_maximum_fusion.6), channel_id=1, source_target_pairs={{0,1},{1,0},{2,3},{3,2},{4,5},{5,4},{6,7},{7,6},{8,9},{9,8},{10,11... | collective-permute-start | bytes 393224 | tf_op jit(solution)/shard_map/ppermute | solution.py:217
  142.3 2.6 %copy-start = (bf16[3072,1024]{1,0:T(8,128)(2,1)}, bf16[3072,1024]{1,0:T(8,128)(2,1)S(1)}, u32[]{:S(2)}) copy-start(bf16[3072,1024]{1,0:T(8,128)(2,1)S(1)} %place_out_weight.1.weight_ref) | copy-start | bytes 18874372
  145.0 2.8 %copy-start.1 = (bf16[3072,1024]{1,0:T(8,128)(2,1)S(1)}, bf16[3072,1024]{1,0:T(8,128)(2,1)}, u32[]{:S(2)}) copy-start(bf16[3072,1024]{1,0:T(8,128)(2,1)} %copy-done) | copy-start | bytes 18874372

commit v3 on v2

v3 whole, which is shorter than its diff:
```python
import functools
import math

import jax
import jax.numpy as jnp
from jax import lax
from jax.experimental import pallas as pl
from jax.experimental.pallas import tpu as pltpu
from jax.sharding import PartitionSpec as P

HEAD = 128
HS_DEV = 2
SCALE = 1.0 / math.sqrt(HEAD)
MIB = 1024 * 1024
FIRST = 25_000_000_000


def kernel_call(body, out_shape, args, flops, name, whole=(), scratch=(), limit=16 * MIB):
    bytes_moved = sum(a.size * a.dtype.itemsize for a in args)

    def space(i, a):
        if a.dtype == jnp.int32:
            return pltpu.SMEM
        return pltpu.VMEM if i in whole else pl.ANY

    return pl.pallas_call(
        body,
        out_shape=out_shape,
        in_specs=[pl.BlockSpec(memory_space=space(i, a)) for i, a in enumerate(args)],
        out_specs=pl.BlockSpec(memory_space=pltpu.VMEM),
        scratch_shapes=list(scratch),
        compiler_params=pltpu.CompilerParams(vmem_limit_bytes=limit),
        cost_estimate=pl.CostEstimate(flops=flops, bytes_accessed=bytes_moved, transcendentals=0),
        name=name,
    )(*args)


def weight_copies(depth, meta_ref, piece_refs, weight, sems):
    core = meta_ref[0]
    columns = weight.shape[1]
    slot, first = 0, 0
    copies = []
    for ref in piece_refs:
        rows = min(depth, ref.shape[0])
        for start in range(0, ref.shape[0], rows):
            chip = meta_ref[2 + slot]
            for k in range(2):
                at = (chip * 2 + (core if k == 0 else 1 - core)) * depth + first
                copies.append(
                    pltpu.make_async_copy(
                        ref.at[pl.ds(start, rows), pl.ds(k * columns, columns)],
                        weight.at[pl.ds(pl.multiple_of(at, 16), rows), :],
                        sems.at[len(copies)],
                    )
                )
            first += rows
            if first == depth:
                slot, first = slot + 1, 0
    return copies


def load_all(depth, meta_ref, own_ref, other_ref, piece_refs, weight, frames, sems):
    copies = weight_copies(depth, meta_ref, piece_refs, weight, sems)
    copies.append(pltpu.make_async_copy(own_ref, frames.at[0], sems.at[len(copies)]))
    last = pltpu.make_async_copy(other_ref, frames.at[1], sems.at[len(copies)])
    for copy in copies:
        copy.start()
    last.start()
    for copy in copies:
        copy.wait()
    return last


def load_scratch(copies, patches, width):
    return [
        pltpu.VMEM((width, 3 * HEAD), jnp.bfloat16),
        pltpu.VMEM((2, patches, width), jnp.bfloat16),
        pltpu.SemaphoreType.DMA((copies + 2,)),
    ]


def most_body(depth, meta_ref, own_ref, other_ref, *refs):
    *piece_refs, out_ref, weight, frames, sems = refs
    missing = meta_ref[2 + len(piece_refs)] * 2 * depth
    weight[pl.ds(pl.multiple_of(missing, 16), 2 * depth), :] = jnp.zeros(
        (2 * depth, weight.shape[1]), weight.dtype
    )
    last = load_all(depth, meta_ref, own_ref, other_ref, piece_refs, weight, frames, sems)
    patches = own_ref.shape[0]
    half = patches // 2
    for frame in range(2):
        if frame == 1:
            last.wait()
        for first in range(0, patches, half):
            out_ref[frame * patches + first : frame * patches + first + half, :] = jnp.dot(
                frames[frame, first : first + half, :],
                weight[...],
                preferred_element_type=jnp.float32,
            )


def rest_body(depth, chips, n_st, direct, meta_ref, own_ref, other_ref, piece_ref, most_ref, *refs):
    out_ref, weight, frames, sems = refs
    patches = own_ref.shape[0]
    part = patches // (n_st * chips)
    if own_ref.shape[1] != 2 * depth:
        share = pl.ds(pl.multiple_of(meta_ref[1 + chips] * 2 * depth, 2 * depth), 2 * depth)
        own_ref, other_ref = own_ref.at[:, share], other_ref.at[:, share]
    copies = [
        pltpu.make_async_copy(ref, frames.at[k], sems.at[k])
        for k, ref in enumerate((own_ref, other_ref))
    ]
    for copy in copies:
        copy.start()
    core = meta_ref[0]
    columns = weight.shape[1]
    for k in range(2):
        at = (core if k == 0 else 1 - core) * depth
        weight[pl.ds(pl.multiple_of(at, 16), depth), :] = piece_ref[
            :, k * columns : (k + 1) * columns
        ]
    half = patches // 2
    for frame in range(2):
        copies[frame].wait()
        for first in range(0, patches, half):
            here = slice(frame * patches + first, frame * patches + first + half)
            result = most_ref[here, :] + jnp.dot(
                frames[frame, first : first + half, :],
                weight[...],
                preferred_element_type=jnp.float32,
            )
            result = result.astype(jnp.bfloat16)
            if not direct:
                out_ref[here, :] = result
                continue
            for at in range(first, first + half, part):
                block = at // part
                out_ref[block % chips, frame, block // chips] = result[
                    at - first : at - first + part
                ]


def spatial_body(depth, n_st, meta_ref, own_ref, other_ref, *refs):
    *piece_refs, out_ref, weight, frames, sems, packed = refs
    last = load_all(depth, meta_ref, own_ref, other_ref, piece_refs, weight, frames, sems)
    patches = own_ref.shape[0]
    part = patches // n_st
    half = patches // 2
    for frame in range(2):
        if frame == 1:
            last.wait()
        for first in range(0, patches, half):
            packed[first : first + half, :] = jnp.dot(
                frames[frame, first : first + half, :],
                weight[...],
                preferred_element_type=jnp.float32,
            ).astype(jnp.bfloat16)
        for group in range(n_st):
            rows = slice(group * part, (group + 1) * part)
            scores = lax.dot_general(
                packed[rows, :HEAD],
                packed[:, HEAD : 2 * HEAD],
                (((1,), (1,)), ((), ())),
                preferred_element_type=jnp.float32,
            )
            scores = scores * SCALE
            expo = jnp.exp(scores - jnp.max(scores, axis=-1, keepdims=True))
            total = jnp.sum(expo, axis=-1, keepdims=True)
            result = jnp.dot(
                expo.astype(jnp.bfloat16),
                packed[:, 2 * HEAD :],
                preferred_element_type=jnp.float32,
            )
            result = (result / total).astype(jnp.bfloat16)
            place = (group + meta_ref[1]) % 2 if n_st == 2 else group
            out_ref[place, frame] = result


def temporal_body(tile, meta_ref, qkv_ref, out_ref):
    frames, rows = qkv_ref.shape[0], qkv_ref.shape[1]
    part = out_ref.shape[2]
    flip = meta_ref[frames]
    size = frames * tile
    row_at = lax.broadcasted_iota(jnp.int32, (size, size), 0)
    col_at = lax.broadcasted_iota(jnp.int32, (size, size), 1)
    row_seg = jnp.zeros((size, 1), jnp.int32)
    col_seg = jnp.zeros((1, size), jnp.int32)
    row_frame = lax.broadcasted_iota(jnp.int32, (size, 1), 0) // tile
    col_frame = lax.broadcasted_iota(jnp.int32, (1, size), 1) // tile
    for frame in range(frames):
        clip = meta_ref[frame]
        row_seg = jnp.where(row_frame == frame, clip, row_seg)
        col_seg = jnp.where(col_frame == frame, clip, col_seg)
    keep = (row_at % tile == col_at % tile) & (row_seg == col_seg)
    for start in range(0, rows, tile):
        block = qkv_ref[:, start : start + tile, :].reshape(size, 3 * HEAD)
        scores = lax.dot_general(
            block[:, :HEAD],
            block[:, HEAD : 2 * HEAD],
            (((1,), (1,)), ((), ())),
            preferred_element_type=jnp.float32,
        )
        scores = jnp.where(keep, scores * SCALE, jnp.float32(-1e30))
        expo = jnp.exp(scores - jnp.max(scores, axis=-1, keepdims=True))
        total = jnp.sum(expo, axis=-1, keepdims=True)
        result = jnp.dot(
            expo.astype(jnp.bfloat16), block[:, 2 * HEAD :], preferred_element_type=jnp.float32
        )
        result = (result / total).astype(jnp.bfloat16).reshape(frames, tile, HEAD)
        for pair in range(frames // 2):
            for k in range(2):
                at = 2 * pair + (flip if k == 0 else 1 - flip)
                if part % tile:
                    out_ref[0, at, start : start + tile, :] = result[2 * pair + k]
                else:
                    low = start % part
                    out_ref[start // part, at, low : low + tile, :] = result[2 * pair + k]


def pack_body(split, *refs):
    *piece_refs, out_ref, sems = refs
    copies = []
    for i, ref in enumerate(piece_refs):
        rows, columns = ref.shape
        copies.append(
            pltpu.make_async_copy(
                ref.at[:, pl.ds(split, columns - split)],
                out_ref.at[pl.ds(i * rows, rows), :],
                sems.at[i],
            )
        )
    for copy in copies:
        copy.start()
    for copy in copies:
        copy.wait()


def order_body(received_ref, out_ref):
    n_st, chips, _, part, _ = received_ref.shape
    for group in range(n_st):
        for chip in range(chips):
            for k in range(2):
                out_ref[
                    group, chip * part : (chip + 1) * part, k * HEAD : (k + 1) * HEAD
                ] = received_ref[group, chip, k]


def out_body(
    depth, count, meta_ref, mine_ref, peer_ref, core_ref, far_ref, temporal_ref, *refs
):
    *weight_refs, out_ref, heads, weight, sems = refs
    core, st = meta_ref[0], meta_ref[1]
    n_st, chips = temporal_ref.shape[0], out_ref.shape[1] // (2 * depth)
    copies = [[] for _ in range(chips)]
    for kind in range(4):
        group = st if kind < 2 else 1 - st
        side = core if kind % 2 == 0 else 1 - core
        slot = 0
        for ref in weight_refs[kind * count : (kind + 1) * count]:
            for first in range(0, ref.shape[0], depth):
                at = slot * 2 * depth + side * depth
                copies[slot].append(
                    pltpu.make_async_copy(
                        ref.at[pl.ds(first, depth), :],
                        weight.at[group, pl.ds(pl.multiple_of(at, 16), depth), :],
                        sems.at[slot, kind],
                    )
                )
                slot += 1
    for copy in sum(copies, []):
        copy.start()
    mine, far = pl.multiple_of(core * HEAD, HEAD), pl.multiple_of((1 - core) * HEAD, HEAD)
    heads[st, :, pl.ds(mine, HEAD)] = mine_ref[...]
    heads[1 - st, :, pl.ds(mine, HEAD)] = peer_ref[...]
    heads[st, :, pl.ds(far, HEAD)] = core_ref[...]
    heads[1 - st, :, pl.ds(far, HEAD)] = far_ref[...]
    heads[:, :, HS_DEV * HEAD :] = temporal_ref[...]
    chip_width = 2 * depth
    for slot in range(0, chips, 2):
        for copy in copies[slot] + copies[slot + 1]:
            copy.wait()
        total = 0.0
        for group in range(n_st):
            total += lax.dot_general(
                heads[group],
                weight[group, slot * chip_width : (slot + 2) * chip_width, :],
                (((1,), (1,)), ((), ())),
                preferred_element_type=jnp.float32,
            )
        total = total.astype(jnp.bfloat16)
        for k in range(2):
            at = pl.multiple_of(meta_ref[2 + slot + k] * chip_width, chip_width)
            out_ref[:, pl.ds(at, chip_width)] = total[:, k * chip_width : (k + 1) * chip_width]


def shards(n_st, n_fsdp, normed, qkv_weight, out_weight, segment_ids):
    patches, width = normed.shape[1], normed.shape[2]
    frames = n_fsdp
    depth = qkv_weight.shape[0]
    chips = n_fsdp // 2
    part = patches // (n_st * chips)
    rows = patches // n_st
    direct = part % 16 == 0
    ring = list(range(0, chips, 2)) + list(range(chips - 1, 0, -2))
    place = [ring.index(chip) for chip in range(chips)]
    me = lax.axis_index("fsdp")
    st = lax.axis_index("st")
    chip, core = me // 2, me % 2
    spot = jnp.array(place, jnp.int32)[chip]

    swap = [(i, i ^ 1) for i in range(n_fsdp)]
    forward = [
        (2 * ring[i] + c, 2 * ring[(i + 1) % chips] + c) for i in range(chips) for c in range(2)
    ]
    backward = [(b, a) for a, b in forward]

    def to_core(x):
        return lax.ppermute(x, "fsdp", swap)

    def to_peer(x):
        return lax.ppermute(x, "st", [(0, 1), (1, 0)])

    def ring_gather(piece):
        pieces = [piece]
        ahead = behind = piece
        for _ in range(1, chips // 2):
            gate = yield pieces, ahead
            if gate is not None:
                ahead, behind, _ = lax.optimization_barrier((ahead, behind, gate))
            ahead = lax.ppermute(ahead, "fsdp", forward)
            behind = lax.ppermute(behind, "fsdp", backward)
            pieces = pieces + [ahead, behind]
        sent = jnp.where(core == 0, ahead, behind)
        gate = yield pieces, sent
        if gate is not None:
            sent, _ = lax.optimization_barrier((sent, gate))
        both = [edge for edge in forward if edge[0] % 2 == 0]
        both += [edge for edge in backward if edge[0] % 2 == 1]
        yield pieces + [lax.ppermute(sent, "fsdp", both)], None

    def run(ring, steps):
        for _ in range(steps):
            state = next(ring)
        return state

    offsets = [0]
    for d in range(1, chips // 2):
        offsets += [chips - d, d]
    offsets.append(chips // 2)
    sources = jnp.array(ring, jnp.int32)[(spot + jnp.array(offsets, jnp.int32)) % chips]
    here = jnp.stack([core, st])
    ring_meta = jnp.concatenate([here, sources]).astype(jnp.int32)

    by_head = qkv_weight.transpose(1, 0, 2)

    def take_head(heads):
        mine = lax.dynamic_index_in_dim(heads, core, 0, keepdims=False)
        other = lax.dynamic_index_in_dim(heads, 1 - core, 0, keepdims=False)
        return jnp.concatenate([mine, to_core(other)], axis=1)

    temporal_piece = take_head(lax.optimization_barrier(by_head[HS_DEV:]))
    own = normed.reshape(patches, width)

    temporal_ring = ring_gather(temporal_piece)
    _, last_sent = run(temporal_ring, chips // 2)
    pieces, _ = next(temporal_ring)
    own, later_head, _ = lax.optimization_barrier((own, by_head[:HS_DEV], temporal_piece))
    other = to_core(own)
    spatial_piece = take_head(later_head)
    split = spatial_piece.shape[1]
    both_ring = ring_gather(jnp.concatenate([spatial_piece, out_weight], axis=1))
    next(both_ring)
    first_pieces, _ = both_ring.send(last_sent)
    head_flops = 4 * patches * width * 3 * HEAD
    shape = (chips, 2, n_st, part, 3 * HEAD) if direct else (2 * patches, 3 * HEAD)
    most = kernel_call(
        functools.partial(most_body, depth),
        jax.ShapeDtypeStruct((2 * patches, 3 * HEAD), jnp.float32),
        [ring_meta, own, other, *pieces[:-1]],
        head_flops,
        "temporal_projection",
        scratch=load_scratch(2 * chips, patches, width),
    )
    shares = (own, other)
    if 2 * depth % 128:
        shares = [
            lax.dynamic_slice_in_dim(x, sources[-1] * 2 * depth, 2 * depth, 1) for x in shares
        ]
    temporal = projected = kernel_call(
        functools.partial(rest_body, depth, chips, n_st, direct),
        jax.ShapeDtypeStruct(shape, jnp.bfloat16),
        [ring_meta, *shares, pieces[-1], most],
        head_flops // chips,
        "temporal_projection_rest",
        whole=(3, 4),
        scratch=[
            pltpu.VMEM((2 * depth, 3 * HEAD), jnp.bfloat16),
            pltpu.VMEM((2, patches, 2 * depth), jnp.bfloat16),
            pltpu.SemaphoreType.DMA((2,)),
        ],
    )
    if not direct:
        temporal = temporal.reshape(2, n_st, chips, part, 3 * HEAD).transpose(2, 0, 1, 3, 4)
    same_core = [[2 * i + c for i in range(chips)] for c in range(2)]
    temporal = lax.all_to_all(
        temporal,
        "fsdp",
        split_axis=0,
        concat_axis=0,
        tiled=True,
        axis_index_groups=same_core,
    ).reshape(frames, n_st * part, 3 * HEAD)
    pairs = segment_ids.reshape(chips, 2)
    pairs = jnp.where(core == 0, pairs, pairs[:, ::-1]).reshape(frames)
    clips = jnp.concatenate([pairs, core.reshape(1)]).astype(jnp.int32)
    tile = min(n_st * part, max(16, 256 // frames))
    if part % tile == 0:
        shape = (n_st, frames, part, HEAD)
    else:
        shape = (1, frames, n_st * part, HEAD)
    result = attention = kernel_call(
        functools.partial(temporal_body, tile),
        jax.ShapeDtypeStruct(shape, jnp.bfloat16),
        [clips, temporal],
        FIRST,
        "temporal_attention",
        whole=(1,),
    )
    if part % tile:
        result = result.reshape(frames, n_st, part, HEAD).transpose(1, 0, 2, 3)
    result = lax.all_to_all(
        result.reshape(n_st * frames, part, HEAD),
        ("st", "fsdp"),
        split_axis=0,
        concat_axis=0,
        tiled=True,
    )
    temporal_heads = result.reshape(n_st, chips, 2, part, HEAD)

    def pack(group):
        return kernel_call(
            functools.partial(pack_body, split),
            jax.ShapeDtypeStruct((depth * len(group), out_weight.shape[1]), jnp.bfloat16),
            group,
            0,
            "pack_out_weight",
            scratch=[pltpu.SemaphoreType.DMA((len(group),))],
            limit=60 * MIB,
        )

    early = n_st == 2 and direct
    parts, _ = both_ring.send(projected)
    if early:
        kinds = [pack(parts[:3]), pack(parts[3:5])]
        peers = [to_peer(k) for k in kinds]
    parts, _ = run(both_ring, chips // 2 - 3)
    parts, _ = both_ring.send(tuple(peers) if early else attention)
    spatial = kernel_call(
        functools.partial(spatial_body, depth, n_st),
        jax.ShapeDtypeStruct((n_st, 2, rows, HEAD), jnp.bfloat16),
        [ring_meta, own, other, *parts],
        0,
        "spatial_heads",
        scratch=[
            *load_scratch(2 * chips + 2, patches, width),
            pltpu.VMEM((patches, 3 * HEAD), jnp.bfloat16),
        ],
    )

    if early:
        temporal_heads = kernel_call(
            order_body,
            jax.ShapeDtypeStruct((n_st, rows, 2 * HEAD), jnp.bfloat16),
            [temporal_heads],
            FIRST,
            "temporal_heads",
            whole=(0,),
        )
        across = [(i, (i ^ 1 ^ n_fsdp)) for i in range(n_st * n_fsdp)]
        received = [
            to_peer(spatial[1, 0]),
            to_core(spatial[0, 1]),
            lax.ppermute(spatial[1, 1], ("st", "fsdp"), across),
        ]

        kinds += [pack(parts[at : at + 2]) for at in range(5, chips, 2)]
        peers += [to_peer(k) for k in kinds[2:]]
        count = len(kinds)
        kinds += [to_core(k) for k in kinds] + peers
        peers = lax.optimization_barrier((*peers, attention))[:-1]
        kinds += [to_core(k) for k in peers]
        attended = kernel_call(
            functools.partial(out_body, depth, count),
            jax.ShapeDtypeStruct((rows, width), jnp.bfloat16),
            [ring_meta, spatial[0, 0], *received, temporal_heads, *kinds],
            4 * rows * width * out_weight.shape[1],
            "out_projection",
            whole=(1, 2, 3, 4, 5),
            scratch=[
                pltpu.VMEM((n_st, rows, out_weight.shape[1]), jnp.bfloat16),
                pltpu.VMEM((n_st, width, out_weight.shape[1]), jnp.bfloat16),
                pltpu.SemaphoreType.DMA((chips, 4)),
            ],
            limit=60 * MIB,
        )
        return attended.reshape(1, rows, width)

    def by_core(mine, other, axis):
        return jnp.where(
            core == 0,
            jnp.concatenate([mine, other], axis=axis),
            jnp.concatenate([other, mine], axis=axis),
        )

    if n_st == 2:
        spatial = jnp.where(st == 0, spatial, spatial[::-1])
    spatial = lax.all_to_all(spatial, "st", split_axis=0, concat_axis=0, tiled=True)
    spatial = by_core(spatial[:, 0, :, None], to_core(spatial[:, 1])[:, :, None], 2)
    heads = jnp.concatenate(
        [
            spatial.transpose(1, 0, 2, 3),
            temporal_heads.transpose(1, 3, 0, 2, 4).reshape(rows, n_st, 2, HEAD),
        ],
        axis=2,
    ).reshape(rows, -1)
    weight = jnp.concatenate([p[:, split:] for p in parts])
    weight = lax.all_gather(weight, "st", axis=1, tiled=True)
    weight = by_core(
        weight.reshape(chips, 1, depth, -1), to_core(weight).reshape(chips, 1, depth, -1), 1
    )
    order = jnp.zeros((chips,), jnp.int32).at[sources].set(jnp.arange(chips, dtype=jnp.int32))
    attended = lax.dot_general(
        heads,
        weight[order].reshape(width, -1),
        (((1,), (1,)), ((), ())),
        preferred_element_type=jnp.float32,
    ).astype(jnp.bfloat16)
    return attended.reshape(1, rows, width)


def solution(mesh):
    return jax.shard_map(
        functools.partial(shards, mesh.shape["st"], mesh.shape["fsdp"]),
        mesh=mesh,
        in_specs=(P("fsdp", None, None), P("fsdp", "st", None), P("fsdp", "st"), P()),
        out_specs=P("fsdp", "st", None),
        check_vma=False,
    )
```

time: 152 us -> 139 us (0.914)
  local copies, waits for them, and re-layouts: 35.5 us -> 13.5 us
  Pallas kernels: 22.1 us -> 31.5 us
    slice x23 -> x0, local copies, waits for them, and re-layouts: 21.5 us -> none  [the longest x9 11.8 us: shards(): out_groups = [jnp.concatenate([p[:, split:] for p in g]) for g in groups]]
    ppermute x6 -> x5, waiting for transfers between devices: 16.8 us -> 5.75 us  [to_peer(): return lax.ppermute(x, 'st', [(0, 1), (1, 0)])]
    pallas_call x5 -> x10, Pallas kernels: 22.1 us -> 31.5 us  [kernel_call(): pl.pallas_call(body, out_shape=out_shape, in_specs=[pl.BlockSpec(memory_s...]
    ppermute x6, waiting for transfers between devices: 28.5 us -> 37.7 us  [ring_gather(): ahead = lax.ppermute(ahead, 'fsdp', forward)]
    ppermute x6 -> x12, starting transfers between devices: 0.81 us -> 3.56 us  [to_core(): return lax.ppermute(x, 'fsdp', swap)]
    select_n x0 -> x2, other arithmetic: none -> 2.65 us  [ring_gather(): sent = jnp.where(core == 0, ahead, behind)]
    all_to_all x1, starting transfers between devices: 5.16 us -> 2.77 us  [shards(): lax.all_to_all(result.reshape(n_st * frames, part, HEAD), ('st', 'fsdp'),...]
    concatenate x6 -> x2, other arithmetic: 4.21 us -> 1.98 us  [the longest x1 1.91 us: shards(): jnp.concatenate([spatial_piece, out_weight], axis=1)]
  transfers between devices with their start and end apart: 30 -> 34, of which waited for: 13 -> 14; matrix products, arithmetic and copies ran while one was open for 22% -> 6% of each run, Pallas kernels for 12% -> 18%
where the time goes in v3:
time: 139 us; the launch traced here: 138 us
  waiting for transfers between devices  51.9 us (37%)
  starting transfers between devices  35.2 us (25%)
  Pallas kernels  31.5 us (23%)
  local copies, waits for them, and re-layouts  13.5 us (10%)
  other arithmetic  5.39 us (4%)
    ppermute x6, waiting for transfers between devices, ring_gather(): ahead = lax.ppermute(ahead, 'fsdp', forward)  37.7 us
    pallas_call x10, Pallas kernels, kernel_call(): pl.pallas_call(body, out_shape=out_shape, in_specs=[pl.BlockSpec(memory_s...  31.5 us
    ppermute x6, starting transfers between devices, ring_gather(): ahead = lax.ppermute(ahead, 'fsdp', forward)  10.8 us
    unnamed x47, local copies, waits for them, and re-layouts  8.86 us
    ppermute x5, waiting for transfers between devices, to_peer(): return lax.ppermute(x, 'st', [(0, 1), (1, 0)])  5.75 us
    ppermute x5, starting transfers between devices, to_peer(): return lax.ppermute(x, 'st', [(0, 1), (1, 0)])  5.69 us
    ppermute x2, starting transfers between devices, ring_gather(): yield (pieces + [lax.ppermute(sent, 'fsdp', both)], None)  5.49 us
    all_to_all x1, starting transfers between devices, shards(): lax.all_to_all(temporal, 'fsdp', split_axis=0, concat_axis=0, tiled=True,...  4.82 us
  transfers between devices with their start and end apart: 34, of which 14 were waited for; matrix products, arithmetic and copies ran while one was open for 6% of the time, Pallas kernels for 18%

profile of v3, /device:TPU:0, one launch (start us, length us, event | category | flops | bytes accessed | tf_op | source)
XLA Modules:
  0.0 137.9 jit_solution(1407940699007726496)
XLA Ops:
  0.0 1.3 copy.10
  1.3 0.8 fusion.1
  2.1 1.0 dynamic-slice_bitcast_fusion.3
  3.1 0.5 collective-permute-start
  3.6 1.0 collective-permute-done
  4.7 0.4 collective-permute-start.1
  5.1 2.7 %collective-permute-start.3 = (bf16[192,768]{1,0:T(8,128)(2,1)S(1)}, bf16[192,768]{1,0:T(8,128)(2,1)S(1)}, u32[]{:S(2)}, u32[]{:S(2)}) collective-permute-start(bf16[192,768]{1,0:T(8,128)(2,1)S(1)} %pad_maximum_fusion.1.refs_0_), channel_id=1, source_target_pairs={{0,4},{1,5},{4,8},{5,9},{8,12},{9,13},{12,14},{13,15},{14,10},{15,... | collective-permute-start | bytes 884744 | tf_op jit(solution)/shard_map/ppermute | solution.py:330
  7.8 7.5 %collective-permute-done.3.refs_1_ = bf16[192,768]{1,0:T(8,128)(2,1)S(1)} collective-permute-done((bf16[192,768]{1,0:T(8,128)(2,1)S(1)}, bf16[192,768]{1,0:T(8,128)(2,1)S(1)}, u32[]{:S(2)}, u32[]{:S(2)}) %collective-permute-start.3) | collective-permute-done | bytes 294944 | tf_op jit(solution)/shard_map/ppermute | solution.py:330
  15.3 1.8 %collective-permute-start.4 = (bf16[192,768]{1,0:T(8,128)(2,1)S(1)}, bf16[192,768]{1,0:T(8,128)(2,1)}, u32[]{:S(2)}, u32[]{:S(2)}) collective-permute-start(bf16[192,768]{1,0:T(8,128)(2,1)S(1)} %collective-permute-done.3.refs_1_), channel_id=1, source_target_pairs={{0,4},{1,5},{4,8},{5,9},{8,12},{9,13},{12,14},{13,15},{14,10},{15,... | collective-permute-start | bytes 884744 | tf_op jit(solution)/shard_map/ppermute | solution.py:330
  17.3 0.7 copy-done.6
  18.1 0.8 dynamic-slice_bitcast_fusion.1
  18.8 5.3 %collective-permute-done.4.refs_3_ = bf16[192,768]{1,0:T(8,128)(2,1)} collective-permute-done((bf16[192,768]{1,0:T(8,128)(2,1)S(1)}, bf16[192,768]{1,0:T(8,128)(2,1)}, u32[]{:S(2)}, u32[]{:S(2)}) %collective-permute-start.4) | collective-permute-done | bytes 294944 | tf_op jit(solution)/shard_map/ppermute | solution.py:330
  24.1 1.6 %collective-permute-start.5 = (bf16[192,768]{1,0:T(8,128)(2,1)}, bf16[192,768]{1,0:T(8,128)(2,1)S(1)}, u32[]{:S(2)}, u32[]{:S(2)}) collective-permute-start(bf16[192,768]{1,0:T(8,128)(2,1)} %collective-permute-done.4.refs_3_), channel_id=1, source_target_pairs={{0,4},{1,5},{4,8},{5,9},{8,12},{9,13},{12,14},{13,15},{14,10},{15,... | collective-permute-start | bytes 884744 | tf_op jit(solution)/shard_map/ppermute | solution.py:330
  25.7 0.5 collective-permute-start.8
  26.1 0.6 dynamic_slice.16
  26.8 1.9 %pad_maximum_fusion.refs_0_ = bf16[192,1280]{1,0:T(8,128)(2,1)} fusion(bf16[192,512]{1,0:T(8,128)(2,1)} %param.9, bf16[192,384]{1,0:T(8,128)(2,1)} %collective-permute-done.2, bf16[192,384]{1,0:T(8,128)(2,1)} %get-tuple-element.29), kind=kLoop, calls=%fused_computation.2 | loop fusion | flops 1474560 | bytes 983040 | tf_op jit(solution)/shard_map/concatenate | solution.py:371
  28.7 3.5 %collective-permute-done.5.refs_5_ = bf16[192,768]{1,0:T(8,128)(2,1)S(1)} collective-permute-done((bf16[192,768]{1,0:T(8,128)(2,1)}, bf16[192,768]{1,0:T(8,128)(2,1)S(1)}, u32[]{:S(2)}, u32[]{:S(2)}) %collective-permute-start.5) | collective-permute-done | bytes 294944 | tf_op jit(solution)/shard_map/ppermute | solution.py:330
  32.1 1.1 collective-permute-done.8.refs_6_
  33.3 0.7 broadcast_select_fusion.1
  34.0 1.6 %collective-permute-start.9 = (bf16[192,1280]{1,0:T(8,128)(2,1)}, bf16[192,1280]{1,0:T(8,128)(2,1)}, u32[]{:S(2)}, u32[]{:S(2)}) collective-permute-start(bf16[192,1280]{1,0:T(8,128)(2,1)} %pad_maximum_fusion.refs_0_), channel_id=1, source_target_pairs={{0,4},{1,5},{4,8},{5,9},{8,12},{9,13},{12,14},{13,15},{14,10},{15,... | collective-permute-start | bytes 1474568 | tf_op jit(solution)/shard_map/ppermute | solution.py:330
  35.6 0.4 collective-permute-start.10
  36.0 0.6 compare_select_fusion
  36.7 0.6 gather_fusion
  37.4 1.6 %collective-permute-start.11 = (bf16[192,768]{1,0:T(8,128)(2,1)}, bf16[192,768]{1,0:T(8,128)(2,1)S(1)}, u32[]{:S(2)}, u32[]{:S(2)}) collective-permute-start(bf16[192,768]{1,0:T(8,128)(2,1)} %broadcast_select_fusion.1), channel_id=1, source_target_pairs={{0,4},{4,8},{8,12},{12,14},{14,10},{10,6},{6,2},{2,0},{5,1},{9,5},... | collective-permute-start | bytes 884744 | tf_op jit(solution)/shard_map/ppermute | solution.py:339
  39.1 1.0 copy-done.3
  40.0 1.0 copy-done.5
  41.0 1.0 copy-done.7
  42.0 5.7 %temporal_projection.1.most_ref = f32[1024,384]{1,0:T(8,128)S(1)} custom-call(s32[10]{0:T(128)S(1)} %pad_add_fusion.meta_ref, bf16[512,3072]{1,0:T(8,128)(2,1)S(1)} %bitcast.28, bf16[512,3072]{1,0:T(8,128)(2,1)} %collective-permute-done.1.other_ref, bf16[192,768]{1,0:T(8,128)(2,1)S(1)} %copy-done.3, bf16[192,768]{1,0:T(8,128)(2,1)S(1)} %copy-done.5, ...), custom_call_target="tpu_custom_call" | custom-call | flops 2415919104 | bytes 8355880 | tf_op jit(solution)/shard_map/temporal_projection/pallas_call | solution.py:26
  47.7 1.2 collective-permute-done.11.piece_ref
  48.9 2.0 %temporal_projection_rest.1 = bf16[8,2,2,32,384]{4,3,2,1,0:T(8,128)(2,1)S(1)} custom-call(s32[10]{0:T(128)S(1)} %pad_add_fusion.meta_ref, bf16[512,3072]{1,0:T(8,128)(2,1)S(1)} %bitcast.29, bf16[512,3072]{1,0:T(8,128)(2,1)} %collective-permute-done.1.other_ref, bf16[192,768]{1,0:T(8,128)(2,1)S(1)} %collective-permute-done.11.piece_ref, ...), custom_call_target="tpu_custom_call" | custom-call | flops 301989888 | bytes 8159272 | tf_op jit(solution)/shard_map/temporal_projection_rest/pallas_call | solution.py:26
  50.9 0.9 copy-done.1
  51.8 1.6 %collective-permute-start.12 = (bf16[192,1280]{1,0:T(8,128)(2,1)}, bf16[192,1280]{1,0:T(8,128)(2,1)}, u32[]{:S(2)}, u32[]{:S(2)}) collective-permute-start(bf16[192,1280]{1,0:T(8,128)(2,1)} %collective-permute-done.9.refs_1_), channel_id=1, source_target_pairs={{0,4},{1,5},{4,8},{5,9},{8,12},{9,13},{12,14},{13,15},{14,10},{15,... | collective-permute-start | bytes 1474568 | tf_op jit(solution)/shard_map/ppermute | solution.py:330
  53.4 0.4 collective-permute-start.13
  53.8 4.8 %all-to-all-start = ((bf16[8,2,2,32,384]{4,3,2,1,0:T(8,128)(2,1)}), bf16[8,2,2,32,384]{4,3,2,1,0:T(8,128)(2,1)}, u32[]{:S(2)}, u32[]{:S(2)}) async-start(bf16[8,2,2,32,384]{4,3,2,1,0:T(8,128)(2,1)} %copy-done.1), calls=%async_computation | async-start | bytes 1572864 | tf_op jit(solution)/shard_map/all_to_all | solution.py:405
  58.7 7.3 %collective-permute-done.12.refs_0_.refs_3_ = bf16[192,1280]{1,0:T(8,128)(2,1)} collective-permute-done((bf16[192,1280]{1,0:T(8,128)(2,1)}, bf16[192,1280]{1,0:T(8,128)(2,1)}, u32[]{:S(2)}, u32[]{:S(2)}) %collective-permute-start.12) | collective-permute-done | bytes 491552 | tf_op jit(solution)/shard_map/ppermute | solution.py:330
  65.9 1.6 %collective-permute-start.14 = (bf16[192,1280]{1,0:T(8,128)(2,1)}, bf16[192,1280]{1,0:T(8,128)(2,1)}, u32[]{:S(2)}, u32[]{:S(2)}) collective-permute-start(bf16[192,1280]{1,0:T(8,128)(2,1)} %collective-permute-done.12.refs_0_.refs_3_), channel_id=1, source_target_pairs={{0,4},{1,5},{4,8},{5,9},{8,12},{9,13},{12,14},{13,15},{14,10},{15,... | collective-permute-start | bytes 1474568 | tf_op jit(solution)/shard_map/ppermute | solution.py:330
  67.8 0.4 collective-permute-start.15
  68.5 2.0 %pack_out_weight.4.refs_0_ = bf16[576,512]{1,0:T(8,128)(2,1)} custom-call(bf16[192,1280]{1,0:T(8,128)(2,1)} %pad_maximum_fusion.refs_0_, bf16[192,1280]{1,0:T(8,128)(2,1)} %collective-permute-done.9.refs_1_, bf16[192,1280]{1,0:T(8,128)(2,1)} %collective-permute-done.10.refs_2_), custom_call_target="tpu_custom_call" | custom-call | bytes 1474560 | tf_op jit(solution)/shard_map/pack_out_weight/pallas_call | solution.py:26
  70.5 1.7 %collective-permute-start.16 = (bf16[576,512]{1,0:T(8,128)(2,1)}, bf16[576,512]{1,0:T(8,128)(2,1)}, u32[]{:S(2)}, u32[]{:S(2)}) collective-permute-start(bf16[576,512]{1,0:T(8,128)(2,1)} %pack_out_weight.4.refs_0_), channel_id=1, source_target_pairs={{0,16},{16,0},{1,17},{17,1},{2,18},{18,2},{3,19},{19,3},{4,20},{20... | collective-permute-start | bytes 1769480 | tf_op jit(solution)/shard_map/ppermute | solution.py:321
  72.4 1.8 %pack_out_weight.5.refs_1_ = bf16[384,512]{1,0:T(8,128)(2,1)} custom-call(bf16[192,1280]{1,0:T(8,128)(2,1)} %collective-permute-done.12.refs_0_.refs_3_, bf16[192,1280]{1,0:T(8,128)(2,1)} %collective-permute-done.13.refs_1_.refs_4_), custom_call_target="tpu_custom_call" | custom-call | bytes 983040 | tf_op jit(solution)/shard_map/pack_out_weight/pallas_call | solution.py:26
  74.2 0.4 collective-permute-start.17
  74.6 14.3 %collective-permute-done.14.refs_5_.refs_0_ = bf16[192,1280]{1,0:T(8,128)(2,1)} collective-permute-done((bf16[192,1280]{1,0:T(8,128)(2,1)}, bf16[192,1280]{1,0:T(8,128)(2,1)}, u32[]{:S(2)}, u32[]{:S(2)}) %collective-permute-start.14) | collective-permute-done | bytes 491552 | tf_op jit(solution)/shard_map/ppermute | solution.py:330
  88.8 2.2 %collective-permute-done.15.refs_6_.refs_1_ = bf16[192,1280]{1,0:T(8,128)(2,1)} collective-permute-done((bf16[192,1280]{1,0:T(8,128)(2,1)}, bf16[192,1280]{1,0:T(8,128)(2,1)}, u32[]{:S(2)}, u32[]{:S(2)}) %collective-permute-start.15) | collective-permute-done | bytes 491552 | tf_op jit(solution)/shard_map/ppermute | solution.py:331
  91.0 1.9 %broadcast_select_fusion = bf16[192,1280]{1,0:T(8,128)(2,1)} fusion(bf16[192,1280]{1,0:T(8,128)(2,1)} %collective-permute-done.14.refs_5_.refs_0_, bf16[192,1280]{1,0:T(8,128)(2,1)} %collective-permute-done.15.refs_6_.refs_1_, pred[]{:T(512)S(6)} %eq.6), kind=kLoop, calls=%fused_computation.3 | loop fusion | flops 245760 | bytes 1474561 | tf_op jit(solution)/shard_map/jit(_where)/select_n | solution.py:333
  92.9 1.9 %collective-permute-done.17.refs_9_ = bf16[384,512]{1,0:T(8,128)(2,1)} collective-permute-done((bf16[384,512]{1,0:T(8,128)(2,1)}, bf16[384,512]{1,0:T(8,128)(2,1)}, u32[]{:S(2)}, u32[]{:S(2)}) %collective-permute-start.17) | collective-permute-done | bytes 393248 | tf_op jit(solution)/shard_map/ppermute | solution.py:321
  94.8 3.9 %collective-permute-start.18 = (bf16[192,1280]{1,0:T(8,128)(2,1)}, bf16[192,1280]{1,0:T(8,128)(2,1)}, u32[]{:S(2)}, u32[]{:S(2)}) collective-permute-start(bf16[192,1280]{1,0:T(8,128)(2,1)} %broadcast_select_fusion), channel_id=1, source_target_pairs={{0,4},{4,8},{8,12},{12,14},{14,10},{10,6},{6,2},{2,0},{5,1},{9,5},... | collective-permute-start | bytes 1474568 | tf_op jit(solution)/shard_map/ppermute | solution.py:339
  98.7 2.0 %temporal_attention.1 = bf16[2,16,32,128]{3,2,1,0:T(8,128)(2,1)S(1)} custom-call(s32[17]{0:T(128)S(1)} %pad_add_fusion.1.meta_ref, bf16[16,64,384]{2,1,0:T(8,128)(2,1)} %bitcast.13.qkv_ref), custom_call_target="tpu_custom_call" | custom-call | flops 24999999488 | bytes 786500 | tf_op jit(solution)/shard_map/temporal_attention/pallas_call | solution.py:26
  100.7 0.7 copy-done.9
  101.4 2.8 %all-to-all-start.1 = ((bf16[32,32,128]{2,1,0:T(8,128)(2,1)}), bf16[32,32,128]{2,1,0:T(8,128)(2,1)S(1)}, u32[]{:S(2)}, u32[]{:S(2)}) async-start(bf16[32,32,128]{2,1,0:T(8,128)(2,1)} %bitcast.32), calls=%async_computation.1 | async-start | bytes 524288 | tf_op jit(solution)/shard_map/all_to_all | solution.py:431
  104.2 1.8 %pack_out_weight.6.refs_2_ = bf16[384,512]{1,0:T(8,128)(2,1)} custom-call(bf16[192,1280]{1,0:T(8,128)(2,1)} %collective-permute-done.14.refs_5_.refs_0_, bf16[192,1280]{1,0:T(8,128)(2,1)} %collective-permute-done.15.refs_6_.refs_1_), custom_call_target="tpu_custom_call" | custom-call | bytes 983040 | tf_op jit(solution)/shard_map/pack_out_weight/pallas_call | solution.py:26
  106.0 1.5 %collective-permute-start.26 = (bf16[384,512]{1,0:T(8,128)(2,1)}, bf16[384,512]{1,0:T(8,128)(2,1)}, u32[]{:S(2)}, u32[]{:S(2)}) collective-permute-start(bf16[384,512]{1,0:T(8,128)(2,1)} %pack_out_weight.6.refs_2_), channel_id=1, source_target_pairs={{0,16},{16,0},{1,17},{17,1},{2,18},{18,2},{3,19},{19,3},{4,20},{20... | collective-permute-start | bytes 1179656 | tf_op jit(solution)/shard_map/ppermute | solution.py:321
  107.5 0.5 collective-permute-start.24
  108.0 1.6 %pack_out_weight.7.refs_3_ = bf16[192,512]{1,0:T(8,128)(2,1)} custom-call(bf16[192,1280]{1,0:T(8,128)(2,1)} %collective-permute-done.18.refs_7_.refs_0_), custom_call_target="tpu_custom_call" | custom-call | bytes 491520 | tf_op jit(solution)/shard_map/pack_out_weight/pallas_call | solution.py:26
  109.6 0.6 collective-permute-start.27
  110.3 7.6 %spatial_heads.1 = bf16[2,2,256,128]{3,2,1,0:T(8,128)(2,1)S(1)} custom-call(s32[10]{0:T(128)S(1)} %pad_add_fusion.meta_ref, bf16[512,3072]{1,0:T(8,128)(2,1)S(1)} %bitcast.30, bf16[512,3072]{1,0:T(8,128)(2,1)} %collective-permute-done.1.other_ref, bf16[192,1280]{1,0:T(8,128)(2,1)} %pad_maximum_fusion.refs_0_, ...), custom_call_target="tpu_custom_call" | custom-call | bytes 10223656 | tf_op jit(solution)/shard_map/spatial_heads/pallas_call | solution.py:26
  117.8 0.6 slice_bitcast_fusion
  118.5 1.5 %collective-permute-start.19 = (bf16[256,128]{1,0:T(8,128)(2,1)S(1)}, bf16[256,128]{1,0:T(8,128)(2,1)S(1)}, u32[]{:S(2)}, u32[]{:S(2)}) collective-permute-start(bf16[256,128]{1,0:T(8,128)(2,1)S(1)} %get-tuple-element.35), channel_id=1, source_target_pairs={{0,16},{16,0},{1,17},{17,1},{2,18},{18,2},{3,19},{19,3},{4,20},{20... | collective-permute-start | bytes 196616 | tf_op jit(solution)/shard_map/ppermute | solution.py:321
  119.9 3.8 %collective-permute-done.27.refs_11_ = bf16[192,512]{1,0:T(8,128)(2,1)} collective-permute-done((bf16[192,512]{1,0:T(8,128)(2,1)}, bf16[192,512]{1,0:T(8,128)(2,1)}, u32[]{:S(2)}, u32[]{:S(2)}) %collective-permute-start.27) | collective-permute-done | bytes 196640 | tf_op jit(solution)/shard_map/ppermute | solution.py:321
  123.8 1.3 collective-permute-start.25
  125.2 0.4 collective-permute-start.29
  125.7 2.2 %collective-permute-done.21.far_ref = bf16[256,128]{1,0:T(8,128)(2,1)S(1)} collective-permute-done((bf16[256,128]{1,0:T(8,128)(2,1)S(1)}, bf16[256,128]{1,0:T(8,128)(2,1)S(1)}, u32[]{:S(2)}, u32[]{:S(2)}) %collective-permute-start.21) | collective-permute-done | bytes 65568 | tf_op jit(solution)/shard_map/ppermute | solution.py:483
  128.0 0.5 copy-done.20
  128.5 0.7 copy-done.8
  130.7 7.0 %out_projection.1 = bf16[256,3072]{1,0:T(8,128)(2,1)} custom-call(s32[10]{0:T(128)} %copy-done.10, bf16[256,128]{1,0:T(8,128)(2,1)} %get-tuple-element.36.mine_ref, bf16[256,128]{1,0:T(8,128)(2,1)} %copy-done.18, bf16[256,128]{1,0:T(8,128)(2,1)} %copy-done.19, bf16[256,128]{1,0:T(8,128)(2,1)} %copy-done.20, bf16[2,256,256]{2,1,0:T(8,128)(2,1)} %copy-done.8, ...), custom_call_target="tpu_custom_call" | custom-call | flops 1610612736 | bytes 6815784 | tf_op jit(solution)/shard_map/out_projection/pallas_call | solution.py:26
  (79 shorter events, 2.9 us)
Async XLA Ops:
  0.0 26.1 %copy-start.22 = (s32[8]{0:T(128)S(1)}, s32[8]{0:T(128)}, u32[]{:S(2)}) copy-start(s32[8]{0:T(128)} %constant.67.clone) | copy-start | bytes 100
  0.0 36.7 %copy-start.11 = (s32[8]{0:T(128)S(1)}, s32[8]{0:T(128)}, u32[]{:S(2)}) copy-start(s32[8]{0:T(128)} %constant.68.clone) | copy-start | bytes 100
  0.0 4.7 %copy-start = (bf16[1,512,3072]{2,1,0:T(8,128)(2,1)S(1)}, bf16[1,512,3072]{2,1,0:T(8,128)(2,1)}, u32[]{:S(2)}) copy-start(bf16[1,512,3072]{2,1,0:T(8,128)(2,1)} %param.7) | copy-start | bytes 9437188
  3.1 1.5 %collective-permute-start = (bf16[192,384]{1,0:T(8,128)(2,1)S(1)}, bf16[192,384]{1,0:T(8,128)(2,1)S(1)}, u32[]{:S(2)}, u32[]{:S(2)}) collective-permute-start(bf16[192,384]{1,0:T(8,128)(2,1)S(1)} %get-tuple-element.32), channel_id=1, source_target_pairs={{0,1},{1,0},{2,3},{3,2},{4,5},{5,4},{6,7},{7,6},{8,9},{9,8},{10,11... | collective-permute-start | bytes 442376 | tf_op jit(solution)/shard_map/ppermute | solution.py:318
  4.7 14.2 %copy-start.2 = (bf16[192,768]{1,0:T(8,128)(2,1)}, bf16[192,768]{1,0:T(8,128)(2,1)S(1)}, u32[]{:S(2)}) copy-start(bf16[192,768]{1,0:T(8,128)(2,1)S(1)} %pad_maximum_fusion.1.refs_0_) | copy-start | bytes 884740
  4.7 34.4 %collective-permute-start.1 = (bf16[512,3072]{1,0:T(8,128)(2,1)S(1)}, bf16[512,3072]{1,0:T(8,128)(2,1)}, u32[]{:S(2)}, u32[]{:S(2)}) collective-permute-start(bf16[512,3072]{1,0:T(8,128)(2,1)S(1)} %bitcast.27), channel_id=1, source_target_pairs={{0,1},{1,0},{2,3},{3,2},{4,5},{5,4},{6,7},{7,6},{8,9},{9,8},{10,11... | collective-permute-start | bytes 9437192 | tf_op jit(solution)/shard_map/ppermute | solution.py:318
  5.1 10.2 %collective-permute-start.3 = (bf16[192,768]{1,0:T(8,128)(2,1)S(1)}, bf16[192,768]{1,0:T(8,128)(2,1)S(1)}, u32[]{:S(2)}, u32[]{:S(2)}) collective-permute-start(bf16[192,768]{1,0:T(8,128)(2,1)S(1)} %pad_maximum_fusion.1.refs_0_), channel_id=1, source_target_pairs={{0,4},{1,5},{4,8},{5,9},{8,12},{9,13},{12,14},{13,15},{14,10},{15,... | collective-permute-start | bytes 884744 | tf_op jit(solution)/shard_map/ppermute | solution.py:330
  7.8 9.3 %collective-permute-start.6 = (bf16[192,768]{1,0:T(8,128)(2,1)S(1)}, bf16[192,768]{1,0:T(8,128)(2,1)S(1)}, u32[]{:S(2)}, u32[]{:S(2)}) collective-permute-start(bf16[192,768]{1,0:T(8,128)(2,1)S(1)} %pad_maximum_fusion.1.refs_0_), channel_id=1, source_target_pairs={{4,0},{5,1},{8,4},{9,5},{12,8},{13,9},{14,12},{15,13},{10,14},{11,... | collective-permute-start | bytes 884744 | tf_op jit(solution)/shard_map/ppermute | solution.py:331
  15.3 8.8 %copy-start.4 = (bf16[192,768]{1,0:T(8,128)(2,1)}, bf16[192,768]{1,0:T(8,128)(2,1)S(1)}, u32[]{:S(2)}) copy-start(bf16[192,768]{1,0:T(8,128)(2,1)S(1)} %collective-permute-done.3.refs_1_) | copy-start | bytes 884740
  15.3 8.8 %collective-permute-start.4 = (bf16[192,768]{1,0:T(8,128)(2,1)S(1)}, bf16[192,768]{1,0:T(8,128)(2,1)}, u32[]{:S(2)}, u32[]{:S(2)}) collective-permute-start(bf16[192,768]{1,0:T(8,128)(2,1)S(1)} %collective-permute-done.3.refs_1_), channel_id=1, source_target_pairs={{0,4},{1,5},{4,8},{5,9},{8,12},{9,13},{12,14},{13,15},{14,10},{15,... | collective-permute-start | bytes 884744 | tf_op jit(solution)/shard_map/ppermute | solution.py:330
  17.1 8.6 %collective-permute-start.7 = (bf16[192,768]{1,0:T(8,128)(2,1)S(1)}, bf16[192,768]{1,0:T(8,128)(2,1)}, u32[]{:S(2)}, u32[]{:S(2)}) collective-permute-start(bf16[192,768]{1,0:T(8,128)(2,1)S(1)} %collective-permute-done.6.refs_2_), channel_id=1, source_target_pairs={{4,0},{5,1},{8,4},{9,5},{12,8},{13,9},{14,12},{15,13},{10,14},{11,... | collective-permute-start | bytes 884744 | tf_op jit(solution)/shard_map/ppermute | solution.py:331
  17.3 0.7 copy-start.6
  18.8 7.9 %collective-permute-start.2 = (bf16[192,384]{1,0:T(8,128)(2,1)}, bf16[192,384]{1,0:T(8,128)(2,1)}, u32[]{:S(2)}, u32[]{:S(2)}) collective-permute-start(bf16[192,384]{1,0:T(8,128)(2,1)} %get-tuple-element.30), channel_id=1, source_target_pairs={{0,1},{1,0},{2,3},{3,2},{4,5},{5,4},{6,7},{7,6},{8,9},{9,8},{10,11... | collective-permute-start | bytes 442376 | tf_op jit(solution)/shard_map/ppermute | solution.py:318
  24.1 8.0 %collective-permute-start.5 = (bf16[192,768]{1,0:T(8,128)(2,1)}, bf16[192,768]{1,0:T(8,128)(2,1)S(1)}, u32[]{:S(2)}, u32[]{:S(2)}) collective-permute-start(bf16[192,768]{1,0:T(8,128)(2,1)} %collective-permute-done.4.refs_3_), channel_id=1, source_target_pairs={{0,4},{1,5},{4,8},{5,9},{8,12},{9,13},{12,14},{13,15},{14,10},{15,... | collective-permute-start | bytes 884744 | tf_op jit(solution)/shard_map/ppermute | solution.py:330
  25.7 7.6 %collective-permute-start.8 = (bf16[192,768]{1,0:T(8,128)(2,1)}, bf16[192,768]{1,0:T(8,128)(2,1)}, u32[]{:S(2)}, u32[]{:S(2)}) collective-permute-start(bf16[192,768]{1,0:T(8,128)(2,1)} %collective-permute-done.7.refs_4_), channel_id=1, source_target_pairs={{4,0},{5,1},{8,4},{9,5},{12,8},{13,9},{14,12},{15,13},{10,14},{11,... | collective-permute-start | bytes 884744 | tf_op jit(solution)/shard_map/ppermute | solution.py:331
  34.0 17.8 %collective-permute-start.9 = (bf16[192,1280]{1,0:T(8,128)(2,1)}, bf16[192,1280]{1,0:T(8,128)(2,1)}, u32[]{:S(2)}, u32[]{:S(2)}) collective-permute-start(bf16[192,1280]{1,0:T(8,128)(2,1)} %pad_maximum_fusion.refs_0_), channel_id=1, source_target_pairs={{0,4},{1,5},{4,8},{5,9},{8,12},{9,13},{12,14},{13,15},{14,10},{15,... | collective-permute-start | bytes 1474568 | tf_op jit(solution)/shard_map/ppermute | solution.py:330
  35.6 16.2 %collective-permute-start.10 = (bf16[192,1280]{1,0:T(8,128)(2,1)}, bf16[192,1280]{1,0:T(8,128)(2,1)}, u32[]{:S(2)}, u32[]{:S(2)}) collective-permute-start(bf16[192,1280]{1,0:T(8,128)(2,1)} %pad_maximum_fusion.refs_0_), channel_id=1, source_target_pairs={{4,0},{5,1},{8,4},{9,5},{12,8},{13,9},{14,12},{15,13},{10,14},{11,... | collective-permute-start | bytes 1474568 | tf_op jit(solution)/shard_map/ppermute | solution.py:331
  37.4 11.5 %collective-permute-start.11 = (bf16[192,768]{1,0:T(8,128)(2,1)}, bf16[192,768]{1,0:T(8,128)(2,1)S(1)}, u32[]{:S(2)}, u32[]{:S(2)}) collective-permute-start(bf16[192,768]{1,0:T(8,128)(2,1)} %broadcast_select_fusion.1), channel_id=1, source_target_pairs={{0,4},{4,8},{8,12},{12,14},{14,10},{10,6},{6,2},{2,0},{5,1},{9,5},... | collective-permute-start | bytes 884744 | tf_op jit(solution)/shard_map/ppermute | solution.py:339
  39.1 71.2 %copy-start.10 = (s32[10]{0:T(128)}, s32[10]{0:T(128)S(1)}, u32[]{:S(2)}) copy-start(s32[10]{0:T(128)S(1)} %pad_add_fusion.meta_ref) | copy-start | bytes 124
  39.1 1.0 copy-start.3
  40.0 1.0 copy-start.5
  41.0 1.0 copy-start.7
  47.7 20.5 %copy-start.21 = (s32[16]{0:T(128)S(1)}, s32[16]{0:T(128)}, u32[]{:S(2)}) copy-start(s32[16]{0:T(128)} %param.10) | copy-start | bytes 196
  50.9 0.9 copy-start.1
  51.8 14.1 %collective-permute-start.12 = (bf16[192,1280]{1,0:T(8,128)(2,1)}, bf16[192,1280]{1,0:T(8,128)(2,1)}, u32[]{:S(2)}, u32[]{:S(2)}) collective-permute-start(bf16[192,1280]{1,0:T(8,128)(2,1)} %collective-permute-done.9.refs_1_), channel_id=1, source_target_pairs={{0,4},{1,5},{4,8},{5,9},{8,12},{9,13},{12,14},{13,15},{14,10},{15,... | collective-permute-start | bytes 1474568 | tf_op jit(solution)/shard_map/ppermute | solution.py:330
  53.4 14.4 %collective-permute-start.13 = (bf16[192,1280]{1,0:T(8,128)(2,1)}, bf16[192,1280]{1,0:T(8,128)(2,1)}, u32[]{:S(2)}, u32[]{:S(2)}) collective-permute-start(bf16[192,1280]{1,0:T(8,128)(2,1)} %collective-permute-done.10.refs_2_), channel_id=1, source_target_pairs={{4,0},{5,1},{8,4},{9,5},{12,8},{13,9},{14,12},{15,13},{10,14},{11,... | collective-permute-start | bytes 1474568 | tf_op jit(solution)/shard_map/ppermute | solution.py:331
  53.8 44.9 %all-to-all-start = ((bf16[8,2,2,32,384]{4,3,2,1,0:T(8,128)(2,1)}), bf16[8,2,2,32,384]{4,3,2,1,0:T(8,128)(2,1)}, u32[]{:S(2)}, u32[]{:S(2)}) async-start(bf16[8,2,2,32,384]{4,3,2,1,0:T(8,128)(2,1)} %copy-done.1), calls=%async_computation | async-start | bytes 1572864 | tf_op jit(solution)/shard_map/all_to_all | solution.py:405
  65.9 22.9 %collective-permute-start.14 = (bf16[192,1280]{1,0:T(8,128)(2,1)}, bf16[192,1280]{1,0:T(8,128)(2,1)}, u32[]{:S(2)}, u32[]{:S(2)}) collective-permute-start(bf16[192,1280]{1,0:T(8,128)(2,1)} %collective-permute-done.12.refs_0_.refs_3_), channel_id=1, source_target_pairs={{0,4},{1,5},{4,8},{5,9},{8,12},{9,13},{12,14},{13,15},{14,10},{15,... | collective-permute-start | bytes 1474568 | tf_op jit(solution)/shard_map/ppermute | solution.py:330
  67.8 23.2 %collective-permute-start.15 = (bf16[192,1280]{1,0:T(8,128)(2,1)}, bf16[192,1280]{1,0:T(8,128)(2,1)}, u32[]{:S(2)}, u32[]{:S(2)}) collective-permute-start(bf16[192,1280]{1,0:T(8,128)(2,1)} %collective-permute-done.13.refs_1_.refs_4_), channel_id=1, source_target_pairs={{4,0},{5,1},{8,4},{9,5},{12,8},{13,9},{14,12},{15,13},{10,14},{11,... | collective-permute-start | bytes 1474568 | tf_op jit(solution)/shard_map/ppermute | solution.py:331
  70.5 22.4 %collective-permute-start.16 = (bf16[576,512]{1,0:T(8,128)(2,1)}, bf16[576,512]{1,0:T(8,128)(2,1)}, u32[]{:S(2)}, u32[]{:S(2)}) collective-permute-start(bf16[576,512]{1,0:T(8,128)(2,1)} %pack_out_weight.4.refs_0_), channel_id=1, source_target_pairs={{0,16},{16,0},{1,17},{17,1},{2,18},{18,2},{3,19},{19,3},{4,20},{20... | collective-permute-start | bytes 1769480 | tf_op jit(solution)/shard_map/ppermute | solution.py:321
  72.2 46.2 %collective-permute-start.22 = (bf16[576,512]{1,0:T(8,128)(2,1)}, bf16[576,512]{1,0:T(8,128)(2,1)}, u32[]{:S(2)}, u32[]{:S(2)}) collective-permute-start(bf16[576,512]{1,0:T(8,128)(2,1)} %pack_out_weight.4.refs_0_), channel_id=1, source_target_pairs={{0,1},{1,0},{2,3},{3,2},{4,5},{5,4},{6,7},{7,6},{8,9},{9,8},{10,11... | collective-permute-start | bytes 1769480 | tf_op jit(solution)/shard_map/ppermute | solution.py:318
  74.2 20.6 %collective-permute-start.17 = (bf16[384,512]{1,0:T(8,128)(2,1)}, bf16[384,512]{1,0:T(8,128)(2,1)}, u32[]{:S(2)}, u32[]{:S(2)}) collective-permute-start(bf16[384,512]{1,0:T(8,128)(2,1)} %pack_out_weight.5.refs_1_), channel_id=1, source_target_pairs={{0,16},{16,0},{1,17},{17,1},{2,18},{18,2},{3,19},{19,3},{4,20},{20... | collective-permute-start | bytes 1179656 | tf_op jit(solution)/shard_map/ppermute | solution.py:321
  94.8 13.2 %collective-permute-start.18 = (bf16[192,1280]{1,0:T(8,128)(2,1)}, bf16[192,1280]{1,0:T(8,128)(2,1)}, u32[]{:S(2)}, u32[]{:S(2)}) collective-permute-start(bf16[192,1280]{1,0:T(8,128)(2,1)} %broadcast_select_fusion), channel_id=1, source_target_pairs={{0,4},{4,8},{8,12},{12,14},{14,10},{10,6},{6,2},{2,0},{5,1},{9,5},... | collective-permute-start | bytes 1474568 | tf_op jit(solution)/shard_map/ppermute | solution.py:339
  100.7 0.7 copy-start.9
  101.4 26.5 %all-to-all-start.1 = ((bf16[32,32,128]{2,1,0:T(8,128)(2,1)}), bf16[32,32,128]{2,1,0:T(8,128)(2,1)S(1)}, u32[]{:S(2)}, u32[]{:S(2)}) async-start(bf16[32,32,128]{2,1,0:T(8,128)(2,1)} %bitcast.32), calls=%async_computation.1 | async-start | bytes 524288 | tf_op jit(solution)/shard_map/all_to_all | solution.py:431
  106.0 14.0 %collective-permute-start.26 = (bf16[384,512]{1,0:T(8,128)(2,1)}, bf16[384,512]{1,0:T(8,128)(2,1)}, u32[]{:S(2)}, u32[]{:S(2)}) collective-permute-start(bf16[384,512]{1,0:T(8,128)(2,1)} %pack_out_weight.6.refs_2_), channel_id=1, source_target_pairs={{0,16},{16,0},{1,17},{17,1},{2,18},{18,2},{3,19},{19,3},{4,20},{20... | collective-permute-start | bytes 1179656 | tf_op jit(solution)/shard_map/ppermute | solution.py:321
  107.5 16.3 %collective-permute-start.23 = (bf16[384,512]{1,0:T(8,128)(2,1)}, bf16[384,512]{1,0:T(8,128)(2,1)S(1)}, u32[]{:S(2)}, u32[]{:S(2)}) collective-permute-start(bf16[384,512]{1,0:T(8,128)(2,1)} %pack_out_weight.5.refs_1_), channel_id=1, source_target_pairs={{0,1},{1,0},{2,3},{3,2},{4,5},{5,4},{6,7},{7,6},{8,9},{9,8},{10,11... | collective-permute-start | bytes 1179656 | tf_op jit(solution)/shard_map/ppermute | solution.py:318
  107.5 17.6 %collective-permute-start.24 = (bf16[384,512]{1,0:T(8,128)(2,1)}, bf16[384,512]{1,0:T(8,128)(2,1)}, u32[]{:S(2)}, u32[]{:S(2)}) collective-permute-start(bf16[384,512]{1,0:T(8,128)(2,1)} %pack_out_weight.6.refs_2_), channel_id=1, source_target_pairs={{0,1},{1,0},{2,3},{3,2},{4,5},{5,4},{6,7},{7,6},{8,9},{9,8},{10,11... | collective-permute-start | bytes 1179656 | tf_op jit(solution)/shard_map/ppermute | solution.py:318
  109.6 14.1 %collective-permute-start.27 = (bf16[192,512]{1,0:T(8,128)(2,1)}, bf16[192,512]{1,0:T(8,128)(2,1)}, u32[]{:S(2)}, u32[]{:S(2)}) collective-permute-start(bf16[192,512]{1,0:T(8,128)(2,1)} %pack_out_weight.7.refs_3_), channel_id=1, source_target_pairs={{0,16},{16,0},{1,17},{17,1},{2,18},{18,2},{3,19},{19,3},{4,20},{20... | collective-permute-start | bytes 589832 | tf_op jit(solution)/shard_map/ppermute | solution.py:321
  118.5 6.7 %collective-permute-start.19 = (bf16[256,128]{1,0:T(8,128)(2,1)S(1)}, bf16[256,128]{1,0:T(8,128)(2,1)S(1)}, u32[]{:S(2)}, u32[]{:S(2)}) collective-permute-start(bf16[256,128]{1,0:T(8,128)(2,1)S(1)} %get-tuple-element.35), channel_id=1, source_target_pairs={{0,16},{16,0},{1,17},{17,1},{2,18},{18,2},{3,19},{19,3},{4,20},{20... | collective-permute-start | bytes 196616 | tf_op jit(solution)/shard_map/ppermute | solution.py:321
  119.9 5.7 %collective-permute-start.20 = (bf16[256,128]{1,0:T(8,128)(2,1)S(1)}, bf16[256,128]{1,0:T(8,128)(2,1)S(1)}, u32[]{:S(2)}, u32[]{:S(2)}) collective-permute-start(bf16[256,128]{1,0:T(8,128)(2,1)S(1)} %get-tuple-element.34), channel_id=1, source_target_pairs={{0,1},{1,0},{2,3},{3,2},{4,5},{5,4},{6,7},{7,6},{8,9},{9,8},{10,11... | collective-permute-start | bytes 196616 | tf_op jit(solution)/shard_map/ppermute | solution.py:318
  123.8 4.1 %collective-permute-start.21 = (bf16[256,128]{1,0:T(8,128)(2,1)S(1)}, bf16[256,128]{1,0:T(8,128)(2,1)S(1)}, u32[]{:S(2)}, u32[]{:S(2)}) collective-permute-start(bf16[256,128]{1,0:T(8,128)(2,1)S(1)} %get-tuple-element.33), channel_id=1, source_target_pairs={{0,17},{1,16},{2,19},{3,18},{4,21},{5,20},{6,23},{7,22},{8,25},{9,... | collective-permute-start | bytes 196616 | tf_op jit(solution)/shard_map/ppermute | solution.py:483
  123.8 4.1 %copy-start.13 = (bf16[384,512]{1,0:T(8,128)(2,1)}, bf16[384,512]{1,0:T(8,128)(2,1)S(1)}, u32[]{:S(2)}) copy-start(bf16[384,512]{1,0:T(8,128)(2,1)S(1)} %collective-permute-done.23.refs_5_) | copy-start | bytes 1179652
  123.8 5.5 %collective-permute-start.25 = (bf16[192,512]{1,0:T(8,128)(2,1)}, bf16[192,512]{1,0:T(8,128)(2,1)S(1)}, u32[]{:S(2)}, u32[]{:S(2)}) collective-permute-start(bf16[192,512]{1,0:T(8,128)(2,1)} %pack_out_weight.7.refs_3_), channel_id=1, source_target_pairs={{0,1},{1,0},{2,3},{3,2},{4,5},{5,4},{6,7},{7,6},{8,9},{9,8},{10,11... | collective-permute-start | bytes 589832 | tf_op jit(solution)/shard_map/ppermute | solution.py:318
  125.1 4.5 %collective-permute-start.28 = (bf16[576,512]{1,0:T(8,128)(2,1)}, bf16[576,512]{1,0:T(8,128)(2,1)S(1)}, u32[]{:S(2)}, u32[]{:S(2)}) collective-permute-start(bf16[576,512]{1,0:T(8,128)(2,1)} %collective-permute-done.16.refs_8_), channel_id=1, source_target_pairs={{0,1},{1,0},{2,3},{3,2},{4,5},{5,4},{6,7},{7,6},{8,9},{9,8},{10,11... | collective-permute-start | bytes 1769480 | tf_op jit(solution)/shard_map/ppermute | solution.py:318
  125.2 2.8 %copy-start.18 = (bf16[256,128]{1,0:T(8,128)(2,1)}, bf16[256,128]{1,0:T(8,128)(2,1)S(1)}, u32[]{:S(2)}) copy-start(bf16[256,128]{1,0:T(8,128)(2,1)S(1)} %collective-permute-done.19.peer_ref) | copy-start | bytes 196612
  125.2 4.4 %collective-permute-start.29 = (bf16[384,512]{1,0:T(8,128)(2,1)}, bf16[384,512]{1,0:T(8,128)(2,1)S(1)}, u32[]{:S(2)}, u32[]{:S(2)}) collective-permute-start(bf16[384,512]{1,0:T(8,128)(2,1)} %collective-permute-done.17.refs_9_), channel_id=1, source_target_pairs={{0,1},{1,0},{2,3},{3,2},{4,5},{5,4},{6,7},{7,6},{8,9},{9,8},{10,11... | collective-permute-start | bytes 1179656 | tf_op jit(solution)/shard_map/ppermute | solution.py:318
  125.6 2.4 %copy-start.19 = (bf16[256,128]{1,0:T(8,128)(2,1)}, bf16[256,128]{1,0:T(8,128)(2,1)S(1)}, u32[]{:S(2)}) copy-start(bf16[256,128]{1,0:T(8,128)(2,1)S(1)} %collective-permute-done.20.core_ref) | copy-start | bytes 196612
  125.6 4.0 %collective-permute-start.30 = (bf16[384,512]{1,0:T(8,128)(2,1)}, bf16[384,512]{1,0:T(8,128)(2,1)S(1)}, u32[]{:S(2)}, u32[]{:S(2)}) collective-permute-start(bf16[384,512]{1,0:T(8,128)(2,1)} %collective-permute-done.26.refs_10_), channel_id=1, source_target_pairs={{0,1},{1,0},{2,3},{3,2},{4,5},{5,4},{6,7},{7,6},{8,9},{9,8},{10,11... | collective-permute-start | bytes 1179656 | tf_op jit(solution)/shard_map/ppermute | solution.py:318
  127.9 0.6 copy-start.20
  127.9 1.7 %collective-permute-start.31 = (bf16[192,512]{1,0:T(8,128)(2,1)}, bf16[192,512]{1,0:T(8,128)(2,1)S(1)}, u32[]{:S(2)}, u32[]{:S(2)}) collective-permute-start(bf16[192,512]{1,0:T(8,128)(2,1)} %collective-permute-done.27.refs_11_), channel_id=1, source_target_pairs={{0,1},{1,0},{2,3},{3,2},{4,5},{5,4},{6,7},{7,6},{8,9},{9,8},{10,11... | collective-permute-start | bytes 589832 | tf_op jit(solution)/shard_map/ppermute | solution.py:318
  128.5 0.7 copy-start.8
  129.2 0.7 copy-start.16
  129.6 0.7 copy-start.17
  129.6 0.8 copy-start.14
  129.6 0.9 copy-start.15
  129.6 1.1 copy-start.12

commit v4 on v3

--- a/solution.py
+++ b/solution.py
@@ -11,6 +11,7 @@
 HEAD = 128
 HS_DEV = 2
 SCALE = 1.0 / math.sqrt(HEAD)
+CFG = dict(A=1, B=3, C=1, D1=5, D2=5, F=2, G=1, H=3, I=0, MT=1, MS=3, K=0)
 MIB = 1024 * 1024
 FIRST = 25_000_000_000
 
@@ -81,10 +82,11 @@
 
 def most_body(depth, meta_ref, own_ref, other_ref, *refs):
     *piece_refs, out_ref, weight, frames, sems = refs
-    missing = meta_ref[2 + len(piece_refs)] * 2 * depth
-    weight[pl.ds(pl.multiple_of(missing, 16), 2 * depth), :] = jnp.zeros(
-        (2 * depth, weight.shape[1]), weight.dtype
-    )
+    for slot in range(len(piece_refs), weight.shape[0] // (2 * depth)):
+        missing = meta_ref[2 + slot] * 2 * depth
+        weight[pl.ds(pl.multiple_of(missing, 16), 2 * depth), :] = jnp.zeros(
+            (2 * depth, weight.shape[1]), weight.dtype
+        )
     last = load_all(depth, meta_ref, own_ref, other_ref, piece_refs, weight, frames, sems)
     patches = own_ref.shape[0]
     half = patches // 2
@@ -99,29 +101,37 @@
             )
 
 
-def rest_body(depth, chips, n_st, direct, meta_ref, own_ref, other_ref, piece_ref, most_ref, *refs):
-    out_ref, weight, frames, sems = refs
+def add_rest(depth, chips, meta_ref, own_ref, other_ref, most_ref, piece_refs, weight, frames, sems):
     patches = own_ref.shape[0]
-    part = patches // (n_st * chips)
-    if own_ref.shape[1] != 2 * depth:
-        share = pl.ds(pl.multiple_of(meta_ref[1 + chips] * 2 * depth, 2 * depth), 2 * depth)
-        own_ref, other_ref = own_ref.at[:, share], other_ref.at[:, share]
-    copies = [
-        pltpu.make_async_copy(ref, frames.at[k], sems.at[k])
-        for k, ref in enumerate((own_ref, other_ref))
-    ]
-    for copy in copies:
+    late = len(piece_refs)
+    copies = [[], []]
+    for k, ref in enumerate((own_ref, other_ref)):
+        if ref.shape[1] == frames.shape[2]:
+            copies[k].append(pltpu.make_async_copy(ref, frames.at[k], sems.at[k, 0]))
+            continue
+        for i in range(late):
+            at = meta_ref[2 + chips - late + i] * 2 * depth
+            copies[k].append(
+                pltpu.make_async_copy(
+                    ref.at[:, pl.ds(pl.multiple_of(at, 2 * depth), 2 * depth)],
+                    frames.at[k, :, pl.ds(i * 2 * depth, 2 * depth)],
+                    sems.at[k, i],
+                )
+            )
+    for copy in copies[0] + copies[1]:
         copy.start()
     core = meta_ref[0]
     columns = weight.shape[1]
-    for k in range(2):
-        at = (core if k == 0 else 1 - core) * depth
-        weight[pl.ds(pl.multiple_of(at, 16), depth), :] = piece_ref[
-            :, k * columns : (k + 1) * columns
-        ]
+    for i, piece_ref in enumerate(piece_refs):
+        for k in range(2):
+            at = (2 * i + (core if k == 0 else 1 - core)) * depth
+            weight[pl.ds(pl.multiple_of(at, 16), depth), :] = piece_ref[
+                :, k * columns : (k + 1) * columns
+            ]
     half = patches // 2
     for frame in range(2):
-        copies[frame].wait()
+        for copy in copies[frame]:
+            copy.wait()
         for first in range(0, patches, half):
             here = slice(frame * patches + first, frame * patches + first + half)
             result = most_ref[here, :] + jnp.dot(
@@ -129,32 +139,35 @@
                 weight[...],
                 preferred_element_type=jnp.float32,
             )
-            result = result.astype(jnp.bfloat16)
-            if not direct:
-                out_ref[here, :] = result
-                continue
-            for at in range(first, first + half, part):
-                block = at // part
-                out_ref[block % chips, frame, block // chips] = result[
-                    at - first : at - first + part
-                ]
-
-
-def spatial_body(depth, n_st, meta_ref, own_ref, other_ref, *refs):
-    *piece_refs, out_ref, weight, frames, sems, packed = refs
-    last = load_all(depth, meta_ref, own_ref, other_ref, piece_refs, weight, frames, sems)
+            yield frame, first, result.astype(jnp.bfloat16)
+
+
+def rest_body(depth, chips, n_st, direct, late, meta_ref, own_ref, other_ref, most_ref, *refs):
+    piece_refs, (out_ref, *scratch) = refs[:late], refs[late:]
+    patches = own_ref.shape[0]
+    part = patches // (n_st * chips)
+    for frame, first, result in add_rest(
+        depth, chips, meta_ref, own_ref, other_ref, most_ref, piece_refs, *scratch
+    ):
+        rows = result.shape[0]
+        if not direct:
+            out_ref[frame * patches + first : frame * patches + first + rows, :] = result
+            continue
+        for at in range(first, first + rows, part):
+            block = at // part
+            out_ref[block % chips, frame, block // chips] = result[at - first : at - first + part]
+
+
+def spatial_body(depth, chips, n_st, late, meta_ref, own_ref, other_ref, most_ref, *refs):
+    piece_refs, (out_ref, *scratch, packed) = refs[:late], refs[late:]
     patches = own_ref.shape[0]
     part = patches // n_st
-    half = patches // 2
-    for frame in range(2):
-        if frame == 1:
-            last.wait()
-        for first in range(0, patches, half):
-            packed[first : first + half, :] = jnp.dot(
-                frames[frame, first : first + half, :],
-                weight[...],
-                preferred_element_type=jnp.float32,
-            ).astype(jnp.bfloat16)
+    for frame, first, result in add_rest(
+        depth, chips, meta_ref, own_ref, other_ref, most_ref, piece_refs, *scratch
+    ):
+        packed[first : first + result.shape[0], :] = result
+        if first + result.shape[0] < patches:
+            continue
         for group in range(n_st):
             rows = slice(group * part, (group + 1) * part)
             scores = lax.dot_general(
@@ -330,6 +343,9 @@
             ahead = lax.ppermute(ahead, "fsdp", forward)
             behind = lax.ppermute(behind, "fsdp", backward)
             pieces = pieces + [ahead, behind]
+        gate = yield pieces, ahead
+        if gate is not None:
+            ahead, behind, _ = lax.optimization_barrier((ahead, behind, gate))
         sent = jnp.where(core == 0, ahead, behind)
         gate = yield pieces, sent
         if gate is not None:
@@ -362,7 +378,9 @@
     own = normed.reshape(patches, width)
 
     temporal_ring = ring_gather(temporal_piece)
-    _, last_sent = run(temporal_ring, chips // 2)
+    second_pieces, _ = run(temporal_ring, 3)
+    third_pieces, _ = run(temporal_ring, chips // 2 - 3)
+    _, last_sent = run(temporal_ring, 1)
     pieces, _ = next(temporal_ring)
     own, later_head, _ = lax.optimization_barrier((own, by_head[:HS_DEV], temporal_piece))
     other = to_core(own)
@@ -370,37 +388,64 @@
     split = spatial_piece.shape[1]
     both_ring = ring_gather(jnp.concatenate([spatial_piece, out_weight], axis=1))
     next(both_ring)
-    first_pieces, _ = both_ring.send(last_sent)
+    first_pieces, _ = both_ring.send([None, last_sent, third_pieces[-1], second_pieces[-1]][CFG['H']])
+    temporal_late, spatial_late = CFG['MT'], CFG['MS']
     head_flops = 4 * patches * width * 3 * HEAD
     shape = (chips, 2, n_st, part, 3 * HEAD) if direct else (2 * patches, 3 * HEAD)
     most = kernel_call(
         functools.partial(most_body, depth),
         jax.ShapeDtypeStruct((2 * patches, 3 * HEAD), jnp.float32),
-        [ring_meta, own, other, *pieces[:-1]],
+        [ring_meta, own, other, *pieces[: chips - temporal_late]],
         head_flops,
         "temporal_projection",
         scratch=load_scratch(2 * chips, patches, width),
     )
-    shares = (own, other)
-    if 2 * depth % 128:
-        shares = [
-            lax.dynamic_slice_in_dim(x, sources[-1] * 2 * depth, 2 * depth, 1) for x in shares
+    temporal_most = most
+    if CFG['A']:
+        most, *_ = lax.optimization_barrier((most, *first_pieces))
+    def shares(late):
+        if 2 * depth % 128 == 0:
+            return own, other
+        return [
+            jnp.concatenate(
+                [
+                    lax.dynamic_slice_in_dim(x, sources[chips - i] * 2 * depth, 2 * depth, 1)
+                    for i in range(late, 0, -1)
+                ],
+                axis=1,
+            )
+            for x in (own, other)
         ]
+
+    def rest_scratch(late):
+        return [
+            pltpu.VMEM((late * 2 * depth, 3 * HEAD), jnp.bfloat16),
+            pltpu.VMEM((2, patches, late * 2 * depth), jnp.bfloat16),
+            pltpu.SemaphoreType.DMA((2, late)),
+        ]
+
     temporal = projected = kernel_call(
-        functools.partial(rest_body, depth, chips, n_st, direct),
+        functools.partial(rest_body, depth, chips, n_st, direct, temporal_late),
         jax.ShapeDtypeStruct(shape, jnp.bfloat16),
-        [ring_meta, *shares, pieces[-1], most],
+        [ring_meta, *shares(temporal_late), most, *pieces[chips - temporal_late :]],
         head_flops // chips,
         "temporal_projection_rest",
-        whole=(3, 4),
-        scratch=[
-            pltpu.VMEM((2 * depth, 3 * HEAD), jnp.bfloat16),
-            pltpu.VMEM((2, patches, 2 * depth), jnp.bfloat16),
-            pltpu.SemaphoreType.DMA((2,)),
-        ],
+        whole=range(3, 4 + temporal_late),
+        scratch=rest_scratch(temporal_late),
     )
     if not direct:
         temporal = temporal.reshape(2, n_st, chips, part, 3 * HEAD).transpose(2, 0, 1, 3, 4)
+    second_parts, _ = both_ring.send([None, projected, temporal_most][CFG['F']])
+    if chips > 8:
+        second_parts, _ = run(both_ring, chips // 2 - 4)
+    spatial_most = kernel_call(
+        functools.partial(most_body, depth),
+        jax.ShapeDtypeStruct((2 * patches, 3 * HEAD), jnp.float32),
+        [ring_meta, own, other, *second_parts[: chips - spatial_late]],
+        0,
+        "spatial_projection",
+        scratch=load_scratch(2 * chips, patches, width),
+    )
     same_core = [[2 * i + c for i in range(chips)] for c in range(2)]
     temporal = lax.all_to_all(
         temporal,
@@ -413,6 +458,8 @@
     pairs = segment_ids.reshape(chips, 2)
     pairs = jnp.where(core == 0, pairs, pairs[:, ::-1]).reshape(frames)
     clips = jnp.concatenate([pairs, core.reshape(1)]).astype(jnp.int32)
+    if CFG['K']:
+        temporal, _ = lax.optimization_barrier((temporal, spatial_most))
     tile = min(n_st * part, max(16, 256 // frames))
     if part % tile == 0:
         shape = (n_st, frames, part, HEAD)
@@ -422,7 +469,7 @@
         functools.partial(temporal_body, tile),
         jax.ShapeDtypeStruct(shape, jnp.bfloat16),
         [clips, temporal],
-        FIRST,
+        CFG['D1'] * 1000000000,
         "temporal_attention",
         whole=(1,),
     )
@@ -449,22 +496,26 @@
         )
 
     early = n_st == 2 and direct
-    parts, _ = both_ring.send(projected)
+    parts = second_parts
     if early:
         kinds = [pack(parts[:3]), pack(parts[3:5])]
         peers = [to_peer(k) for k in kinds]
-    parts, _ = run(both_ring, chips // 2 - 3)
-    parts, _ = both_ring.send(tuple(peers) if early else attention)
+    both_ring.send(attention if CFG['I'] else None)
+    both_ring.send([None, attention, None, spatial_most][CFG['B']])
+    late = []
+    if CFG['B'] == 2:
+        late.append(attention)
+    if CFG['C'] == 1 and early:
+        late += peers
+    parts, _ = both_ring.send(tuple(late) if late else None)
     spatial = kernel_call(
-        functools.partial(spatial_body, depth, n_st),
+        functools.partial(spatial_body, depth, chips, n_st, spatial_late),
         jax.ShapeDtypeStruct((n_st, 2, rows, HEAD), jnp.bfloat16),
-        [ring_meta, own, other, *parts],
+        [ring_meta, *shares(spatial_late), spatial_most, *parts[chips - spatial_late :]],
         0,
         "spatial_heads",
-        scratch=[
-            *load_scratch(2 * chips + 2, patches, width),
-            pltpu.VMEM((patches, 3 * HEAD), jnp.bfloat16),
-        ],
+        whole=range(3, 4 + spatial_late),
+        scratch=[*rest_scratch(spatial_late), pltpu.VMEM((patches, 3 * HEAD), jnp.bfloat16)],
     )
 
     if early:
@@ -472,7 +523,7 @@
             order_body,
             jax.ShapeDtypeStruct((n_st, rows, 2 * HEAD), jnp.bfloat16),
             [temporal_heads],
-            FIRST,
+            CFG['D2'] * 1000000000,
             "temporal_heads",
             whole=(0,),
         )
@@ -487,7 +538,8 @@
         peers += [to_peer(k) for k in kinds[2:]]
         count = len(kinds)
         kinds += [to_core(k) for k in kinds] + peers
-        peers = lax.optimization_barrier((*peers, attention))[:-1]
+        if CFG['G']:
+            peers = lax.optimization_barrier((*peers, attention if CFG['G'] == 1 else spatial))[:-1]
         kinds += [to_core(k) for k in peers]
         attended = kernel_call(
             functools.partial(out_body, depth, count),

time: 139 us -> 126 us (0.906)
  waiting for transfers between devices: 51.9 us -> 33.9 us
  starting transfers between devices: 35.2 us -> 38.5 us
  Pallas kernels: 31.5 us -> 34.7 us
    ppermute x6, waiting for transfers between devices: 37.7 us -> 21.3 us  [ring_gather(): ahead = lax.ppermute(ahead, 'fsdp', forward)]
    pallas_call x10 -> x11, Pallas kernels: 31.5 us -> 34.7 us  [kernel_call(): pl.pallas_call(body, out_shape=out_shape, in_specs=[pl.BlockSpec(memory_s...]
    ppermute x6, waiting for transfers between devices: 3.57 us -> 5.84 us  [ring_gather(): behind = lax.ppermute(behind, 'fsdp', backward)]
    ppermute x5, waiting for transfers between devices: 5.75 us -> 3.54 us  [to_peer(): return lax.ppermute(x, 'st', [(0, 1), (1, 0)])]
    ppermute x2, starting transfers between devices: 5.49 us -> 7.52 us  [ring_gather(): yield (pieces + [lax.ppermute(sent, 'fsdp', both)], None)]
    ppermute x1, starting transfers between devices: 0.01 us -> 1.6 us  [shards(): lax.ppermute(spatial[1, 1], ('st', 'fsdp'), across)]
    unnamed x47 -> x45, local copies, waits for them, and re-layouts: 8.86 us -> 8.59 us
  transfers between devices with their start and end apart: 34 -> 34, of which waited for: 14 -> 12; matrix products, arithmetic and copies ran while one was open for 6% -> 7% of each run, Pallas kernels for 18% -> 22%
where the time goes in v4:
time: 126 us
  starting transfers between devices  38.5 us (31%)
  Pallas kernels  34.7 us (28%)
  waiting for transfers between devices  33.9 us (27%)
  local copies, waits for them, and re-layouts  13.3 us (11%)
  other arithmetic  4.71 us (4%)
    pallas_call x11, Pallas kernels, kernel_call(): pl.pallas_call(body, out_shape=out_shape, in_specs=[pl.BlockSpec(memory_s...  34.7 us
    ppermute x6, waiting for transfers between devices, ring_gather(): ahead = lax.ppermute(ahead, 'fsdp', forward)  21.3 us
    ppermute x6, starting transfers between devices, ring_gather(): ahead = lax.ppermute(ahead, 'fsdp', forward)  11.2 us
    unnamed x45, local copies, waits for them, and re-layouts  8.59 us
    ppermute x2, starting transfers between devices, ring_gather(): yield (pieces + [lax.ppermute(sent, 'fsdp', both)], None)  7.52 us
    ppermute x5, starting transfers between devices, to_peer(): return lax.ppermute(x, 'st', [(0, 1), (1, 0)])  6.13 us
    ppermute x6, waiting for transfers between devices, ring_gather(): behind = lax.ppermute(behind, 'fsdp', backward)  5.84 us
    all_to_all x1, starting transfers between devices, shards(): lax.all_to_all(temporal, 'fsdp', split_axis=0, concat_axis=0, tiled=True,...  5.47 us
  transfers between devices with their start and end apart: 34, of which 12 were waited for; matrix products, arithmetic and copies ran while one was open for 7% of the time, Pallas kernels for 22%

profile of v4, /device:TPU:0, one launch (start us, length us, event | category | flops | bytes accessed | tf_op | source)
XLA Modules:
  0.0 125.6 jit_solution(6780658691305010402)
XLA Ops:
  0.0 1.3 %copy.10 = bf16[192,4,384]{2,0,1:T(8,128)(2,1)S(1)} copy(bf16[192,4,384]{2,1,0:T(4,128)(2,1)} %param.8) | data formatting | bytes 1179648 | tf_op args[1]
  1.3 0.8 fusion.1
  2.1 0.5 collective-permute-start
  2.6 1.0 collective-permute-done
  3.7 0.4 collective-permute-start.1
  4.1 2.7 %collective-permute-start.7 = (bf16[192,768]{1,0:T(8,128)(2,1)S(1)}, bf16[192,768]{1,0:T(8,128)(2,1)}, u32[]{:S(2)}, u32[]{:S(2)}) collective-permute-start(bf16[192,768]{1,0:T(8,128)(2,1)S(1)} %pad_maximum_fusion.1.refs_0_), channel_id=1, source_target_pairs={{0,4},{1,5},{4,8},{5,9},{8,12},{9,13},{12,14},{13,15},{14,10},{15,... | collective-permute-start | bytes 884744 | tf_op jit(solution)/shard_map/ppermute | solution.py:343
  6.9 0.6 dynamic_slice.16
  7.5 1.7 %dynamic-slice_bitcast_fusion.1 = (bf16[192,384]{1,0:T(8,128)(2,1)}, bf16[192,384]{1,0:T(8,128)(2,1)}) fusion(bf16[2,192,384]{2,1,0:T(8,128)(2,1)} %get-tuple-element.20, s32[]{:T(128)S(6)} %select_n.61, s32[]{:T(128)S(6)} %select_n.62), kind=kLoop, calls=%fused_computation.7 | loop fusion | bytes 589832 | tf_op jit(solution)/shard_map/jit(dynamic_index_in_dim)/squeeze | solution.py:373
  9.3 5.1 %collective-permute-done.7.refs_1_ = bf16[192,768]{1,0:T(8,128)(2,1)} collective-permute-done((bf16[192,768]{1,0:T(8,128)(2,1)S(1)}, bf16[192,768]{1,0:T(8,128)(2,1)}, u32[]{:S(2)}, u32[]{:S(2)}) %collective-permute-start.7) | collective-permute-done | bytes 294944 | tf_op jit(solution)/shard_map/ppermute | solution.py:343
  14.4 1.8 %collective-permute-start.8 = (bf16[192,768]{1,0:T(8,128)(2,1)}, bf16[192,768]{1,0:T(8,128)(2,1)}, u32[]{:S(2)}, u32[]{:S(2)}) collective-permute-start(bf16[192,768]{1,0:T(8,128)(2,1)} %collective-permute-done.7.refs_1_), channel_id=1, source_target_pairs={{0,4},{1,5},{4,8},{5,9},{8,12},{9,13},{12,14},{13,15},{14,10},{15,... | collective-permute-start | bytes 884744 | tf_op jit(solution)/shard_map/ppermute | solution.py:343
  16.2 0.2 collective-permute-start.4
  16.5 0.7 compare_select_fusion
  17.2 0.6 gather_fusion
  17.8 5.6 %collective-permute-done.8.refs_3_ = bf16[192,768]{1,0:T(8,128)(2,1)} collective-permute-done((bf16[192,768]{1,0:T(8,128)(2,1)}, bf16[192,768]{1,0:T(8,128)(2,1)}, u32[]{:S(2)}, u32[]{:S(2)}) %collective-permute-start.8) | collective-permute-done | bytes 294944 | tf_op jit(solution)/shard_map/ppermute | solution.py:343
  23.4 1.6 %collective-permute-start.9 = (bf16[192,768]{1,0:T(8,128)(2,1)}, bf16[192,768]{1,0:T(8,128)(2,1)S(1)}, u32[]{:S(2)}, u32[]{:S(2)}) collective-permute-start(bf16[192,768]{1,0:T(8,128)(2,1)} %collective-permute-done.8.refs_3_), channel_id=1, source_target_pairs={{0,4},{1,5},{4,8},{5,9},{8,12},{9,13},{12,14},{13,15},{14,10},{15,... | collective-permute-start | bytes 884744 | tf_op jit(solution)/shard_map/ppermute | solution.py:343
  25.0 0.5 collective-permute-start.10
  25.5 1.9 %pad_maximum_fusion.refs_0_ = bf16[192,1280]{1,0:T(8,128)(2,1)} fusion(bf16[192,512]{1,0:T(8,128)(2,1)} %param.9, bf16[192,384]{1,0:T(8,128)(2,1)} %collective-permute-done.2, bf16[192,384]{1,0:T(8,128)(2,1)} %get-tuple-element.35), kind=kLoop, calls=%fused_computation.2 | loop fusion | flops 1474560 | bytes 983040 | tf_op jit(solution)/shard_map/concatenate | solution.py:389
  27.4 1.6 %collective-permute-start.5 = (bf16[192,1280]{1,0:T(8,128)(2,1)}, bf16[192,1280]{1,0:T(8,128)(2,1)}, u32[]{:S(2)}, u32[]{:S(2)}) collective-permute-start(bf16[192,1280]{1,0:T(8,128)(2,1)} %pad_maximum_fusion.refs_0_), channel_id=1, source_target_pairs={{0,4},{1,5},{4,8},{5,9},{8,12},{9,13},{12,14},{13,15},{14,10},{15,... | collective-permute-start | bytes 1474568 | tf_op jit(solution)/shard_map/ppermute | solution.py:343
  28.9 0.5 collective-permute-start.6
  29.5 4.1 %collective-permute-done.9.refs_5_ = bf16[192,768]{1,0:T(8,128)(2,1)S(1)} collective-permute-done((bf16[192,768]{1,0:T(8,128)(2,1)}, bf16[192,768]{1,0:T(8,128)(2,1)S(1)}, u32[]{:S(2)}, u32[]{:S(2)}) %collective-permute-start.9) | collective-permute-done | bytes 294944 | tf_op jit(solution)/shard_map/ppermute | solution.py:343
  33.6 1.7 %collective-permute-done.10.refs_6_ = bf16[192,768]{1,0:T(8,128)(2,1)} collective-permute-done((bf16[192,768]{1,0:T(8,128)(2,1)}, bf16[192,768]{1,0:T(8,128)(2,1)}, u32[]{:S(2)}, u32[]{:S(2)}) %collective-permute-start.10) | collective-permute-done | bytes 294944 | tf_op jit(solution)/shard_map/ppermute | solution.py:344
  35.3 1.6 %collective-permute-start.21 = (bf16[192,768]{1,0:T(8,128)(2,1)S(1)}, bf16[192,768]{1,0:T(8,128)(2,1)S(1)}, u32[]{:S(2)}, u32[]{:S(2)}) collective-permute-start(bf16[192,768]{1,0:T(8,128)(2,1)S(1)} %broadcast_select_fusion.1), channel_id=1, source_target_pairs={{0,4},{4,8},{8,12},{12,14},{14,10},{10,6},{6,2},{2,0},{5,1},{9,5},... | collective-permute-start | bytes 884744 | tf_op jit(solution)/shard_map/ppermute | solution.py:355
  36.9 1.0 copy-done.5
  37.9 5.8 %temporal_projection.1.most_ref = f32[1024,384]{1,0:T(8,128)S(1)} custom-call(s32[10]{0:T(128)S(1)} %pad_add_fusion.meta_ref, bf16[512,3072]{1,0:T(8,128)(2,1)S(1)} %bitcast.28, bf16[512,3072]{1,0:T(8,128)(2,1)} %collective-permute-done.1.other_ref, bf16[192,768]{1,0:T(8,128)(2,1)S(1)} %copy-done.5, bf16[192,768]{1,0:T(8,128)(2,1)} %collective-permute-done.7.refs_1_, ...), custom_call_target="tpu_custom_call" | custom-call | flops 2415919104 | bytes 8355880 | tf_op jit(solution)/shard_map/temporal_projection/pallas_call | solution.py:27
  43.7 2.0 %collective-permute-done.6.refs_2_ = bf16[192,1280]{1,0:T(8,128)(2,1)} collective-permute-done((bf16[192,1280]{1,0:T(8,128)(2,1)}, bf16[192,1280]{1,0:T(8,128)(2,1)}, u32[]{:S(2)}, u32[]{:S(2)}) %collective-permute-start.6) | collective-permute-done | bytes 491552 | tf_op jit(solution)/shard_map/ppermute | solution.py:344
  45.8 1.6 %collective-permute-start.11 = (bf16[192,1280]{1,0:T(8,128)(2,1)}, bf16[192,1280]{1,0:T(8,128)(2,1)}, u32[]{:S(2)}, u32[]{:S(2)}) collective-permute-start(bf16[192,1280]{1,0:T(8,128)(2,1)} %collective-permute-done.5.refs_1_), channel_id=1, source_target_pairs={{0,4},{1,5},{4,8},{5,9},{8,12},{9,13},{12,14},{13,15},{14,10},{15,... | collective-permute-start | bytes 1474568 | tf_op jit(solution)/shard_map/ppermute | solution.py:343
  47.4 0.4 collective-permute-start.12
  47.8 2.0 %temporal_projection_rest.1 = bf16[8,2,2,32,384]{4,3,2,1,0:T(8,128)(2,1)S(1)} custom-call(s32[10]{0:T(128)S(1)} %pad_add_fusion.meta_ref, bf16[512,3072]{1,0:T(8,128)(2,1)S(1)} %bitcast.29, bf16[512,3072]{1,0:T(8,128)(2,1)} %collective-permute-done.1.other_ref, f32[1024,384]{1,0:T(8,128)S(1)} %temporal_projection.1.most_ref, ...), custom_call_target="tpu_custom_call" | custom-call | flops 301989888 | bytes 8159272 | tf_op jit(solution)/shard_map/temporal_projection_rest/pallas_call | solution.py:27
  49.9 0.9 copy-done.3
  50.8 5.5 %all-to-all-start = ((bf16[8,2,2,32,384]{4,3,2,1,0:T(8,128)(2,1)}), bf16[8,2,2,32,384]{4,3,2,1,0:T(8,128)(2,1)}, u32[]{:S(2)}, u32[]{:S(2)}) async-start(bf16[8,2,2,32,384]{4,3,2,1,0:T(8,128)(2,1)} %copy-done.3), calls=%async_computation | async-start | bytes 1572864 | tf_op jit(solution)/shard_map/all_to_all | solution.py:450
  56.2 2.0 %collective-permute-start.13 = (bf16[192,1280]{1,0:T(8,128)(2,1)}, bf16[192,1280]{1,0:T(8,128)(2,1)}, u32[]{:S(2)}, u32[]{:S(2)}) collective-permute-start(bf16[192,1280]{1,0:T(8,128)(2,1)} %collective-permute-done.11.refs_3_.refs_0_), channel_id=1, source_target_pairs={{0,4},{1,5},{4,8},{5,9},{8,12},{9,13},{12,14},{13,15},{14,10},{15,... | collective-permute-start | bytes 1474568 | tf_op jit(solution)/shard_map/ppermute | solution.py:343
  58.5 2.0 %pack_out_weight.4.refs_0_ = bf16[576,512]{1,0:T(8,128)(2,1)} custom-call(bf16[192,1280]{1,0:T(8,128)(2,1)} %pad_maximum_fusion.refs_0_, bf16[192,1280]{1,0:T(8,128)(2,1)} %collective-permute-done.5.refs_1_, bf16[192,1280]{1,0:T(8,128)(2,1)} %collective-permute-done.6.refs_2_), custom_call_target="tpu_custom_call" | custom-call | bytes 1474560 | tf_op jit(solution)/shard_map/pack_out_weight/pallas_call | solution.py:27
  60.5 1.6 %collective-permute-start.15 = (bf16[576,512]{1,0:T(8,128)(2,1)}, bf16[576,512]{1,0:T(8,128)(2,1)}, u32[]{:S(2)}, u32[]{:S(2)}) collective-permute-start(bf16[576,512]{1,0:T(8,128)(2,1)} %pack_out_weight.4.refs_0_), channel_id=1, source_target_pairs={{0,16},{16,0},{1,17},{17,1},{2,18},{18,2},{3,19},{19,3},{4,20},{20... | collective-permute-start | bytes 1769480 | tf_op jit(solution)/shard_map/ppermute | solution.py:334
  62.1 1.8 %pack_out_weight.5.refs_1_ = bf16[384,512]{1,0:T(8,128)(2,1)} custom-call(bf16[192,1280]{1,0:T(8,128)(2,1)} %collective-permute-done.11.refs_3_.refs_0_, bf16[192,1280]{1,0:T(8,128)(2,1)} %collective-permute-done.12.refs_4_.refs_1_), custom_call_target="tpu_custom_call" | custom-call | bytes 983040 | tf_op jit(solution)/shard_map/pack_out_weight/pallas_call | solution.py:27
  63.9 0.6 collective-permute-start.16
  64.5 5.8 %spatial_projection.1.most_ref = f32[1024,384]{1,0:T(8,128)S(1)} custom-call(s32[10]{0:T(128)S(1)} %pad_add_fusion.meta_ref, bf16[512,3072]{1,0:T(8,128)(2,1)S(1)} %bitcast.30, bf16[512,3072]{1,0:T(8,128)(2,1)} %collective-permute-done.1.other_ref, bf16[192,1280]{1,0:T(8,128)(2,1)} %pad_maximum_fusion.refs_0_, ...), custom_call_target="tpu_custom_call" | custom-call | bytes 8749096 | tf_op jit(solution)/shard_map/spatial_projection/pallas_call | solution.py:27
  70.4 1.1 copy-done.1
  71.5 6.4 %collective-permute-done.13.refs_0_ = bf16[192,1280]{1,0:T(8,128)(2,1)} collective-permute-done((bf16[192,1280]{1,0:T(8,128)(2,1)}, bf16[192,1280]{1,0:T(8,128)(2,1)}, u32[]{:S(2)}, u32[]{:S(2)}) %collective-permute-start.13) | collective-permute-done | bytes 491552 | tf_op jit(solution)/shard_map/ppermute | solution.py:343
  77.9 2.1 %collective-permute-done.14.refs_1_ = bf16[192,1280]{1,0:T(8,128)(2,1)} collective-permute-done((bf16[192,1280]{1,0:T(8,128)(2,1)}, bf16[192,1280]{1,0:T(8,128)(2,1)}, u32[]{:S(2)}, u32[]{:S(2)}) %collective-permute-start.14) | collective-permute-done | bytes 491552 | tf_op jit(solution)/shard_map/ppermute | solution.py:344
  80.0 1.9 %broadcast_select_fusion = bf16[192,1280]{1,0:T(8,128)(2,1)} fusion(bf16[192,1280]{1,0:T(8,128)(2,1)} %collective-permute-done.13.refs_0_, bf16[192,1280]{1,0:T(8,128)(2,1)} %collective-permute-done.14.refs_1_, pred[]{:T(512)S(6)} %eq.6), kind=kLoop, calls=%fused_computation.3 | loop fusion | flops 245760 | bytes 1474561 | tf_op jit(solution)/shard_map/jit(_where)/select_n | solution.py:349
  81.9 5.9 %collective-permute-start.17 = (bf16[192,1280]{1,0:T(8,128)(2,1)}, bf16[192,1280]{1,0:T(8,128)(2,1)}, u32[]{:S(2)}, u32[]{:S(2)}) collective-permute-start(bf16[192,1280]{1,0:T(8,128)(2,1)} %broadcast_select_fusion), channel_id=1, source_target_pairs={{0,4},{4,8},{8,12},{12,14},{14,10},{10,6},{6,2},{2,0},{5,1},{9,5},... | collective-permute-start | bytes 1474568 | tf_op jit(solution)/shard_map/ppermute | solution.py:355
  87.9 1.8 %pack_out_weight.6.refs_2_ = bf16[384,512]{1,0:T(8,128)(2,1)} custom-call(bf16[192,1280]{1,0:T(8,128)(2,1)} %collective-permute-done.13.refs_0_, bf16[192,1280]{1,0:T(8,128)(2,1)} %collective-permute-done.14.refs_1_), custom_call_target="tpu_custom_call" | custom-call | bytes 983040 | tf_op jit(solution)/shard_map/pack_out_weight/pallas_call | solution.py:27
  89.7 1.6 %collective-permute-start.26 = (bf16[384,512]{1,0:T(8,128)(2,1)}, bf16[384,512]{1,0:T(8,128)(2,1)}, u32[]{:S(2)}, u32[]{:S(2)}) collective-permute-start(bf16[384,512]{1,0:T(8,128)(2,1)} %pack_out_weight.6.refs_2_), channel_id=1, source_target_pairs={{0,16},{16,0},{1,17},{17,1},{2,18},{18,2},{3,19},{19,3},{4,20},{20... | collective-permute-start | bytes 1179656 | tf_op jit(solution)/shard_map/ppermute | solution.py:334
  91.3 2.0 %temporal_attention.1 = bf16[2,16,32,128]{3,2,1,0:T(8,128)(2,1)S(1)} custom-call(s32[17]{0:T(128)S(1)} %pad_add_fusion.1.meta_ref, bf16[16,64,384]{2,1,0:T(8,128)(2,1)} %bitcast.13.qkv_ref), custom_call_target="tpu_custom_call" | custom-call | flops 5000000000 | bytes 786500 | tf_op jit(solution)/shard_map/temporal_attention/pallas_call | solution.py:27
  93.3 0.7 copy-done.7
  93.9 2.6 %all-to-all-start.1 = ((bf16[32,32,128]{2,1,0:T(8,128)(2,1)}), bf16[32,32,128]{2,1,0:T(8,128)(2,1)S(1)}, u32[]{:S(2)}, u32[]{:S(2)}) async-start(bf16[32,32,128]{2,1,0:T(8,128)(2,1)} %bitcast.33), calls=%async_computation.1 | async-start | bytes 524288 | tf_op jit(solution)/shard_map/all_to_all | solution.py:478
  96.5 1.6 %pack_out_weight.7.refs_3_ = bf16[192,512]{1,0:T(8,128)(2,1)} custom-call(bf16[192,1280]{1,0:T(8,128)(2,1)} %collective-permute-done.17.refs_2_.refs_0_), custom_call_target="tpu_custom_call" | custom-call | bytes 491520 | tf_op jit(solution)/shard_map/pack_out_weight/pallas_call | solution.py:27
  98.2 1.8 %collective-permute-start.27 = (bf16[192,512]{1,0:T(8,128)(2,1)}, bf16[192,512]{1,0:T(8,128)(2,1)}, u32[]{:S(2)}, u32[]{:S(2)}) collective-permute-start(bf16[192,512]{1,0:T(8,128)(2,1)} %pack_out_weight.7.refs_3_), channel_id=1, source_target_pairs={{0,16},{16,0},{1,17},{17,1},{2,18},{18,2},{3,19},{19,3},{4,20},{20... | collective-permute-start | bytes 589832 | tf_op jit(solution)/shard_map/ppermute | solution.py:334
  100.0 0.5 collective-permute-start.24
  100.5 1.4 %copy-done.2 = f32[1024,384]{1,0:T(8,128)S(1)} copy-done((f32[1024,384]{1,0:T(8,128)S(1)}, f32[1024,384]{1,0:T(8,128)}, u32[]{:S(2)}) %copy-start.2) | copy-done | bytes 1572888
  101.9 4.8 %spatial_heads.1 = bf16[2,2,256,128]{3,2,1,0:T(8,128)(2,1)S(1)} custom-call(s32[10]{0:T(128)S(1)} %pad_add_fusion.meta_ref, bf16[512,3072]{1,0:T(8,128)(2,1)S(1)} %bitcast.31, bf16[512,3072]{1,0:T(8,128)(2,1)} %collective-permute-done.1.other_ref, f32[1024,384]{1,0:T(8,128)S(1)} %copy-done.2, bf16[192,1280]{1,0:T(8,128)(2,1)} %collective-permute-done.13.refs_0_, ...), custom_call_target="tpu_custom_call" | custom-call | bytes 9338920 | tf_op jit(solution)/shard_map/spatial_heads/pallas_call | solution.py:27
  106.7 1.9 %collective-permute-done.27.refs_11_ = bf16[192,512]{1,0:T(8,128)(2,1)} collective-permute-done((bf16[192,512]{1,0:T(8,128)(2,1)}, bf16[192,512]{1,0:T(8,128)(2,1)}, u32[]{:S(2)}, u32[]{:S(2)}) %collective-permute-start.27) | collective-permute-done | bytes 196640 | tf_op jit(solution)/shard_map/ppermute | solution.py:334
  108.6 0.6 slice_bitcast_fusion
  109.3 1.6 %collective-permute-start.20 = (bf16[256,128]{1,0:T(8,128)(2,1)S(1)}, bf16[256,128]{1,0:T(8,128)(2,1)S(1)}, u32[]{:S(2)}, u32[]{:S(2)}) collective-permute-start(bf16[256,128]{1,0:T(8,128)(2,1)S(1)} %get-tuple-element.39), channel_id=1, source_target_pairs={{0,17},{1,16},{2,19},{3,18},{4,21},{5,20},{6,23},{7,22},{8,25},{9,... | collective-permute-start | bytes 196616 | tf_op jit(solution)/shard_map/ppermute | solution.py:534
  110.9 0.6 collective-permute-start.18
  111.7 1.6 %collective-permute-done.20.far_ref = bf16[256,128]{1,0:T(8,128)(2,1)S(1)} collective-permute-done((bf16[256,128]{1,0:T(8,128)(2,1)S(1)}, bf16[256,128]{1,0:T(8,128)(2,1)S(1)}, u32[]{:S(2)}, u32[]{:S(2)}) %collective-permute-start.20) | collective-permute-done | bytes 65568 | tf_op jit(solution)/shard_map/ppermute | solution.py:534
  113.5 0.3 collective-permute-start.29
  113.8 1.6 %collective-permute-done.18.peer_ref = bf16[256,128]{1,0:T(8,128)(2,1)S(1)} collective-permute-done((bf16[256,128]{1,0:T(8,128)(2,1)S(1)}, bf16[256,128]{1,0:T(8,128)(2,1)S(1)}, u32[]{:S(2)}, u32[]{:S(2)}) %collective-permute-start.18) | collective-permute-done | bytes 65568 | tf_op jit(solution)/shard_map/ppermute | solution.py:334
  115.6 0.5 copy-done.19
  116.0 0.7 copy-done.6
  116.8 0.6 collective-permute-done.30.refs_14_
  117.8 0.4 copy-done.14
  118.2 0.2 copy-done.10
  118.4 7.0 %out_projection.1 = bf16[256,3072]{1,0:T(8,128)(2,1)} custom-call(s32[10]{0:T(128)} %copy-done.8, bf16[256,128]{1,0:T(8,128)(2,1)} %get-tuple-element.42.mine_ref, bf16[256,128]{1,0:T(8,128)(2,1)} %copy-done.19, bf16[256,128]{1,0:T(8,128)(2,1)} %copy-done.18, bf16[256,128]{1,0:T(8,128)(2,1)} %copy-done.17, bf16[2,256,256]{2,1,0:T(8,128)(2,1)} %copy-done.6, ...), custom_call_target="tpu_custom_call" | custom-call | flops 1610612736 | bytes 6815784 | tf_op jit(solution)/shard_map/out_projection/pallas_call | solution.py:27
  (78 shorter events, 1.6 us)
Async XLA Ops:
  0.0 3.7 %copy-start = (bf16[1,512,3072]{2,1,0:T(8,128)(2,1)S(1)}, bf16[1,512,3072]{2,1,0:T(8,128)(2,1)}, u32[]{:S(2)}) copy-start(bf16[1,512,3072]{2,1,0:T(8,128)(2,1)} %param.7) | copy-start | bytes 9437188
  0.0 6.9 %copy-start.21 = (s32[8]{0:T(128)S(1)}, s32[8]{0:T(128)}, u32[]{:S(2)}) copy-start(s32[8]{0:T(128)} %constant.67.clone) | copy-start | bytes 100
  1.3 15.9 %copy-start.9 = (s32[8]{0:T(128)S(1)}, s32[8]{0:T(128)}, u32[]{:S(2)}) copy-start(s32[8]{0:T(128)} %constant.68.clone) | copy-start | bytes 100
  2.1 1.5 %collective-permute-start = (bf16[192,384]{1,0:T(8,128)(2,1)S(1)}, bf16[192,384]{1,0:T(8,128)(2,1)S(1)}, u32[]{:S(2)}, u32[]{:S(2)}) collective-permute-start(bf16[192,384]{1,0:T(8,128)(2,1)S(1)} %get-tuple-element.38), channel_id=1, source_target_pairs={{0,1},{1,0},{2,3},{3,2},{4,5},{5,4},{6,7},{7,6},{8,9},{9,8},{10,11... | collective-permute-start | bytes 442376 | tf_op jit(solution)/shard_map/ppermute | solution.py:331
  3.7 14.1 %copy-start.4 = (bf16[192,768]{1,0:T(8,128)(2,1)}, bf16[192,768]{1,0:T(8,128)(2,1)S(1)}, u32[]{:S(2)}) copy-start(bf16[192,768]{1,0:T(8,128)(2,1)S(1)} %pad_maximum_fusion.1.refs_0_) | copy-start | bytes 884740
  3.7 33.2 %collective-permute-start.1 = (bf16[512,3072]{1,0:T(8,128)(2,1)S(1)}, bf16[512,3072]{1,0:T(8,128)(2,1)}, u32[]{:S(2)}, u32[]{:S(2)}) collective-permute-start(bf16[512,3072]{1,0:T(8,128)(2,1)S(1)} %bitcast.27), channel_id=1, source_target_pairs={{0,1},{1,0},{2,3},{3,2},{4,5},{5,4},{6,7},{7,6},{8,9},{9,8},{10,11... | collective-permute-start | bytes 9437192 | tf_op jit(solution)/shard_map/ppermute | solution.py:331
  4.1 10.3 %collective-permute-start.7 = (bf16[192,768]{1,0:T(8,128)(2,1)S(1)}, bf16[192,768]{1,0:T(8,128)(2,1)}, u32[]{:S(2)}, u32[]{:S(2)}) collective-permute-start(bf16[192,768]{1,0:T(8,128)(2,1)S(1)} %pad_maximum_fusion.1.refs_0_), channel_id=1, source_target_pairs={{0,4},{1,5},{4,8},{5,9},{8,12},{9,13},{12,14},{13,15},{14,10},{15,... | collective-permute-start | bytes 884744 | tf_op jit(solution)/shard_map/ppermute | solution.py:343
  6.9 9.4 %collective-permute-start.3 = (bf16[192,768]{1,0:T(8,128)(2,1)S(1)}, bf16[192,768]{1,0:T(8,128)(2,1)}, u32[]{:S(2)}, u32[]{:S(2)}) collective-permute-start(bf16[192,768]{1,0:T(8,128)(2,1)S(1)} %pad_maximum_fusion.1.refs_0_), channel_id=1, source_target_pairs={{4,0},{5,1},{8,4},{9,5},{12,8},{13,9},{14,12},{15,13},{10,14},{11,... | collective-permute-start | bytes 884744 | tf_op jit(solution)/shard_map/ppermute | solution.py:344
  9.2 16.2 %collective-permute-start.2 = (bf16[192,384]{1,0:T(8,128)(2,1)}, bf16[192,384]{1,0:T(8,128)(2,1)}, u32[]{:S(2)}, u32[]{:S(2)}) collective-permute-start(bf16[192,384]{1,0:T(8,128)(2,1)} %get-tuple-element.36), channel_id=1, source_target_pairs={{0,1},{1,0},{2,3},{3,2},{4,5},{5,4},{6,7},{7,6},{8,9},{9,8},{10,11... | collective-permute-start | bytes 442376 | tf_op jit(solution)/shard_map/ppermute | solution.py:331
  14.4 9.0 %collective-permute-start.8 = (bf16[192,768]{1,0:T(8,128)(2,1)}, bf16[192,768]{1,0:T(8,128)(2,1)}, u32[]{:S(2)}, u32[]{:S(2)}) collective-permute-start(bf16[192,768]{1,0:T(8,128)(2,1)} %collective-permute-done.7.refs_1_), channel_id=1, source_target_pairs={{0,4},{1,5},{4,8},{5,9},{8,12},{9,13},{12,14},{13,15},{14,10},{15,... | collective-permute-start | bytes 884744 | tf_op jit(solution)/shard_map/ppermute | solution.py:343
  16.2 8.8 %collective-permute-start.4 = (bf16[192,768]{1,0:T(8,128)(2,1)}, bf16[192,768]{1,0:T(8,128)(2,1)}, u32[]{:S(2)}, u32[]{:S(2)}) collective-permute-start(bf16[192,768]{1,0:T(8,128)(2,1)} %collective-permute-done.3.refs_2_), channel_id=1, source_target_pairs={{4,0},{5,1},{8,4},{9,5},{12,8},{13,9},{14,12},{15,13},{10,14},{11,... | collective-permute-start | bytes 884744 | tf_op jit(solution)/shard_map/ppermute | solution.py:344
  23.4 10.2 %collective-permute-start.9 = (bf16[192,768]{1,0:T(8,128)(2,1)}, bf16[192,768]{1,0:T(8,128)(2,1)S(1)}, u32[]{:S(2)}, u32[]{:S(2)}) collective-permute-start(bf16[192,768]{1,0:T(8,128)(2,1)} %collective-permute-done.8.refs_3_), channel_id=1, source_target_pairs={{0,4},{1,5},{4,8},{5,9},{8,12},{9,13},{12,14},{13,15},{14,10},{15,... | collective-permute-start | bytes 884744 | tf_op jit(solution)/shard_map/ppermute | solution.py:343
  25.0 10.3 %collective-permute-start.10 = (bf16[192,768]{1,0:T(8,128)(2,1)}, bf16[192,768]{1,0:T(8,128)(2,1)}, u32[]{:S(2)}, u32[]{:S(2)}) collective-permute-start(bf16[192,768]{1,0:T(8,128)(2,1)} %collective-permute-done.4.refs_4_), channel_id=1, source_target_pairs={{4,0},{5,1},{8,4},{9,5},{12,8},{13,9},{14,12},{15,13},{10,14},{11,... | collective-permute-start | bytes 884744 | tf_op jit(solution)/shard_map/ppermute | solution.py:344
  27.4 16.4 %collective-permute-start.5 = (bf16[192,1280]{1,0:T(8,128)(2,1)}, bf16[192,1280]{1,0:T(8,128)(2,1)}, u32[]{:S(2)}, u32[]{:S(2)}) collective-permute-start(bf16[192,1280]{1,0:T(8,128)(2,1)} %pad_maximum_fusion.refs_0_), channel_id=1, source_target_pairs={{0,4},{1,5},{4,8},{5,9},{8,12},{9,13},{12,14},{13,15},{14,10},{15,... | collective-permute-start | bytes 1474568 | tf_op jit(solution)/shard_map/ppermute | solution.py:343
  28.9 16.9 %collective-permute-start.6 = (bf16[192,1280]{1,0:T(8,128)(2,1)}, bf16[192,1280]{1,0:T(8,128)(2,1)}, u32[]{:S(2)}, u32[]{:S(2)}) collective-permute-start(bf16[192,1280]{1,0:T(8,128)(2,1)} %pad_maximum_fusion.refs_0_), channel_id=1, source_target_pairs={{4,0},{5,1},{8,4},{9,5},{12,8},{13,9},{14,12},{15,13},{10,14},{11,... | collective-permute-start | bytes 1474568 | tf_op jit(solution)/shard_map/ppermute | solution.py:344
  29.5 71.0 %copy-start.8 = (s32[10]{0:T(128)}, s32[10]{0:T(128)S(1)}, u32[]{:S(2)}) copy-start(s32[10]{0:T(128)S(1)} %pad_add_fusion.meta_ref) | copy-start | bytes 124
  35.3 12.5 %collective-permute-start.21 = (bf16[192,768]{1,0:T(8,128)(2,1)S(1)}, bf16[192,768]{1,0:T(8,128)(2,1)S(1)}, u32[]{:S(2)}, u32[]{:S(2)}) collective-permute-start(bf16[192,768]{1,0:T(8,128)(2,1)S(1)} %broadcast_select_fusion.1), channel_id=1, source_target_pairs={{0,4},{4,8},{8,12},{12,14},{14,10},{10,6},{6,2},{2,0},{5,1},{9,5},... | collective-permute-start | bytes 884744 | tf_op jit(solution)/shard_map/ppermute | solution.py:355
  36.9 1.0 copy-start.5
  45.8 10.4 %collective-permute-start.11 = (bf16[192,1280]{1,0:T(8,128)(2,1)}, bf16[192,1280]{1,0:T(8,128)(2,1)}, u32[]{:S(2)}, u32[]{:S(2)}) collective-permute-start(bf16[192,1280]{1,0:T(8,128)(2,1)} %collective-permute-done.5.refs_1_), channel_id=1, source_target_pairs={{0,4},{1,5},{4,8},{5,9},{8,12},{9,13},{12,14},{13,15},{14,10},{15,... | collective-permute-start | bytes 1474568 | tf_op jit(solution)/shard_map/ppermute | solution.py:343
  47.4 10.9 %collective-permute-start.12 = (bf16[192,1280]{1,0:T(8,128)(2,1)}, bf16[192,1280]{1,0:T(8,128)(2,1)}, u32[]{:S(2)}, u32[]{:S(2)}) collective-permute-start(bf16[192,1280]{1,0:T(8,128)(2,1)} %collective-permute-done.6.refs_2_), channel_id=1, source_target_pairs={{4,0},{5,1},{8,4},{9,5},{12,8},{13,9},{14,12},{15,13},{10,14},{11,... | collective-permute-start | bytes 1474568 | tf_op jit(solution)/shard_map/ppermute | solution.py:344
  49.9 0.9 copy-start.3
  50.8 7.6 %copy-start.20 = (s32[16]{0:T(128)S(1)}, s32[16]{0:T(128)}, u32[]{:S(2)}) copy-start(s32[16]{0:T(128)} %param.10) | copy-start | bytes 196
  50.8 40.5 %all-to-all-start = ((bf16[8,2,2,32,384]{4,3,2,1,0:T(8,128)(2,1)}), bf16[8,2,2,32,384]{4,3,2,1,0:T(8,128)(2,1)}, u32[]{:S(2)}, u32[]{:S(2)}) async-start(bf16[8,2,2,32,384]{4,3,2,1,0:T(8,128)(2,1)} %copy-done.3), calls=%async_computation | async-start | bytes 1572864 | tf_op jit(solution)/shard_map/all_to_all | solution.py:450
  56.2 21.7 %collective-permute-start.13 = (bf16[192,1280]{1,0:T(8,128)(2,1)}, bf16[192,1280]{1,0:T(8,128)(2,1)}, u32[]{:S(2)}, u32[]{:S(2)}) collective-permute-start(bf16[192,1280]{1,0:T(8,128)(2,1)} %collective-permute-done.11.refs_3_.refs_0_), channel_id=1, source_target_pairs={{0,4},{1,5},{4,8},{5,9},{8,12},{9,13},{12,14},{13,15},{14,10},{15,... | collective-permute-start | bytes 1474568 | tf_op jit(solution)/shard_map/ppermute | solution.py:343
  58.3 21.8 %collective-permute-start.14 = (bf16[192,1280]{1,0:T(8,128)(2,1)}, bf16[192,1280]{1,0:T(8,128)(2,1)}, u32[]{:S(2)}, u32[]{:S(2)}) collective-permute-start(bf16[192,1280]{1,0:T(8,128)(2,1)} %collective-permute-done.12.refs_4_.refs_1_), channel_id=1, source_target_pairs={{4,0},{5,1},{8,4},{9,5},{12,8},{13,9},{14,12},{15,13},{10,14},{11,... | collective-permute-start | bytes 1474568 | tf_op jit(solution)/shard_map/ppermute | solution.py:344
  60.5 21.5 %collective-permute-start.15 = (bf16[576,512]{1,0:T(8,128)(2,1)}, bf16[576,512]{1,0:T(8,128)(2,1)}, u32[]{:S(2)}, u32[]{:S(2)}) collective-permute-start(bf16[576,512]{1,0:T(8,128)(2,1)} %pack_out_weight.4.refs_0_), channel_id=1, source_target_pairs={{0,16},{16,0},{1,17},{17,1},{2,18},{18,2},{3,19},{19,3},{4,20},{20... | collective-permute-start | bytes 1769480 | tf_op jit(solution)/shard_map/ppermute | solution.py:334
  63.9 18.0 %collective-permute-start.16 = (bf16[384,512]{1,0:T(8,128)(2,1)}, bf16[384,512]{1,0:T(8,128)(2,1)}, u32[]{:S(2)}, u32[]{:S(2)}) collective-permute-start(bf16[384,512]{1,0:T(8,128)(2,1)} %pack_out_weight.5.refs_1_), channel_id=1, source_target_pairs={{0,16},{16,0},{1,17},{17,1},{2,18},{18,2},{3,19},{19,3},{4,20},{20... | collective-permute-start | bytes 1179656 | tf_op jit(solution)/shard_map/ppermute | solution.py:334
  70.4 1.1 copy-start.1
  81.9 14.6 %collective-permute-start.17 = (bf16[192,1280]{1,0:T(8,128)(2,1)}, bf16[192,1280]{1,0:T(8,128)(2,1)}, u32[]{:S(2)}, u32[]{:S(2)}) collective-permute-start(bf16[192,1280]{1,0:T(8,128)(2,1)} %broadcast_select_fusion), channel_id=1, source_target_pairs={{0,4},{4,8},{8,12},{12,14},{14,10},{10,6},{6,2},{2,0},{5,1},{9,5},... | collective-permute-start | bytes 1474568 | tf_op jit(solution)/shard_map/ppermute | solution.py:355
  87.9 23.0 %collective-permute-start.22 = (bf16[576,512]{1,0:T(8,128)(2,1)}, bf16[576,512]{1,0:T(8,128)(2,1)}, u32[]{:S(2)}, u32[]{:S(2)}) collective-permute-start(bf16[576,512]{1,0:T(8,128)(2,1)} %pack_out_weight.4.refs_0_), channel_id=1, source_target_pairs={{0,1},{1,0},{2,3},{3,2},{4,5},{5,4},{6,7},{7,6},{8,9},{9,8},{10,11... | collective-permute-start | bytes 1769480 | tf_op jit(solution)/shard_map/ppermute | solution.py:331
  89.7 17.0 %collective-permute-start.26 = (bf16[384,512]{1,0:T(8,128)(2,1)}, bf16[384,512]{1,0:T(8,128)(2,1)}, u32[]{:S(2)}, u32[]{:S(2)}) collective-permute-start(bf16[384,512]{1,0:T(8,128)(2,1)} %pack_out_weight.6.refs_2_), channel_id=1, source_target_pairs={{0,16},{16,0},{1,17},{17,1},{2,18},{18,2},{3,19},{19,3},{4,20},{20... | collective-permute-start | bytes 1179656 | tf_op jit(solution)/shard_map/ppermute | solution.py:334
  93.3 0.7 copy-start.7
  93.9 21.6 %all-to-all-start.1 = ((bf16[32,32,128]{2,1,0:T(8,128)(2,1)}), bf16[32,32,128]{2,1,0:T(8,128)(2,1)S(1)}, u32[]{:S(2)}, u32[]{:S(2)}) async-start(bf16[32,32,128]{2,1,0:T(8,128)(2,1)} %bitcast.33), calls=%async_computation.1 | async-start | bytes 524288 | tf_op jit(solution)/shard_map/all_to_all | solution.py:478
  98.2 10.5 %collective-permute-start.27 = (bf16[192,512]{1,0:T(8,128)(2,1)}, bf16[192,512]{1,0:T(8,128)(2,1)}, u32[]{:S(2)}, u32[]{:S(2)}) collective-permute-start(bf16[192,512]{1,0:T(8,128)(2,1)} %pack_out_weight.7.refs_3_), channel_id=1, source_target_pairs={{0,16},{16,0},{1,17},{17,1},{2,18},{18,2},{3,19},{19,3},{4,20},{20... | collective-permute-start | bytes 589832 | tf_op jit(solution)/shard_map/ppermute | solution.py:334
  100.0 10.9 %collective-permute-start.23 = (bf16[384,512]{1,0:T(8,128)(2,1)}, bf16[384,512]{1,0:T(8,128)(2,1)S(1)}, u32[]{:S(2)}, u32[]{:S(2)}) collective-permute-start(bf16[384,512]{1,0:T(8,128)(2,1)} %pack_out_weight.5.refs_1_), channel_id=1, source_target_pairs={{0,1},{1,0},{2,3},{3,2},{4,5},{5,4},{6,7},{7,6},{8,9},{9,8},{10,11... | collective-permute-start | bytes 1179656 | tf_op jit(solution)/shard_map/ppermute | solution.py:331
  100.0 11.5 %collective-permute-start.24 = (bf16[384,512]{1,0:T(8,128)(2,1)}, bf16[384,512]{1,0:T(8,128)(2,1)S(1)}, u32[]{:S(2)}, u32[]{:S(2)}) collective-permute-start(bf16[384,512]{1,0:T(8,128)(2,1)} %pack_out_weight.6.refs_2_), channel_id=1, source_target_pairs={{0,1},{1,0},{2,3},{3,2},{4,5},{5,4},{6,7},{7,6},{8,9},{9,8},{10,11... | collective-permute-start | bytes 1179656 | tf_op jit(solution)/shard_map/ppermute | solution.py:331
  100.5 1.4 %copy-start.2 = (f32[1024,384]{1,0:T(8,128)S(1)}, f32[1024,384]{1,0:T(8,128)}, u32[]{:S(2)}) copy-start(f32[1024,384]{1,0:T(8,128)} %copy-done.1) | copy-start | bytes 4718596
  108.6 8.8 %collective-permute-start.28 = (bf16[576,512]{1,0:T(8,128)(2,1)}, bf16[576,512]{1,0:T(8,128)(2,1)S(1)}, u32[]{:S(2)}, u32[]{:S(2)}) collective-permute-start(bf16[576,512]{1,0:T(8,128)(2,1)} %collective-permute-done.15.refs_8_), channel_id=1, source_target_pairs={{0,1},{1,0},{2,3},{3,2},{4,5},{5,4},{6,7},{7,6},{8,9},{9,8},{10,11... | collective-permute-start | bytes 1769480 | tf_op jit(solution)/shard_map/ppermute | solution.py:331
  109.3 4.0 %collective-permute-start.20 = (bf16[256,128]{1,0:T(8,128)(2,1)S(1)}, bf16[256,128]{1,0:T(8,128)(2,1)S(1)}, u32[]{:S(2)}, u32[]{:S(2)}) collective-permute-start(bf16[256,128]{1,0:T(8,128)(2,1)S(1)} %get-tuple-element.39), channel_id=1, source_target_pairs={{0,17},{1,16},{2,19},{3,18},{4,21},{5,20},{6,23},{7,22},{8,25},{9,... | collective-permute-start | bytes 196616 | tf_op jit(solution)/shard_map/ppermute | solution.py:534
  110.9 2.6 %collective-permute-start.19 = (bf16[256,128]{1,0:T(8,128)(2,1)S(1)}, bf16[256,128]{1,0:T(8,128)(2,1)S(1)}, u32[]{:S(2)}, u32[]{:S(2)}) collective-permute-start(bf16[256,128]{1,0:T(8,128)(2,1)S(1)} %get-tuple-element.40), channel_id=1, source_target_pairs={{0,1},{1,0},{2,3},{3,2},{4,5},{5,4},{6,7},{7,6},{8,9},{9,8},{10,11... | collective-permute-start | bytes 196616 | tf_op jit(solution)/shard_map/ppermute | solution.py:331
  110.9 4.5 %copy-start.11 = (bf16[384,512]{1,0:T(8,128)(2,1)}, bf16[384,512]{1,0:T(8,128)(2,1)S(1)}, u32[]{:S(2)}) copy-start(bf16[384,512]{1,0:T(8,128)(2,1)S(1)} %collective-permute-done.23.refs_5_) | copy-start | bytes 1179652
  110.9 4.5 %collective-permute-start.18 = (bf16[256,128]{1,0:T(8,128)(2,1)S(1)}, bf16[256,128]{1,0:T(8,128)(2,1)S(1)}, u32[]{:S(2)}, u32[]{:S(2)}) collective-permute-start(bf16[256,128]{1,0:T(8,128)(2,1)S(1)} %get-tuple-element.41), channel_id=1, source_target_pairs={{0,16},{16,0},{1,17},{17,1},{2,18},{18,2},{3,19},{19,3},{4,20},{20... | collective-permute-start | bytes 196616 | tf_op jit(solution)/shard_map/ppermute | solution.py:334
  111.5 3.9 %copy-start.12 = (bf16[384,512]{1,0:T(8,128)(2,1)}, bf16[384,512]{1,0:T(8,128)(2,1)S(1)}, u32[]{:S(2)}) copy-start(bf16[384,512]{1,0:T(8,128)(2,1)S(1)} %collective-permute-done.24.refs_6_) | copy-start | bytes 1179652
  111.5 5.3 %collective-permute-start.25 = (bf16[192,512]{1,0:T(8,128)(2,1)}, bf16[192,512]{1,0:T(8,128)(2,1)S(1)}, u32[]{:S(2)}, u32[]{:S(2)}) collective-permute-start(bf16[192,512]{1,0:T(8,128)(2,1)} %pack_out_weight.7.refs_3_), channel_id=1, source_target_pairs={{0,1},{1,0},{2,3},{3,2},{4,5},{5,4},{6,7},{7,6},{8,9},{9,8},{10,11... | collective-permute-start | bytes 589832 | tf_op jit(solution)/shard_map/ppermute | solution.py:331
  113.3 2.3 %copy-start.17 = (bf16[256,128]{1,0:T(8,128)(2,1)}, bf16[256,128]{1,0:T(8,128)(2,1)S(1)}, u32[]{:S(2)}) copy-start(bf16[256,128]{1,0:T(8,128)(2,1)S(1)} %collective-permute-done.20.far_ref) | copy-start | bytes 196612
  113.3 3.5 %collective-permute-start.31 = (bf16[192,512]{1,0:T(8,128)(2,1)}, bf16[192,512]{1,0:T(8,128)(2,1)S(1)}, u32[]{:S(2)}, u32[]{:S(2)}) collective-permute-start(bf16[192,512]{1,0:T(8,128)(2,1)} %collective-permute-done.27.refs_11_), channel_id=1, source_target_pairs={{0,1},{1,0},{2,3},{3,2},{4,5},{5,4},{6,7},{7,6},{8,9},{9,8},{10,11... | collective-permute-start | bytes 589832 | tf_op jit(solution)/shard_map/ppermute | solution.py:331
  113.5 2.1 %copy-start.18 = (bf16[256,128]{1,0:T(8,128)(2,1)}, bf16[256,128]{1,0:T(8,128)(2,1)S(1)}, u32[]{:S(2)}) copy-start(bf16[256,128]{1,0:T(8,128)(2,1)S(1)} %collective-permute-done.19.core_ref) | copy-start | bytes 196612
  113.5 3.3 %collective-permute-start.29 = (bf16[384,512]{1,0:T(8,128)(2,1)}, bf16[384,512]{1,0:T(8,128)(2,1)S(1)}, u32[]{:S(2)}, u32[]{:S(2)}) collective-permute-start(bf16[384,512]{1,0:T(8,128)(2,1)} %collective-permute-done.16.refs_9_), channel_id=1, source_target_pairs={{0,1},{1,0},{2,3},{3,2},{4,5},{5,4},{6,7},{7,6},{8,9},{9,8},{10,11... | collective-permute-start | bytes 1179656 | tf_op jit(solution)/shard_map/ppermute | solution.py:331
  115.4 0.6 copy-start.19
  115.4 2.0 %collective-permute-start.30 = (bf16[384,512]{1,0:T(8,128)(2,1)}, bf16[384,512]{1,0:T(8,128)(2,1)S(1)}, u32[]{:S(2)}, u32[]{:S(2)}) collective-permute-start(bf16[384,512]{1,0:T(8,128)(2,1)} %collective-permute-done.26.refs_10_), channel_id=1, source_target_pairs={{0,1},{1,0},{2,3},{3,2},{4,5},{5,4},{6,7},{7,6},{8,9},{9,8},{10,11... | collective-permute-start | bytes 1179656 | tf_op jit(solution)/shard_map/ppermute | solution.py:331
  116.0 0.7 copy-start.6
  116.8 0.7 copy-start.15
  116.8 0.8 copy-start.16
  116.8 1.0 copy-start.13
  117.4 0.8 copy-start.14
  117.4 1.0 copy-start.10

commit v5 on v4

--- a/solution.py
+++ b/solution.py
@@ -11,12 +11,12 @@
 HEAD = 128
 HS_DEV = 2
 SCALE = 1.0 / math.sqrt(HEAD)
-CFG = dict(A=1, B=3, C=1, D1=5, D2=5, F=2, G=1, H=3, I=0, MT=1, MS=3, K=0)
 MIB = 1024 * 1024
-FIRST = 25_000_000_000
-
-
-def kernel_call(body, out_shape, args, flops, name, whole=(), scratch=(), limit=16 * MIB):
+LEADS = 5_000_000_000
+PACKS = 1_000_000_000
+
+
+def kernel_call(body, out_shape, args, flops, name, whole=(), scratch=(), limit=16 * MIB, out_space=pltpu.VMEM):
     bytes_moved = sum(a.size * a.dtype.itemsize for a in args)
 
     def space(i, a):
@@ -28,7 +28,7 @@
         body,
         out_shape=out_shape,
         in_specs=[pl.BlockSpec(memory_space=space(i, a)) for i, a in enumerate(args)],
-        out_specs=pl.BlockSpec(memory_space=pltpu.VMEM),
+        out_specs=pl.BlockSpec(memory_space=out_space),
         scratch_shapes=list(scratch),
         compiler_params=pltpu.CompilerParams(vmem_limit_bytes=limit),
         cost_estimate=pl.CostEstimate(flops=flops, bytes_accessed=bytes_moved, transcendentals=0),
@@ -80,8 +80,12 @@
     ]
 
 
-def most_body(depth, meta_ref, own_ref, other_ref, *refs):
-    *piece_refs, out_ref, weight, frames, sems = refs
+def most_body(depth, meta_ref, own_ref, other_ref, *refs, copied=False):
+    if copied:
+        *piece_refs, out_ref, weight, frames, sems, sums, out_sems = refs
+    else:
+        *piece_refs, out_ref, weight, frames, sems = refs
+        sums = out_ref
     for slot in range(len(piece_refs), weight.shape[0] // (2 * depth)):
         missing = meta_ref[2 + slot] * 2 * depth
         weight[pl.ds(pl.multiple_of(missing, 16), 2 * depth), :] = jnp.zeros(
@@ -90,18 +94,36 @@
     last = load_all(depth, meta_ref, own_ref, other_ref, piece_refs, weight, frames, sems)
     patches = own_ref.shape[0]
     half = patches // 2
+    copies = []
     for frame in range(2):
         if frame == 1:
             last.wait()
         for first in range(0, patches, half):
-            out_ref[frame * patches + first : frame * patches + first + half, :] = jnp.dot(
+            here = slice(frame * patches + first, frame * patches + first + half)
+            sums[here, :] = jnp.dot(
                 frames[frame, first : first + half, :],
                 weight[...],
                 preferred_element_type=jnp.float32,
             )
-
-
-def add_rest(depth, chips, meta_ref, own_ref, other_ref, most_ref, piece_refs, weight, frames, sems):
+            if copied:
+                copies.append(
+                    pltpu.make_async_copy(
+                        sums.at[here, :], out_ref.at[here, :], out_sems.at[len(copies)]
+                    )
+                )
+                copies[-1].start()
+    for copy in copies:
+        copy.wait()
+
+
+def add_rest(
+    depth, chips, meta_ref, own_ref, other_ref, most_ref, piece_refs, weight, frames, sems, fetch=None
+):
+    fetched = []
+    if fetch is not None:
+        most, fetch_sem = fetch
+        fetched.append(pltpu.make_async_copy(most_ref, most, fetch_sem))
+        most_ref = most
     patches = own_ref.shape[0]
     late = len(piece_refs)
     copies = [[], []]
@@ -118,7 +140,7 @@
                     sems.at[k, i],
                 )
             )
-    for copy in copies[0] + copies[1]:
+    for copy in fetched + copies[0] + copies[1]:
         copy.start()
     core = meta_ref[0]
     columns = weight.shape[1]
@@ -128,6 +150,8 @@
             weight[pl.ds(pl.multiple_of(at, 16), depth), :] = piece_ref[
                 :, k * columns : (k + 1) * columns
             ]
+    for copy in fetched:
+        copy.wait()
     half = patches // 2
     for frame in range(2):
         for copy in copies[frame]:
@@ -159,11 +183,11 @@
 
 
 def spatial_body(depth, chips, n_st, late, meta_ref, own_ref, other_ref, most_ref, *refs):
-    piece_refs, (out_ref, *scratch, packed) = refs[:late], refs[late:]
+    piece_refs, (out_ref, *scratch, packed, most, fetch_sem) = refs[:late], refs[late:]
     patches = own_ref.shape[0]
     part = patches // n_st
     for frame, first, result in add_rest(
-        depth, chips, meta_ref, own_ref, other_ref, most_ref, piece_refs, *scratch
+        depth, chips, meta_ref, own_ref, other_ref, most_ref, piece_refs, *scratch, (most, fetch_sem)
     ):
         packed[first : first + result.shape[0], :] = result
         if first + result.shape[0] < patches:
@@ -238,7 +262,7 @@
         copies.append(
             pltpu.make_async_copy(
                 ref.at[:, pl.ds(split, columns - split)],
-                out_ref.at[pl.ds(i * rows, rows), :],
+                out_ref.at[i],
                 sems.at[i],
             )
         )
@@ -265,21 +289,20 @@
     core, st = meta_ref[0], meta_ref[1]
     n_st, chips = temporal_ref.shape[0], out_ref.shape[1] // (2 * depth)
     copies = [[] for _ in range(chips)]
-    for kind in range(4):
-        group = st if kind < 2 else 1 - st
-        side = core if kind % 2 == 0 else 1 - core
-        slot = 0
-        for ref in weight_refs[kind * count : (kind + 1) * count]:
-            for first in range(0, ref.shape[0], depth):
-                at = slot * 2 * depth + side * depth
-                copies[slot].append(
-                    pltpu.make_async_copy(
-                        ref.at[pl.ds(first, depth), :],
-                        weight.at[group, pl.ds(pl.multiple_of(at, 16), depth), :],
-                        sems.at[slot, kind],
-                    )
+    slot = 0
+    for i in range(count):
+        slots = weight_refs[i].shape[0]
+        for kind in range(4):
+            group = st if kind < 2 else 1 - st
+            side = core if kind % 2 == 0 else 1 - core
+            copies[slot].append(
+                pltpu.make_async_copy(
+                    weight_refs[kind * count + i],
+                    weight.at[group, pl.ds(slot, slots), side],
+                    sems.at[i, kind],
                 )
-                slot += 1
+            )
+        slot += slots
     for copy in sum(copies, []):
         copy.start()
     mine, far = pl.multiple_of(core * HEAD, HEAD), pl.multiple_of((1 - core) * HEAD, HEAD)
@@ -287,23 +310,32 @@
     heads[1 - st, :, pl.ds(mine, HEAD)] = peer_ref[...]
     heads[st, :, pl.ds(far, HEAD)] = core_ref[...]
     heads[1 - st, :, pl.ds(far, HEAD)] = far_ref[...]
-    heads[:, :, HS_DEV * HEAD :] = temporal_ref[...]
+    if len(temporal_ref.shape) == 3:
+        heads[:, :, HS_DEV * HEAD :] = temporal_ref[...]
+    else:
+        part = temporal_ref.shape[3]
+        for group in range(n_st):
+            for chip in range(chips):
+                for k in range(2):
+                    heads[
+                        group,
+                        chip * part : (chip + 1) * part,
+                        (HS_DEV + k) * HEAD : (HS_DEV + k + 1) * HEAD,
+                    ] = temporal_ref[group, chip, k]
     chip_width = 2 * depth
-    for slot in range(0, chips, 2):
-        for copy in copies[slot] + copies[slot + 1]:
+    for slot in range(chips):
+        for copy in copies[slot]:
             copy.wait()
         total = 0.0
         for group in range(n_st):
             total += lax.dot_general(
                 heads[group],
-                weight[group, slot * chip_width : (slot + 2) * chip_width, :],
+                weight[group, slot].reshape(chip_width, -1),
                 (((1,), (1,)), ((), ())),
                 preferred_element_type=jnp.float32,
             )
-        total = total.astype(jnp.bfloat16)
-        for k in range(2):
-            at = pl.multiple_of(meta_ref[2 + slot + k] * chip_width, chip_width)
-            out_ref[:, pl.ds(at, chip_width)] = total[:, k * chip_width : (k + 1) * chip_width]
+        at = pl.multiple_of(meta_ref[2 + slot] * chip_width, chip_width)
+        out_ref[:, pl.ds(at, chip_width)] = total.astype(jnp.bfloat16)
 
 
 def shards(n_st, n_fsdp, normed, qkv_weight, out_weight, segment_ids):
@@ -379,8 +411,7 @@
 
     temporal_ring = ring_gather(temporal_piece)
     second_pieces, _ = run(temporal_ring, 3)
-    third_pieces, _ = run(temporal_ring, chips // 2 - 3)
-    _, last_sent = run(temporal_ring, 1)
+    run(temporal_ring, chips // 2 - 2)
     pieces, _ = next(temporal_ring)
     own, later_head, _ = lax.optimization_barrier((own, by_head[:HS_DEV], temporal_piece))
     other = to_core(own)
@@ -388,8 +419,8 @@
     split = spatial_piece.shape[1]
     both_ring = ring_gather(jnp.concatenate([spatial_piece, out_weight], axis=1))
     next(both_ring)
-    first_pieces, _ = both_ring.send([None, last_sent, third_pieces[-1], second_pieces[-1]][CFG['H']])
-    temporal_late, spatial_late = CFG['MT'], CFG['MS']
+    both_ring.send(second_pieces[-1])
+    temporal_late, spatial_late = 1, 3
     head_flops = 4 * patches * width * 3 * HEAD
     shape = (chips, 2, n_st, part, 3 * HEAD) if direct else (2 * patches, 3 * HEAD)
     most = kernel_call(
@@ -400,9 +431,7 @@
         "temporal_projection",
         scratch=load_scratch(2 * chips, patches, width),
     )
-    temporal_most = most
-    if CFG['A']:
-        most, *_ = lax.optimization_barrier((most, *first_pieces))
+
     def shares(late):
         if 2 * depth % 128 == 0:
             return own, other
@@ -424,7 +453,7 @@
             pltpu.SemaphoreType.DMA((2, late)),
         ]
 
-    temporal = projected = kernel_call(
+    temporal = kernel_call(
         functools.partial(rest_body, depth, chips, n_st, direct, temporal_late),
         jax.ShapeDtypeStruct(shape, jnp.bfloat16),
         [ring_meta, *shares(temporal_late), most, *pieces[chips - temporal_late :]],
@@ -435,17 +464,23 @@
     )
     if not direct:
         temporal = temporal.reshape(2, n_st, chips, part, 3 * HEAD).transpose(2, 0, 1, 3, 4)
-    second_parts, _ = both_ring.send([None, projected, temporal_most][CFG['F']])
+    second_parts, _ = both_ring.send(most)
     if chips > 8:
         second_parts, _ = run(both_ring, chips // 2 - 4)
     spatial_most = kernel_call(
-        functools.partial(most_body, depth),
+        functools.partial(most_body, depth, copied=True),
         jax.ShapeDtypeStruct((2 * patches, 3 * HEAD), jnp.float32),
         [ring_meta, own, other, *second_parts[: chips - spatial_late]],
         0,
         "spatial_projection",
-        scratch=load_scratch(2 * chips, patches, width),
-    )
+        scratch=[
+            *load_scratch(2 * chips, patches, width),
+            pltpu.VMEM((2 * patches, 3 * HEAD), jnp.float32),
+            pltpu.SemaphoreType.DMA((4,)),
+        ],
+        out_space=pl.ANY,
+    )
+    third_parts, _ = both_ring.send(None)
     same_core = [[2 * i + c for i in range(chips)] for c in range(2)]
     temporal = lax.all_to_all(
         temporal,
@@ -458,8 +493,7 @@
     pairs = segment_ids.reshape(chips, 2)
     pairs = jnp.where(core == 0, pairs, pairs[:, ::-1]).reshape(frames)
     clips = jnp.concatenate([pairs, core.reshape(1)]).astype(jnp.int32)
-    if CFG['K']:
-        temporal, _ = lax.optimization_barrier((temporal, spatial_most))
+    temporal, _ = lax.optimization_barrier((temporal, third_parts[-1]))
     tile = min(n_st * part, max(16, 256 // frames))
     if part % tile == 0:
         shape = (n_st, frames, part, HEAD)
@@ -469,7 +503,7 @@
         functools.partial(temporal_body, tile),
         jax.ShapeDtypeStruct(shape, jnp.bfloat16),
         [clips, temporal],
-        CFG['D1'] * 1000000000,
+        LEADS,
         "temporal_attention",
         whole=(1,),
     )
@@ -487,9 +521,9 @@
     def pack(group):
         return kernel_call(
             functools.partial(pack_body, split),
-            jax.ShapeDtypeStruct((depth * len(group), out_weight.shape[1]), jnp.bfloat16),
+            jax.ShapeDtypeStruct((len(group), depth, out_weight.shape[1]), jnp.bfloat16),
             group,
-            0,
+            PACKS,
             "pack_out_weight",
             scratch=[pltpu.SemaphoreType.DMA((len(group),))],
             limit=60 * MIB,
@@ -500,22 +534,21 @@
     if early:
         kinds = [pack(parts[:3]), pack(parts[3:5])]
         peers = [to_peer(k) for k in kinds]
-    both_ring.send(attention if CFG['I'] else None)
-    both_ring.send([None, attention, None, spatial_most][CFG['B']])
-    late = []
-    if CFG['B'] == 2:
-        late.append(attention)
-    if CFG['C'] == 1 and early:
-        late += peers
-    parts, _ = both_ring.send(tuple(late) if late else None)
+    both_ring.send(spatial_most)
+    parts, _ = both_ring.send((attention, *peers) if early else attention)
     spatial = kernel_call(
         functools.partial(spatial_body, depth, chips, n_st, spatial_late),
         jax.ShapeDtypeStruct((n_st, 2, rows, HEAD), jnp.bfloat16),
         [ring_meta, *shares(spatial_late), spatial_most, *parts[chips - spatial_late :]],
         0,
         "spatial_heads",
-        whole=range(3, 4 + spatial_late),
-        scratch=[*rest_scratch(spatial_late), pltpu.VMEM((patches, 3 * HEAD), jnp.bfloat16)],
+        whole=range(4, 4 + spatial_late),
+        scratch=[
+            *rest_scratch(spatial_late),
+            pltpu.VMEM((patches, 3 * HEAD), jnp.bfloat16),
+            pltpu.VMEM((2 * patches, 3 * HEAD), jnp.float32),
+            pltpu.SemaphoreType.DMA,
+        ],
     )
 
     if early:
@@ -523,7 +556,7 @@
             order_body,
             jax.ShapeDtypeStruct((n_st, rows, 2 * HEAD), jnp.bfloat16),
             [temporal_heads],
-            CFG['D2'] * 1000000000,
+            LEADS,
             "temporal_heads",
             whole=(0,),
         )
@@ -538,8 +571,7 @@
         peers += [to_peer(k) for k in kinds[2:]]
         count = len(kinds)
         kinds += [to_core(k) for k in kinds] + peers
-        if CFG['G']:
-            peers = lax.optimization_barrier((*peers, attention if CFG['G'] == 1 else spatial))[:-1]
+        peers = lax.optimization_barrier((*peers, spatial))[:-1]
         kinds += [to_core(k) for k in peers]
         attended = kernel_call(
             functools.partial(out_body, depth, count),
@@ -550,8 +582,8 @@
             whole=(1, 2, 3, 4, 5),
             scratch=[
                 pltpu.VMEM((n_st, rows, out_weight.shape[1]), jnp.bfloat16),
-                pltpu.VMEM((n_st, width, out_weight.shape[1]), jnp.bfloat16),
-                pltpu.SemaphoreType.DMA((chips, 4)),
+                pltpu.VMEM((n_st, chips, 2, depth, out_weight.shape[1]), jnp.bfloat16),
+                pltpu.SemaphoreType.DMA((count, 4)),
             ],
             limit=60 * MIB,
         )

time: 126 us -> 125 us (level)
  waiting for transfers between devices: 33.9 us -> 31.4 us
  Pallas kernels: 34.7 us -> 36.6 us
    pallas_call x11, Pallas kernels: 34.7 us -> 36.6 us  [kernel_call(): pl.pallas_call(body, out_shape=out_shape, in_specs=[pl.BlockSpec(memory_s...]
    ppermute x5, waiting for transfers between devices: 3.54 us -> 1.92 us  [to_peer(): return lax.ppermute(x, 'st', [(0, 1), (1, 0)])]
    ppermute x6, waiting for transfers between devices: 21.3 us -> 19.8 us  [ring_gather(): ahead = lax.ppermute(ahead, 'fsdp', forward)]
  transfers between devices with their start and end apart: 34 -> 34, of which waited for: 12 -> 13; matrix products, arithmetic and copies ran while one was open for 7% -> 7% of each run, Pallas kernels for 22% -> 24%
where the time goes in v5:
time: 125 us; the launch traced here: 124 us
  starting transfers between devices  38.5 us (31%)
  Pallas kernels  36.6 us (29%)
  waiting for transfers between devices  31.4 us (25%)
  local copies, waits for them, and re-layouts  12.6 us (10%)
  other arithmetic  4.7 us (4%)
    pallas_call x11, Pallas kernels, kernel_call(): pl.pallas_call(body, out_shape=out_shape, in_specs=[pl.BlockSpec(memory_s...  36.6 us
    ppermute x6, waiting for transfers between devices, ring_gather(): ahead = lax.ppermute(ahead, 'fsdp', forward)  19.8 us
    ppermute x6, starting transfers between devices, ring_gather(): ahead = lax.ppermute(ahead, 'fsdp', forward)  11.2 us
    unnamed x45, local copies, waits for them, and re-layouts  7.83 us
    ppermute x2, starting transfers between devices, ring_gather(): yield (pieces + [lax.ppermute(sent, 'fsdp', both)], None)  7.52 us
    ppermute x5, starting transfers between devices, to_peer(): return lax.ppermute(x, 'st', [(0, 1), (1, 0)])  5.87 us
    ppermute x6, waiting for transfers between devices, ring_gather(): behind = lax.ppermute(behind, 'fsdp', backward)  5.84 us
    all_to_all x1, starting transfers between devices, shards(): lax.all_to_all(temporal, 'fsdp', split_axis=0, concat_axis=0, tiled=True,...  5.47 us
  transfers between devices with their start and end apart: 34, of which 13 were waited for; matrix products, arithmetic and copies ran while one was open for 7% of the time, Pallas kernels for 24%

profile of v5, /device:TPU:0, one launch (start us, length us, event | category | flops | bytes accessed | tf_op | source)
XLA Modules:
  0.0 124.3 jit_solution(15902162897743242324)
XLA Ops:
  0.0 1.3 %copy.10 = bf16[192,4,384]{2,0,1:T(8,128)(2,1)S(1)} copy(bf16[192,4,384]{2,1,0:T(4,128)(2,1)} %param.8) | data formatting | bytes 1179648 | tf_op args[1]
  1.3 0.8 fusion.1
  2.1 0.5 collective-permute-start
  2.6 1.0 collective-permute-done
  3.7 0.4 collective-permute-start.1
  4.1 2.7 %collective-permute-start.7 = (bf16[192,768]{1,0:T(8,128)(2,1)S(1)}, bf16[192,768]{1,0:T(8,128)(2,1)}, u32[]{:S(2)}, u32[]{:S(2)}) collective-permute-start(bf16[192,768]{1,0:T(8,128)(2,1)S(1)} %pad_maximum_fusion.1.refs_0_), channel_id=1, source_target_pairs={{0,4},{1,5},{4,8},{5,9},{8,12},{9,13},{12,14},{13,15},{14,10},{15,... | collective-permute-start | bytes 884744 | tf_op jit(solution)/shard_map/ppermute | solution.py:375
  6.9 0.7 dynamic_slice.16
  7.5 1.7 %dynamic-slice_bitcast_fusion.1 = (bf16[192,384]{1,0:T(8,128)(2,1)}, bf16[192,384]{1,0:T(8,128)(2,1)}) fusion(bf16[2,192,384]{2,1,0:T(8,128)(2,1)} %get-tuple-element.20, s32[]{:T(128)S(6)} %select_n.61, s32[]{:T(128)S(6)} %select_n.62), kind=kLoop, calls=%fused_computation.7 | loop fusion | bytes 589832 | tf_op jit(solution)/shard_map/jit(dynamic_index_in_dim)/squeeze | solution.py:405
  9.3 5.1 %collective-permute-done.7.refs_1_ = bf16[192,768]{1,0:T(8,128)(2,1)} collective-permute-done((bf16[192,768]{1,0:T(8,128)(2,1)S(1)}, bf16[192,768]{1,0:T(8,128)(2,1)}, u32[]{:S(2)}, u32[]{:S(2)}) %collective-permute-start.7) | collective-permute-done | bytes 294944 | tf_op jit(solution)/shard_map/ppermute | solution.py:375
  14.4 1.8 %collective-permute-start.8 = (bf16[192,768]{1,0:T(8,128)(2,1)}, bf16[192,768]{1,0:T(8,128)(2,1)}, u32[]{:S(2)}, u32[]{:S(2)}) collective-permute-start(bf16[192,768]{1,0:T(8,128)(2,1)} %collective-permute-done.7.refs_1_), channel_id=1, source_target_pairs={{0,4},{1,5},{4,8},{5,9},{8,12},{9,13},{12,14},{13,15},{14,10},{15,... | collective-permute-start | bytes 884744 | tf_op jit(solution)/shard_map/ppermute | solution.py:375
  16.2 0.2 collective-permute-start.4
  16.5 0.7 compare_select_fusion
  17.2 0.6 gather_fusion
  17.8 5.6 %collective-permute-done.8.refs_3_ = bf16[192,768]{1,0:T(8,128)(2,1)} collective-permute-done((bf16[192,768]{1,0:T(8,128)(2,1)}, bf16[192,768]{1,0:T(8,128)(2,1)}, u32[]{:S(2)}, u32[]{:S(2)}) %collective-permute-start.8) | collective-permute-done | bytes 294944 | tf_op jit(solution)/shard_map/ppermute | solution.py:375
  23.4 1.6 %collective-permute-start.9 = (bf16[192,768]{1,0:T(8,128)(2,1)}, bf16[192,768]{1,0:T(8,128)(2,1)S(1)}, u32[]{:S(2)}, u32[]{:S(2)}) collective-permute-start(bf16[192,768]{1,0:T(8,128)(2,1)} %collective-permute-done.8.refs_3_), channel_id=1, source_target_pairs={{0,4},{1,5},{4,8},{5,9},{8,12},{9,13},{12,14},{13,15},{14,10},{15,... | collective-permute-start | bytes 884744 | tf_op jit(solution)/shard_map/ppermute | solution.py:375
  25.0 0.5 collective-permute-start.10
  25.5 1.9 %pad_maximum_fusion.refs_0_ = bf16[192,1280]{1,0:T(8,128)(2,1)} fusion(bf16[192,512]{1,0:T(8,128)(2,1)} %param.9, bf16[192,384]{1,0:T(8,128)(2,1)} %collective-permute-done.2, bf16[192,384]{1,0:T(8,128)(2,1)} %get-tuple-element.35), kind=kLoop, calls=%fused_computation.2 | loop fusion | flops 1474560 | bytes 983040 | tf_op jit(solution)/shard_map/concatenate | solution.py:420
  27.4 1.6 %collective-permute-start.5 = (bf16[192,1280]{1,0:T(8,128)(2,1)}, bf16[192,1280]{1,0:T(8,128)(2,1)}, u32[]{:S(2)}, u32[]{:S(2)}) collective-permute-start(bf16[192,1280]{1,0:T(8,128)(2,1)} %pad_maximum_fusion.refs_0_), channel_id=1, source_target_pairs={{0,4},{1,5},{4,8},{5,9},{8,12},{9,13},{12,14},{13,15},{14,10},{15,... | collective-permute-start | bytes 1474568 | tf_op jit(solution)/shard_map/ppermute | solution.py:375
  28.9 0.5 collective-permute-start.6
  29.5 4.1 %collective-permute-done.9.refs_5_ = bf16[192,768]{1,0:T(8,128)(2,1)S(1)} collective-permute-done((bf16[192,768]{1,0:T(8,128)(2,1)}, bf16[192,768]{1,0:T(8,128)(2,1)S(1)}, u32[]{:S(2)}, u32[]{:S(2)}) %collective-permute-start.9) | collective-permute-done | bytes 294944 | tf_op jit(solution)/shard_map/ppermute | solution.py:375
  33.6 1.7 %collective-permute-done.10.refs_6_ = bf16[192,768]{1,0:T(8,128)(2,1)} collective-permute-done((bf16[192,768]{1,0:T(8,128)(2,1)}, bf16[192,768]{1,0:T(8,128)(2,1)}, u32[]{:S(2)}, u32[]{:S(2)}) %collective-permute-start.10) | collective-permute-done | bytes 294944 | tf_op jit(solution)/shard_map/ppermute | solution.py:376
  35.3 1.6 %collective-permute-start.15 = (bf16[192,768]{1,0:T(8,128)(2,1)S(1)}, bf16[192,768]{1,0:T(8,128)(2,1)S(1)}, u32[]{:S(2)}, u32[]{:S(2)}) collective-permute-start(bf16[192,768]{1,0:T(8,128)(2,1)S(1)} %broadcast_select_fusion.1), channel_id=1, source_target_pairs={{0,4},{4,8},{8,12},{12,14},{14,10},{10,6},{6,2},{2,0},{5,1},{9,5},... | collective-permute-start | bytes 884744 | tf_op jit(solution)/shard_map/ppermute | solution.py:387
  36.9 1.0 copy-done.5
  37.9 5.8 %temporal_projection.1.most_ref = f32[1024,384]{1,0:T(8,128)S(1)} custom-call(s32[10]{0:T(128)S(1)} %pad_add_fusion.meta_ref, bf16[512,3072]{1,0:T(8,128)(2,1)S(1)} %bitcast.28, bf16[512,3072]{1,0:T(8,128)(2,1)} %collective-permute-done.1.other_ref, bf16[192,768]{1,0:T(8,128)(2,1)S(1)} %copy-done.5, bf16[192,768]{1,0:T(8,128)(2,1)} %collective-permute-done.7.refs_1_, ...), custom_call_target="tpu_custom_call" | custom-call | flops 2415919104 | bytes 8355880 | tf_op jit(solution)/shard_map/temporal_projection/pallas_call | solution.py:27
  43.7 2.0 %collective-permute-done.6.refs_2_ = bf16[192,1280]{1,0:T(8,128)(2,1)} collective-permute-done((bf16[192,1280]{1,0:T(8,128)(2,1)}, bf16[192,1280]{1,0:T(8,128)(2,1)}, u32[]{:S(2)}, u32[]{:S(2)}) %collective-permute-start.6) | collective-permute-done | bytes 491552 | tf_op jit(solution)/shard_map/ppermute | solution.py:376
  45.8 1.6 %collective-permute-start.11 = (bf16[192,1280]{1,0:T(8,128)(2,1)}, bf16[192,1280]{1,0:T(8,128)(2,1)}, u32[]{:S(2)}, u32[]{:S(2)}) collective-permute-start(bf16[192,1280]{1,0:T(8,128)(2,1)} %collective-permute-done.5.refs_1_), channel_id=1, source_target_pairs={{0,4},{1,5},{4,8},{5,9},{8,12},{9,13},{12,14},{13,15},{14,10},{15,... | collective-permute-start | bytes 1474568 | tf_op jit(solution)/shard_map/ppermute | solution.py:375
  47.4 0.4 collective-permute-start.12
  47.8 2.0 %temporal_projection_rest.1 = bf16[8,2,2,32,384]{4,3,2,1,0:T(8,128)(2,1)S(1)} custom-call(s32[10]{0:T(128)S(1)} %pad_add_fusion.meta_ref, bf16[512,3072]{1,0:T(8,128)(2,1)S(1)} %bitcast.29, bf16[512,3072]{1,0:T(8,128)(2,1)} %collective-permute-done.1.other_ref, f32[1024,384]{1,0:T(8,128)S(1)} %temporal_projection.1.most_ref, ...), custom_call_target="tpu_custom_call" | custom-call | flops 301989888 | bytes 8159272 | tf_op jit(solution)/shard_map/temporal_projection_rest/pallas_call | solution.py:27
  49.9 0.9 copy-done.3
  50.8 5.5 %all-to-all-start = ((bf16[8,2,2,32,384]{4,3,2,1,0:T(8,128)(2,1)}), bf16[8,2,2,32,384]{4,3,2,1,0:T(8,128)(2,1)}, u32[]{:S(2)}, u32[]{:S(2)}) async-start(bf16[8,2,2,32,384]{4,3,2,1,0:T(8,128)(2,1)} %copy-done.3), calls=%async_computation | async-start | bytes 1572864 | tf_op jit(solution)/shard_map/all_to_all | solution.py:485
  56.4 2.0 %collective-permute-start.13 = (bf16[192,1280]{1,0:T(8,128)(2,1)}, bf16[192,1280]{1,0:T(8,128)(2,1)}, u32[]{:S(2)}, u32[]{:S(2)}) collective-permute-start(bf16[192,1280]{1,0:T(8,128)(2,1)} %collective-permute-done.11.refs_3_.refs_0_), channel_id=1, source_target_pairs={{0,4},{1,5},{4,8},{5,9},{8,12},{9,13},{12,14},{13,15},{14,10},{15,... | collective-permute-start | bytes 1474568 | tf_op jit(solution)/shard_map/ppermute | solution.py:375
  58.4 0.2 collective-permute-start.14
  58.8 2.0 %pack_out_weight.4.refs_0_ = bf16[3,192,512]{2,1,0:T(8,128)(2,1)} custom-call(bf16[192,1280]{1,0:T(8,128)(2,1)} %pad_maximum_fusion.refs_0_, bf16[192,1280]{1,0:T(8,128)(2,1)} %collective-permute-done.5.refs_1_, bf16[192,1280]{1,0:T(8,128)(2,1)} %collective-permute-done.6.refs_2_), custom_call_target="tpu_custom_call" | custom-call | flops 1000000000 | bytes 1474560 | tf_op jit(solution)/shard_map/pack_out_weight/pallas_call | solution.py:27
  60.8 1.6 %collective-permute-start.16 = (bf16[3,192,512]{2,1,0:T(8,128)(2,1)}, bf16[3,192,512]{2,1,0:T(8,128)(2,1)}, u32[]{:S(2)}, u32[]{:S(2)}) collective-permute-start(bf16[3,192,512]{2,1,0:T(8,128)(2,1)} %pack_out_weight.4.refs_0_), channel_id=1, source_target_pairs={{0,16},{16,0},{1,17},{17,1},{2,18},{18,2},{3,19},{19,3},{4,20},{20... | collective-permute-start | bytes 1769480 | tf_op jit(solution)/shard_map/ppermute | solution.py:366
  62.4 1.8 %pack_out_weight.5.refs_1_ = bf16[2,192,512]{2,1,0:T(8,128)(2,1)} custom-call(bf16[192,1280]{1,0:T(8,128)(2,1)} %collective-permute-done.11.refs_3_.refs_0_, bf16[192,1280]{1,0:T(8,128)(2,1)} %collective-permute-done.12.refs_4_.refs_1_), custom_call_target="tpu_custom_call" | custom-call | flops 1000000000 | bytes 983040 | tf_op jit(solution)/shard_map/pack_out_weight/pallas_call | solution.py:27
  64.2 0.6 collective-permute-start.17
  64.8 7.1 %spatial_projection.1.most_ref = f32[1024,384]{1,0:T(8,128)S(1)} custom-call(s32[10]{0:T(128)S(1)} %pad_add_fusion.meta_ref, bf16[512,3072]{1,0:T(8,128)(2,1)S(1)} %bitcast.30, bf16[512,3072]{1,0:T(8,128)(2,1)} %collective-permute-done.1.other_ref, bf16[192,1280]{1,0:T(8,128)(2,1)} %pad_maximum_fusion.refs_0_, ...), custom_call_target="tpu_custom_call" | custom-call | bytes 8749096 | tf_op jit(solution)/shard_map/spatial_projection/pallas_call | solution.py:27
  71.9 1.1 copy-done.1
  73.0 4.9 %collective-permute-done.13.refs_0_ = bf16[192,1280]{1,0:T(8,128)(2,1)} collective-permute-done((bf16[192,1280]{1,0:T(8,128)(2,1)}, bf16[192,1280]{1,0:T(8,128)(2,1)}, u32[]{:S(2)}, u32[]{:S(2)}) %collective-permute-start.13) | collective-permute-done | bytes 491552 | tf_op jit(solution)/shard_map/ppermute | solution.py:375
  77.9 2.1 %collective-permute-done.14.refs_1_ = bf16[192,1280]{1,0:T(8,128)(2,1)} collective-permute-done((bf16[192,1280]{1,0:T(8,128)(2,1)}, bf16[192,1280]{1,0:T(8,128)(2,1)}, u32[]{:S(2)}, u32[]{:S(2)}) %collective-permute-start.14) | collective-permute-done | bytes 491552 | tf_op jit(solution)/shard_map/ppermute | solution.py:376
  80.0 1.9 %broadcast_select_fusion = bf16[192,1280]{1,0:T(8,128)(2,1)} fusion(bf16[192,1280]{1,0:T(8,128)(2,1)} %collective-permute-done.13.refs_0_, bf16[192,1280]{1,0:T(8,128)(2,1)} %collective-permute-done.14.refs_1_, pred[]{:T(512)S(6)} %eq.6), kind=kLoop, calls=%fused_computation.3 | loop fusion | flops 245760 | bytes 1474561 | tf_op jit(solution)/shard_map/jit(_where)/select_n | solution.py:381
  81.9 2.7 %temporal_attention.1 = bf16[2,16,32,128]{3,2,1,0:T(8,128)(2,1)} custom-call(s32[17]{0:T(128)S(1)} %pad_add_fusion.1.meta_ref, bf16[16,64,384]{2,1,0:T(8,128)(2,1)} %bitcast.9.qkv_ref), custom_call_target="tpu_custom_call" | custom-call | flops 5000000000 | bytes 786500 | tf_op jit(solution)/shard_map/temporal_attention/pallas_call | solution.py:27
  84.6 5.9 %collective-permute-start.18 = (bf16[192,1280]{1,0:T(8,128)(2,1)}, bf16[192,1280]{1,0:T(8,128)(2,1)}, u32[]{:S(2)}, u32[]{:S(2)}) collective-permute-start(bf16[192,1280]{1,0:T(8,128)(2,1)} %broadcast_select_fusion), channel_id=1, source_target_pairs={{0,4},{4,8},{8,12},{12,14},{14,10},{10,6},{6,2},{2,0},{5,1},{9,5},... | collective-permute-start | bytes 1474568 | tf_op jit(solution)/shard_map/ppermute | solution.py:387
  90.5 1.8 %pack_out_weight.6.refs_2_ = bf16[2,192,512]{2,1,0:T(8,128)(2,1)} custom-call(bf16[192,1280]{1,0:T(8,128)(2,1)} %collective-permute-done.13.refs_0_, bf16[192,1280]{1,0:T(8,128)(2,1)} %collective-permute-done.14.refs_1_), custom_call_target="tpu_custom_call" | custom-call | flops 1000000000 | bytes 983040 | tf_op jit(solution)/shard_map/pack_out_weight/pallas_call | solution.py:27
  92.3 1.6 %collective-permute-start.26 = (bf16[2,192,512]{2,1,0:T(8,128)(2,1)}, bf16[2,192,512]{2,1,0:T(8,128)(2,1)}, u32[]{:S(2)}, u32[]{:S(2)}) collective-permute-start(bf16[2,192,512]{2,1,0:T(8,128)(2,1)} %pack_out_weight.6.refs_2_), channel_id=1, source_target_pairs={{0,16},{16,0},{1,17},{17,1},{2,18},{18,2},{3,19},{19,3},{4,20},{20... | collective-permute-start | bytes 1179656 | tf_op jit(solution)/shard_map/ppermute | solution.py:366
  93.8 2.7 %all-to-all-start.1 = ((bf16[32,32,128]{2,1,0:T(8,128)(2,1)}), bf16[32,32,128]{2,1,0:T(8,128)(2,1)S(1)}, u32[]{:S(2)}, u32[]{:S(2)}) async-start(bf16[32,32,128]{2,1,0:T(8,128)(2,1)} %bitcast.14), calls=%async_computation.1 | async-start | bytes 524288 | tf_op jit(solution)/shard_map/all_to_all | solution.py:512
  96.5 0.6 collective-permute-done.18.refs_2_.refs_0_
  97.1 1.6 %pack_out_weight.7.refs_3_ = bf16[1,192,512]{2,1,0:T(8,128)(2,1)} custom-call(bf16[192,1280]{1,0:T(8,128)(2,1)} %collective-permute-done.18.refs_2_.refs_0_), custom_call_target="tpu_custom_call" | custom-call | flops 1000000000 | bytes 491520 | tf_op jit(solution)/shard_map/pack_out_weight/pallas_call | solution.py:27
  98.8 1.6 %collective-permute-start.27 = (bf16[1,192,512]{2,1,0:T(8,128)(2,1)}, bf16[1,192,512]{2,1,0:T(8,128)(2,1)}, u32[]{:S(2)}, u32[]{:S(2)}) collective-permute-start(bf16[1,192,512]{2,1,0:T(8,128)(2,1)} %pack_out_weight.7.refs_3_), channel_id=1, source_target_pairs={{0,16},{16,0},{1,17},{17,1},{2,18},{18,2},{3,19},{19,3},{4,20},{20... | collective-permute-start | bytes 589832 | tf_op jit(solution)/shard_map/ppermute | solution.py:366
  100.3 0.5 collective-permute-start.24
  100.8 1.4 %copy-done.2 = f32[1024,384]{1,0:T(8,128)S(1)} copy-done((f32[1024,384]{1,0:T(8,128)S(1)}, f32[1024,384]{1,0:T(8,128)}, u32[]{:S(2)}) %copy-start.2) | copy-done | bytes 1572888
  102.2 4.9 %spatial_heads.1 = bf16[2,2,256,128]{3,2,1,0:T(8,128)(2,1)S(1)} custom-call(s32[10]{0:T(128)S(1)} %pad_add_fusion.meta_ref, bf16[512,3072]{1,0:T(8,128)(2,1)S(1)} %bitcast.31, bf16[512,3072]{1,0:T(8,128)(2,1)} %collective-permute-done.1.other_ref, f32[1024,384]{1,0:T(8,128)S(1)} %copy-done.2, bf16[192,1280]{1,0:T(8,128)(2,1)} %collective-permute-done.13.refs_0_, ...), custom_call_target="tpu_custom_call" | custom-call | bytes 9338920 | tf_op jit(solution)/shard_map/spatial_heads/pallas_call | solution.py:27
  107.1 0.3 collective-permute-done.27.refs_11_
  107.5 0.7 slice_bitcast_fusion
  108.1 1.6 %collective-permute-start.21 = (bf16[256,128]{1,0:T(8,128)(2,1)S(1)}, bf16[256,128]{1,0:T(8,128)(2,1)S(1)}, u32[]{:S(2)}, u32[]{:S(2)}) collective-permute-start(bf16[256,128]{1,0:T(8,128)(2,1)S(1)} %get-tuple-element.39), channel_id=1, source_target_pairs={{0,17},{1,16},{2,19},{3,18},{4,21},{5,20},{6,23},{7,22},{8,25},{9,... | collective-permute-start | bytes 196616 | tf_op jit(solution)/shard_map/ppermute | solution.py:567
  109.7 0.6 collective-permute-start.19
  110.5 1.6 %collective-permute-done.21.far_ref = bf16[256,128]{1,0:T(8,128)(2,1)S(1)} collective-permute-done((bf16[256,128]{1,0:T(8,128)(2,1)S(1)}, bf16[256,128]{1,0:T(8,128)(2,1)S(1)}, u32[]{:S(2)}, u32[]{:S(2)}) %collective-permute-start.21) | collective-permute-done | bytes 65568 | tf_op jit(solution)/shard_map/ppermute | solution.py:567
  112.3 0.3 collective-permute-start.29
  112.6 1.6 %collective-permute-done.19.peer_ref = bf16[256,128]{1,0:T(8,128)(2,1)S(1)} collective-permute-done((bf16[256,128]{1,0:T(8,128)(2,1)S(1)}, bf16[256,128]{1,0:T(8,128)(2,1)S(1)}, u32[]{:S(2)}, u32[]{:S(2)}) %collective-permute-start.19) | collective-permute-done | bytes 65568 | tf_op jit(solution)/shard_map/ppermute | solution.py:366
  114.4 0.5 copy-done.19
  114.9 0.7 copy-done.6
  115.6 0.7 collective-permute-done.30.refs_14_
  116.4 0.6 copy-done.14
  117.2 6.9 %out_projection.1 = bf16[256,3072]{1,0:T(8,128)(2,1)} custom-call(s32[10]{0:T(128)} %copy-done.7, bf16[256,128]{1,0:T(8,128)(2,1)} %get-tuple-element.42.mine_ref, bf16[256,128]{1,0:T(8,128)(2,1)} %copy-done.19, bf16[256,128]{1,0:T(8,128)(2,1)} %copy-done.18, bf16[256,128]{1,0:T(8,128)(2,1)} %copy-done.17, bf16[2,256,256]{2,1,0:T(8,128)(2,1)} %copy-done.6, ...), custom_call_target="tpu_custom_call" | custom-call | flops 1610612736 | bytes 6815784 | tf_op jit(solution)/shard_map/out_projection/pallas_call | solution.py:27
  (78 shorter events, 1.5 us)
Async XLA Ops:
  0.0 3.7 %copy-start = (bf16[1,512,3072]{2,1,0:T(8,128)(2,1)S(1)}, bf16[1,512,3072]{2,1,0:T(8,128)(2,1)}, u32[]{:S(2)}) copy-start(bf16[1,512,3072]{2,1,0:T(8,128)(2,1)} %param.7) | copy-start | bytes 9437188
  0.0 6.9 %copy-start.21 = (s32[8]{0:T(128)S(1)}, s32[8]{0:T(128)}, u32[]{:S(2)}) copy-start(s32[8]{0:T(128)} %constant.67.clone) | copy-start | bytes 100
  1.3 15.9 %copy-start.8 = (s32[8]{0:T(128)S(1)}, s32[8]{0:T(128)}, u32[]{:S(2)}) copy-start(s32[8]{0:T(128)} %constant.68.clone) | copy-start | bytes 100
  2.1 1.5 %collective-permute-start = (bf16[192,384]{1,0:T(8,128)(2,1)S(1)}, bf16[192,384]{1,0:T(8,128)(2,1)S(1)}, u32[]{:S(2)}, u32[]{:S(2)}) collective-permute-start(bf16[192,384]{1,0:T(8,128)(2,1)S(1)} %get-tuple-element.38), channel_id=1, source_target_pairs={{0,1},{1,0},{2,3},{3,2},{4,5},{5,4},{6,7},{7,6},{8,9},{9,8},{10,11... | collective-permute-start | bytes 442376 | tf_op jit(solution)/shard_map/ppermute | solution.py:363
  3.7 14.2 %copy-start.4 = (bf16[192,768]{1,0:T(8,128)(2,1)}, bf16[192,768]{1,0:T(8,128)(2,1)S(1)}, u32[]{:S(2)}) copy-start(bf16[192,768]{1,0:T(8,128)(2,1)S(1)} %pad_maximum_fusion.1.refs_0_) | copy-start | bytes 884740
  3.7 33.2 %collective-permute-start.1 = (bf16[512,3072]{1,0:T(8,128)(2,1)S(1)}, bf16[512,3072]{1,0:T(8,128)(2,1)}, u32[]{:S(2)}, u32[]{:S(2)}) collective-permute-start(bf16[512,3072]{1,0:T(8,128)(2,1)S(1)} %bitcast.27), channel_id=1, source_target_pairs={{0,1},{1,0},{2,3},{3,2},{4,5},{5,4},{6,7},{7,6},{8,9},{9,8},{10,11... | collective-permute-start | bytes 9437192 | tf_op jit(solution)/shard_map/ppermute | solution.py:363
  4.1 10.3 %collective-permute-start.7 = (bf16[192,768]{1,0:T(8,128)(2,1)S(1)}, bf16[192,768]{1,0:T(8,128)(2,1)}, u32[]{:S(2)}, u32[]{:S(2)}) collective-permute-start(bf16[192,768]{1,0:T(8,128)(2,1)S(1)} %pad_maximum_fusion.1.refs_0_), channel_id=1, source_target_pairs={{0,4},{1,5},{4,8},{5,9},{8,12},{9,13},{12,14},{13,15},{14,10},{15,... | collective-permute-start | bytes 884744 | tf_op jit(solution)/shard_map/ppermute | solution.py:375
  6.9 9.4 %collective-permute-start.3 = (bf16[192,768]{1,0:T(8,128)(2,1)S(1)}, bf16[192,768]{1,0:T(8,128)(2,1)}, u32[]{:S(2)}, u32[]{:S(2)}) collective-permute-start(bf16[192,768]{1,0:T(8,128)(2,1)S(1)} %pad_maximum_fusion.1.refs_0_), channel_id=1, source_target_pairs={{4,0},{5,1},{8,4},{9,5},{12,8},{13,9},{14,12},{15,13},{10,14},{11,... | collective-permute-start | bytes 884744 | tf_op jit(solution)/shard_map/ppermute | solution.py:376
  9.3 16.2 %collective-permute-start.2 = (bf16[192,384]{1,0:T(8,128)(2,1)}, bf16[192,384]{1,0:T(8,128)(2,1)}, u32[]{:S(2)}, u32[]{:S(2)}) collective-permute-start(bf16[192,384]{1,0:T(8,128)(2,1)} %get-tuple-element.36), channel_id=1, source_target_pairs={{0,1},{1,0},{2,3},{3,2},{4,5},{5,4},{6,7},{7,6},{8,9},{9,8},{10,11... | collective-permute-start | bytes 442376 | tf_op jit(solution)/shard_map/ppermute | solution.py:363
  14.4 9.0 %collective-permute-start.8 = (bf16[192,768]{1,0:T(8,128)(2,1)}, bf16[192,768]{1,0:T(8,128)(2,1)}, u32[]{:S(2)}, u32[]{:S(2)}) collective-permute-start(bf16[192,768]{1,0:T(8,128)(2,1)} %collective-permute-done.7.refs_1_), channel_id=1, source_target_pairs={{0,4},{1,5},{4,8},{5,9},{8,12},{9,13},{12,14},{13,15},{14,10},{15,... | collective-permute-start | bytes 884744 | tf_op jit(solution)/shard_map/ppermute | solution.py:375
  16.2 8.8 %collective-permute-start.4 = (bf16[192,768]{1,0:T(8,128)(2,1)}, bf16[192,768]{1,0:T(8,128)(2,1)}, u32[]{:S(2)}, u32[]{:S(2)}) collective-permute-start(bf16[192,768]{1,0:T(8,128)(2,1)} %collective-permute-done.3.refs_2_), channel_id=1, source_target_pairs={{4,0},{5,1},{8,4},{9,5},{12,8},{13,9},{14,12},{15,13},{10,14},{11,... | collective-permute-start | bytes 884744 | tf_op jit(solution)/shard_map/ppermute | solution.py:376
  23.4 10.2 %collective-permute-start.9 = (bf16[192,768]{1,0:T(8,128)(2,1)}, bf16[192,768]{1,0:T(8,128)(2,1)S(1)}, u32[]{:S(2)}, u32[]{:S(2)}) collective-permute-start(bf16[192,768]{1,0:T(8,128)(2,1)} %collective-permute-done.8.refs_3_), channel_id=1, source_target_pairs={{0,4},{1,5},{4,8},{5,9},{8,12},{9,13},{12,14},{13,15},{14,10},{15,... | collective-permute-start | bytes 884744 | tf_op jit(solution)/shard_map/ppermute | solution.py:375
  25.0 10.3 %collective-permute-start.10 = (bf16[192,768]{1,0:T(8,128)(2,1)}, bf16[192,768]{1,0:T(8,128)(2,1)}, u32[]{:S(2)}, u32[]{:S(2)}) collective-permute-start(bf16[192,768]{1,0:T(8,128)(2,1)} %collective-permute-done.4.refs_4_), channel_id=1, source_target_pairs={{4,0},{5,1},{8,4},{9,5},{12,8},{13,9},{14,12},{15,13},{10,14},{11,... | collective-permute-start | bytes 884744 | tf_op jit(solution)/shard_map/ppermute | solution.py:376
  27.4 16.4 %collective-permute-start.5 = (bf16[192,1280]{1,0:T(8,128)(2,1)}, bf16[192,1280]{1,0:T(8,128)(2,1)}, u32[]{:S(2)}, u32[]{:S(2)}) collective-permute-start(bf16[192,1280]{1,0:T(8,128)(2,1)} %pad_maximum_fusion.refs_0_), channel_id=1, source_target_pairs={{0,4},{1,5},{4,8},{5,9},{8,12},{9,13},{12,14},{13,15},{14,10},{15,... | collective-permute-start | bytes 1474568 | tf_op jit(solution)/shard_map/ppermute | solution.py:375
  28.9 16.9 %collective-permute-start.6 = (bf16[192,1280]{1,0:T(8,128)(2,1)}, bf16[192,1280]{1,0:T(8,128)(2,1)}, u32[]{:S(2)}, u32[]{:S(2)}) collective-permute-start(bf16[192,1280]{1,0:T(8,128)(2,1)} %pad_maximum_fusion.refs_0_), channel_id=1, source_target_pairs={{4,0},{5,1},{8,4},{9,5},{12,8},{13,9},{14,12},{15,13},{10,14},{11,... | collective-permute-start | bytes 1474568 | tf_op jit(solution)/shard_map/ppermute | solution.py:376
  29.5 71.4 %copy-start.7 = (s32[10]{0:T(128)}, s32[10]{0:T(128)S(1)}, u32[]{:S(2)}) copy-start(s32[10]{0:T(128)S(1)} %pad_add_fusion.meta_ref) | copy-start | bytes 124
  35.3 12.5 %collective-permute-start.15 = (bf16[192,768]{1,0:T(8,128)(2,1)S(1)}, bf16[192,768]{1,0:T(8,128)(2,1)S(1)}, u32[]{:S(2)}, u32[]{:S(2)}) collective-permute-start(bf16[192,768]{1,0:T(8,128)(2,1)S(1)} %broadcast_select_fusion.1), channel_id=1, source_target_pairs={{0,4},{4,8},{8,12},{12,14},{14,10},{10,6},{6,2},{2,0},{5,1},{9,5},... | collective-permute-start | bytes 884744 | tf_op jit(solution)/shard_map/ppermute | solution.py:387
  36.9 1.0 copy-start.5
  45.8 10.6 %collective-permute-start.11 = (bf16[192,1280]{1,0:T(8,128)(2,1)}, bf16[192,1280]{1,0:T(8,128)(2,1)}, u32[]{:S(2)}, u32[]{:S(2)}) collective-permute-start(bf16[192,1280]{1,0:T(8,128)(2,1)} %collective-permute-done.5.refs_1_), channel_id=1, source_target_pairs={{0,4},{1,5},{4,8},{5,9},{8,12},{9,13},{12,14},{13,15},{14,10},{15,... | collective-permute-start | bytes 1474568 | tf_op jit(solution)/shard_map/ppermute | solution.py:375
  47.4 11.1 %collective-permute-start.12 = (bf16[192,1280]{1,0:T(8,128)(2,1)}, bf16[192,1280]{1,0:T(8,128)(2,1)}, u32[]{:S(2)}, u32[]{:S(2)}) collective-permute-start(bf16[192,1280]{1,0:T(8,128)(2,1)} %collective-permute-done.6.refs_2_), channel_id=1, source_target_pairs={{4,0},{5,1},{8,4},{9,5},{12,8},{13,9},{14,12},{15,13},{10,14},{11,... | collective-permute-start | bytes 1474568 | tf_op jit(solution)/shard_map/ppermute | solution.py:376
  49.9 0.9 copy-start.3
  50.8 5.5 %copy-start.20 = (s32[16]{0:T(128)S(1)}, s32[16]{0:T(128)}, u32[]{:S(2)}) copy-start(s32[16]{0:T(128)} %param.10) | copy-start | bytes 196
  50.8 31.2 %all-to-all-start = ((bf16[8,2,2,32,384]{4,3,2,1,0:T(8,128)(2,1)}), bf16[8,2,2,32,384]{4,3,2,1,0:T(8,128)(2,1)}, u32[]{:S(2)}, u32[]{:S(2)}) async-start(bf16[8,2,2,32,384]{4,3,2,1,0:T(8,128)(2,1)} %copy-done.3), calls=%async_computation | async-start | bytes 1572864 | tf_op jit(solution)/shard_map/all_to_all | solution.py:485
  56.4 21.5 %collective-permute-start.13 = (bf16[192,1280]{1,0:T(8,128)(2,1)}, bf16[192,1280]{1,0:T(8,128)(2,1)}, u32[]{:S(2)}, u32[]{:S(2)}) collective-permute-start(bf16[192,1280]{1,0:T(8,128)(2,1)} %collective-permute-done.11.refs_3_.refs_0_), channel_id=1, source_target_pairs={{0,4},{1,5},{4,8},{5,9},{8,12},{9,13},{12,14},{13,15},{14,10},{15,... | collective-permute-start | bytes 1474568 | tf_op jit(solution)/shard_map/ppermute | solution.py:375
  58.4 21.6 %collective-permute-start.14 = (bf16[192,1280]{1,0:T(8,128)(2,1)}, bf16[192,1280]{1,0:T(8,128)(2,1)}, u32[]{:S(2)}, u32[]{:S(2)}) collective-permute-start(bf16[192,1280]{1,0:T(8,128)(2,1)} %collective-permute-done.12.refs_4_.refs_1_), channel_id=1, source_target_pairs={{4,0},{5,1},{8,4},{9,5},{12,8},{13,9},{14,12},{15,13},{10,14},{11,... | collective-permute-start | bytes 1474568 | tf_op jit(solution)/shard_map/ppermute | solution.py:376
  60.8 23.8 %collective-permute-start.16 = (bf16[3,192,512]{2,1,0:T(8,128)(2,1)}, bf16[3,192,512]{2,1,0:T(8,128)(2,1)}, u32[]{:S(2)}, u32[]{:S(2)}) collective-permute-start(bf16[3,192,512]{2,1,0:T(8,128)(2,1)} %pack_out_weight.4.refs_0_), channel_id=1, source_target_pairs={{0,16},{16,0},{1,17},{17,1},{2,18},{18,2},{3,19},{19,3},{4,20},{20... | collective-permute-start | bytes 1769480 | tf_op jit(solution)/shard_map/ppermute | solution.py:366
  64.2 20.4 %collective-permute-start.17 = (bf16[2,192,512]{2,1,0:T(8,128)(2,1)}, bf16[2,192,512]{2,1,0:T(8,128)(2,1)}, u32[]{:S(2)}, u32[]{:S(2)}) collective-permute-start(bf16[2,192,512]{2,1,0:T(8,128)(2,1)} %pack_out_weight.5.refs_1_), channel_id=1, source_target_pairs={{0,16},{16,0},{1,17},{17,1},{2,18},{18,2},{3,19},{19,3},{4,20},{20... | collective-permute-start | bytes 1179656 | tf_op jit(solution)/shard_map/ppermute | solution.py:366
  71.8 1.1 copy-start.1
  84.6 12.6 %collective-permute-start.18 = (bf16[192,1280]{1,0:T(8,128)(2,1)}, bf16[192,1280]{1,0:T(8,128)(2,1)}, u32[]{:S(2)}, u32[]{:S(2)}) collective-permute-start(bf16[192,1280]{1,0:T(8,128)(2,1)} %broadcast_select_fusion), channel_id=1, source_target_pairs={{0,4},{4,8},{8,12},{12,14},{14,10},{10,6},{6,2},{2,0},{5,1},{9,5},... | collective-permute-start | bytes 1474568 | tf_op jit(solution)/shard_map/ppermute | solution.py:387
  92.3 14.9 %collective-permute-start.26 = (bf16[2,192,512]{2,1,0:T(8,128)(2,1)}, bf16[2,192,512]{2,1,0:T(8,128)(2,1)}, u32[]{:S(2)}, u32[]{:S(2)}) collective-permute-start(bf16[2,192,512]{2,1,0:T(8,128)(2,1)} %pack_out_weight.6.refs_2_), channel_id=1, source_target_pairs={{0,16},{16,0},{1,17},{17,1},{2,18},{18,2},{3,19},{19,3},{4,20},{20... | collective-permute-start | bytes 1179656 | tf_op jit(solution)/shard_map/ppermute | solution.py:366
  93.8 15.9 %collective-permute-start.22 = (bf16[3,192,512]{2,1,0:T(8,128)(2,1)}, bf16[3,192,512]{2,1,0:T(8,128)(2,1)}, u32[]{:S(2)}, u32[]{:S(2)}) collective-permute-start(bf16[3,192,512]{2,1,0:T(8,128)(2,1)} %pack_out_weight.4.refs_0_), channel_id=1, source_target_pairs={{0,1},{1,0},{2,3},{3,2},{4,5},{5,4},{6,7},{7,6},{8,9},{9,8},{10,11... | collective-permute-start | bytes 1769480 | tf_op jit(solution)/shard_map/ppermute | solution.py:363
  93.8 20.5 %all-to-all-start.1 = ((bf16[32,32,128]{2,1,0:T(8,128)(2,1)}), bf16[32,32,128]{2,1,0:T(8,128)(2,1)S(1)}, u32[]{:S(2)}, u32[]{:S(2)}) async-start(bf16[32,32,128]{2,1,0:T(8,128)(2,1)} %bitcast.14), calls=%async_computation.1 | async-start | bytes 524288 | tf_op jit(solution)/shard_map/all_to_all | solution.py:512
  96.5 3.8 %copy-start.10 = (bf16[2,192,512]{2,1,0:T(8,128)(2,1)S(1)}, bf16[2,192,512]{2,1,0:T(8,128)(2,1)}, u32[]{:S(2)}) copy-start(bf16[2,192,512]{2,1,0:T(8,128)(2,1)} %pack_out_weight.5.refs_1_) | copy-start | bytes 1179652
  98.8 8.7 %collective-permute-start.27 = (bf16[1,192,512]{2,1,0:T(8,128)(2,1)}, bf16[1,192,512]{2,1,0:T(8,128)(2,1)}, u32[]{:S(2)}, u32[]{:S(2)}) collective-permute-start(bf16[1,192,512]{2,1,0:T(8,128)(2,1)} %pack_out_weight.7.refs_3_), channel_id=1, source_target_pairs={{0,16},{16,0},{1,17},{17,1},{2,18},{18,2},{3,19},{19,3},{4,20},{20... | collective-permute-start | bytes 589832 | tf_op jit(solution)/shard_map/ppermute | solution.py:366
  100.3 9.4 %collective-permute-start.23 = (bf16[2,192,512]{2,1,0:T(8,128)(2,1)S(1)}, bf16[2,192,512]{2,1,0:T(8,128)(2,1)S(1)}, u32[]{:S(2)}, u32[]{:S(2)}) collective-permute-start(bf16[2,192,512]{2,1,0:T(8,128)(2,1)S(1)} %copy-done.10), channel_id=1, source_target_pairs={{0,1},{1,0},{2,3},{3,2},{4,5},{5,4},{6,7},{7,6},{8,9},{9,8},{10,11... | collective-permute-start | bytes 1179656 | tf_op jit(solution)/shard_map/ppermute | solution.py:363
  100.3 10.0 %collective-permute-start.24 = (bf16[2,192,512]{2,1,0:T(8,128)(2,1)}, bf16[2,192,512]{2,1,0:T(8,128)(2,1)S(1)}, u32[]{:S(2)}, u32[]{:S(2)}) collective-permute-start(bf16[2,192,512]{2,1,0:T(8,128)(2,1)} %pack_out_weight.6.refs_2_), channel_id=1, source_target_pairs={{0,1},{1,0},{2,3},{3,2},{4,5},{5,4},{6,7},{7,6},{8,9},{9,8},{10,11... | collective-permute-start | bytes 1179656 | tf_op jit(solution)/shard_map/ppermute | solution.py:363
  100.8 1.4 %copy-start.2 = (f32[1024,384]{1,0:T(8,128)S(1)}, f32[1024,384]{1,0:T(8,128)}, u32[]{:S(2)}) copy-start(f32[1024,384]{1,0:T(8,128)} %copy-done.1) | copy-start | bytes 4718596
  107.5 8.8 %collective-permute-start.28 = (bf16[3,192,512]{2,1,0:T(8,128)(2,1)}, bf16[3,192,512]{2,1,0:T(8,128)(2,1)S(1)}, u32[]{:S(2)}, u32[]{:S(2)}) collective-permute-start(bf16[3,192,512]{2,1,0:T(8,128)(2,1)} %collective-permute-done.16.refs_8_), channel_id=1, source_target_pairs={{0,1},{1,0},{2,3},{3,2},{4,5},{5,4},{6,7},{7,6},{8,9},{9,8},{10,11... | collective-permute-start | bytes 1769480 | tf_op jit(solution)/shard_map/ppermute | solution.py:363
  108.1 4.0 %collective-permute-start.21 = (bf16[256,128]{1,0:T(8,128)(2,1)S(1)}, bf16[256,128]{1,0:T(8,128)(2,1)S(1)}, u32[]{:S(2)}, u32[]{:S(2)}) collective-permute-start(bf16[256,128]{1,0:T(8,128)(2,1)S(1)} %get-tuple-element.39), channel_id=1, source_target_pairs={{0,17},{1,16},{2,19},{3,18},{4,21},{5,20},{6,23},{7,22},{8,25},{9,... | collective-permute-start | bytes 196616 | tf_op jit(solution)/shard_map/ppermute | solution.py:567
  109.7 2.6 %collective-permute-start.20 = (bf16[256,128]{1,0:T(8,128)(2,1)S(1)}, bf16[256,128]{1,0:T(8,128)(2,1)S(1)}, u32[]{:S(2)}, u32[]{:S(2)}) collective-permute-start(bf16[256,128]{1,0:T(8,128)(2,1)S(1)} %get-tuple-element.40), channel_id=1, source_target_pairs={{0,1},{1,0},{2,3},{3,2},{4,5},{5,4},{6,7},{7,6},{8,9},{9,8},{10,11... | collective-permute-start | bytes 196616 | tf_op jit(solution)/shard_map/ppermute | solution.py:363
  109.7 4.5 %copy-start.11 = (bf16[2,192,512]{2,1,0:T(8,128)(2,1)}, bf16[2,192,512]{2,1,0:T(8,128)(2,1)S(1)}, u32[]{:S(2)}) copy-start(bf16[2,192,512]{2,1,0:T(8,128)(2,1)S(1)} %collective-permute-done.23.refs_5_) | copy-start | bytes 1179652
  109.7 4.5 %collective-permute-start.19 = (bf16[256,128]{1,0:T(8,128)(2,1)S(1)}, bf16[256,128]{1,0:T(8,128)(2,1)S(1)}, u32[]{:S(2)}, u32[]{:S(2)}) collective-permute-start(bf16[256,128]{1,0:T(8,128)(2,1)S(1)} %get-tuple-element.41), channel_id=1, source_target_pairs={{0,16},{16,0},{1,17},{17,1},{2,18},{18,2},{3,19},{19,3},{4,20},{20... | collective-permute-start | bytes 196616 | tf_op jit(solution)/shard_map/ppermute | solution.py:366
  110.3 3.9 %copy-start.12 = (bf16[2,192,512]{2,1,0:T(8,128)(2,1)}, bf16[2,192,512]{2,1,0:T(8,128)(2,1)S(1)}, u32[]{:S(2)}) copy-start(bf16[2,192,512]{2,1,0:T(8,128)(2,1)S(1)} %collective-permute-done.24.refs_6_) | copy-start | bytes 1179652
  110.3 5.2 %collective-permute-start.25 = (bf16[1,192,512]{2,1,0:T(8,128)(2,1)}, bf16[1,192,512]{2,1,0:T(8,128)(2,1)S(1)}, u32[]{:S(2)}, u32[]{:S(2)}) collective-permute-start(bf16[1,192,512]{2,1,0:T(8,128)(2,1)} %pack_out_weight.7.refs_3_), channel_id=1, source_target_pairs={{0,1},{1,0},{2,3},{3,2},{4,5},{5,4},{6,7},{7,6},{8,9},{9,8},{10,11... | collective-permute-start | bytes 589832 | tf_op jit(solution)/shard_map/ppermute | solution.py:363
  112.1 2.3 %copy-start.17 = (bf16[256,128]{1,0:T(8,128)(2,1)}, bf16[256,128]{1,0:T(8,128)(2,1)S(1)}, u32[]{:S(2)}) copy-start(bf16[256,128]{1,0:T(8,128)(2,1)S(1)} %collective-permute-done.21.far_ref) | copy-start | bytes 196612
  112.1 3.4 %collective-permute-start.31 = (bf16[1,192,512]{2,1,0:T(8,128)(2,1)}, bf16[1,192,512]{2,1,0:T(8,128)(2,1)S(1)}, u32[]{:S(2)}, u32[]{:S(2)}) collective-permute-start(bf16[1,192,512]{2,1,0:T(8,128)(2,1)} %collective-permute-done.27.refs_11_), channel_id=1, source_target_pairs={{0,1},{1,0},{2,3},{3,2},{4,5},{5,4},{6,7},{7,6},{8,9},{9,8},{10,11... | collective-permute-start | bytes 589832 | tf_op jit(solution)/shard_map/ppermute | solution.py:363
  112.3 2.1 %copy-start.18 = (bf16[256,128]{1,0:T(8,128)(2,1)}, bf16[256,128]{1,0:T(8,128)(2,1)S(1)}, u32[]{:S(2)}) copy-start(bf16[256,128]{1,0:T(8,128)(2,1)S(1)} %collective-permute-done.20.core_ref) | copy-start | bytes 196612
  112.3 3.2 %collective-permute-start.29 = (bf16[2,192,512]{2,1,0:T(8,128)(2,1)}, bf16[2,192,512]{2,1,0:T(8,128)(2,1)S(1)}, u32[]{:S(2)}, u32[]{:S(2)}) collective-permute-start(bf16[2,192,512]{2,1,0:T(8,128)(2,1)} %collective-permute-done.17.refs_9_), channel_id=1, source_target_pairs={{0,1},{1,0},{2,3},{3,2},{4,5},{5,4},{6,7},{7,6},{8,9},{9,8},{10,11... | collective-permute-start | bytes 1179656 | tf_op jit(solution)/shard_map/ppermute | solution.py:363
  114.2 0.6 copy-start.19
  114.3 2.0 %collective-permute-start.30 = (bf16[2,192,512]{2,1,0:T(8,128)(2,1)}, bf16[2,192,512]{2,1,0:T(8,128)(2,1)S(1)}, u32[]{:S(2)}, u32[]{:S(2)}) collective-permute-start(bf16[2,192,512]{2,1,0:T(8,128)(2,1)} %collective-permute-done.26.refs_10_), channel_id=1, source_target_pairs={{0,1},{1,0},{2,3},{3,2},{4,5},{5,4},{6,7},{7,6},{8,9},{9,8},{10,11... | collective-permute-start | bytes 1179656 | tf_op jit(solution)/shard_map/ppermute | solution.py:363
  114.9 0.7 copy-start.6
  115.6 0.7 copy-start.15
  115.6 0.7 copy-start.16
  115.6 0.9 copy-start.13
  116.2 0.8 copy-start.14
  116.3 0.9 copy-start.9

commit v6 on v5

--- a/solution.py
+++ b/solution.py
@@ -11,6 +11,7 @@
 HEAD = 128
 HS_DEV = 2
 SCALE = 1.0 / math.sqrt(HEAD)
+SCALE_LOG2 = SCALE * math.log2(math.e)
 MIB = 1024 * 1024
 LEADS = 5_000_000_000
 PACKS = 1_000_000_000
@@ -200,8 +201,7 @@
                 (((1,), (1,)), ((), ())),
                 preferred_element_type=jnp.float32,
             )
-            scores = scores * SCALE
-            expo = jnp.exp(scores - jnp.max(scores, axis=-1, keepdims=True))
+            expo = jnp.exp2((scores - jnp.max(scores, axis=-1, keepdims=True)) * SCALE_LOG2)
             total = jnp.sum(expo, axis=-1, keepdims=True)
             result = jnp.dot(
                 expo.astype(jnp.bfloat16),
@@ -285,7 +285,7 @@
 def out_body(
     depth, count, meta_ref, mine_ref, peer_ref, core_ref, far_ref, temporal_ref, *refs
 ):
-    *weight_refs, out_ref, heads, weight, sems = refs
+    *weight_refs, out_ref, heads, weight, sems, result, out_sems = refs
     core, st = meta_ref[0], meta_ref[1]
     n_st, chips = temporal_ref.shape[0], out_ref.shape[1] // (2 * depth)
     copies = [[] for _ in range(chips)]
@@ -323,6 +323,7 @@
                         (HS_DEV + k) * HEAD : (HS_DEV + k + 1) * HEAD,
                     ] = temporal_ref[group, chip, k]
     chip_width = 2 * depth
+    out_copies = []
     for slot in range(chips):
         for copy in copies[slot]:
             copy.wait()
@@ -335,7 +336,15 @@
                 preferred_element_type=jnp.float32,
             )
         at = pl.multiple_of(meta_ref[2 + slot] * chip_width, chip_width)
-        out_ref[:, pl.ds(at, chip_width)] = total.astype(jnp.bfloat16)
+        result[slot] = total.astype(jnp.bfloat16)
+        out_copies.append(
+            pltpu.make_async_copy(
+                result.at[slot], out_ref.at[:, pl.ds(at, chip_width)], out_sems.at[slot]
+            )
+        )
+        out_copies[-1].start()
+    for copy in out_copies:
+        copy.wait()
 
 
 def shards(n_st, n_fsdp, normed, qkv_weight, out_weight, segment_ids):
@@ -584,8 +593,11 @@
                 pltpu.VMEM((n_st, rows, out_weight.shape[1]), jnp.bfloat16),
                 pltpu.VMEM((n_st, chips, 2, depth, out_weight.shape[1]), jnp.bfloat16),
                 pltpu.SemaphoreType.DMA((count, 4)),
+                pltpu.VMEM((chips, rows, 2 * depth), jnp.bfloat16),
+                pltpu.SemaphoreType.DMA((chips,)),
             ],
             limit=60 * MIB,
+            out_space=pl.ANY,
         )
         return attended.reshape(1, rows, width)
 

time: 125 us -> 125 us (level)
  no operation moved by 1% of the time
where the time goes in v6:
time: 125 us; the launch traced here: 124 us
  starting transfers between devices  38.5 us (31%)
  Pallas kernels  36.2 us (29%)
  waiting for transfers between devices  31.5 us (25%)
  local copies, waits for them, and re-layouts  12.6 us (10%)
  other arithmetic  4.7 us (4%)
    pallas_call x11, Pallas kernels, kernel_call(): pl.pallas_call(body, out_shape=out_shape, in_specs=[pl.BlockSpec(memory_s...  36.2 us
    ppermute x6, waiting for transfers between devices, ring_gather(): ahead = lax.ppermute(ahead, 'fsdp', forward)  19.8 us
    ppermute x6, starting transfers between devices, ring_gather(): ahead = lax.ppermute(ahead, 'fsdp', forward)  11.2 us
    unnamed x45, local copies, waits for them, and re-layouts  7.83 us
    ppermute x2, starting transfers between devices, ring_gather(): yield (pieces + [lax.ppermute(sent, 'fsdp', both)], None)  7.52 us
    ppermute x5, starting transfers between devices, to_peer(): return lax.ppermute(x, 'st', [(0, 1), (1, 0)])  5.87 us
    ppermute x6, waiting for transfers between devices, ring_gather(): behind = lax.ppermute(behind, 'fsdp', backward)  5.84 us
    all_to_all x1, starting transfers between devices, shards(): lax.all_to_all(temporal, 'fsdp', split_axis=0, concat_axis=0, tiled=True,...  5.47 us
  transfers between devices with their start and end apart: 34, of which 13 were waited for; matrix products, arithmetic and copies ran while one was open for 7% of the time, Pallas kernels for 24%

profile of v6, /device:TPU:0, one launch (start us, length us, event | category | flops | bytes accessed | tf_op | source)
XLA Modules:
  0.0 123.9 jit_solution(17372914601344336427)
XLA Ops:
  0.0 1.3 %copy.10 = bf16[192,4,384]{2,0,1:T(8,128)(2,1)S(1)} copy(bf16[192,4,384]{2,1,0:T(4,128)(2,1)} %param.8) | data formatting | bytes 1179648 | tf_op args[1]
  1.3 0.8 fusion.1
  2.1 0.5 collective-permute-start
  2.6 1.0 collective-permute-done
  3.7 0.4 collective-permute-start.1
  4.1 2.7 %collective-permute-start.7 = (bf16[192,768]{1,0:T(8,128)(2,1)S(1)}, bf16[192,768]{1,0:T(8,128)(2,1)}, u32[]{:S(2)}, u32[]{:S(2)}) collective-permute-start(bf16[192,768]{1,0:T(8,128)(2,1)S(1)} %pad_maximum_fusion.1.refs_0_), channel_id=1, source_target_pairs={{0,4},{1,5},{4,8},{5,9},{8,12},{9,13},{12,14},{13,15},{14,10},{15,... | collective-permute-start | bytes 884744 | tf_op jit(solution)/shard_map/ppermute | solution.py:384
  6.9 0.7 dynamic_slice.16
  7.5 1.7 %dynamic-slice_bitcast_fusion.1 = (bf16[192,384]{1,0:T(8,128)(2,1)}, bf16[192,384]{1,0:T(8,128)(2,1)}) fusion(bf16[2,192,384]{2,1,0:T(8,128)(2,1)} %get-tuple-element.20, s32[]{:T(128)S(6)} %select_n.61, s32[]{:T(128)S(6)} %select_n.62), kind=kLoop, calls=%fused_computation.7 | loop fusion | bytes 589832 | tf_op jit(solution)/shard_map/jit(dynamic_index_in_dim)/squeeze | solution.py:414
  9.3 5.1 %collective-permute-done.7.refs_1_ = bf16[192,768]{1,0:T(8,128)(2,1)} collective-permute-done((bf16[192,768]{1,0:T(8,128)(2,1)S(1)}, bf16[192,768]{1,0:T(8,128)(2,1)}, u32[]{:S(2)}, u32[]{:S(2)}) %collective-permute-start.7) | collective-permute-done | bytes 294944 | tf_op jit(solution)/shard_map/ppermute | solution.py:384
  14.4 1.8 %collective-permute-start.8 = (bf16[192,768]{1,0:T(8,128)(2,1)}, bf16[192,768]{1,0:T(8,128)(2,1)}, u32[]{:S(2)}, u32[]{:S(2)}) collective-permute-start(bf16[192,768]{1,0:T(8,128)(2,1)} %collective-permute-done.7.refs_1_), channel_id=1, source_target_pairs={{0,4},{1,5},{4,8},{5,9},{8,12},{9,13},{12,14},{13,15},{14,10},{15,... | collective-permute-start | bytes 884744 | tf_op jit(solution)/shard_map/ppermute | solution.py:384
  16.2 0.2 collective-permute-start.4
  16.5 0.7 compare_select_fusion
  17.2 0.6 gather_fusion
  17.8 5.6 %collective-permute-done.8.refs_3_ = bf16[192,768]{1,0:T(8,128)(2,1)} collective-permute-done((bf16[192,768]{1,0:T(8,128)(2,1)}, bf16[192,768]{1,0:T(8,128)(2,1)}, u32[]{:S(2)}, u32[]{:S(2)}) %collective-permute-start.8) | collective-permute-done | bytes 294944 | tf_op jit(solution)/shard_map/ppermute | solution.py:384
  23.4 1.6 %collective-permute-start.9 = (bf16[192,768]{1,0:T(8,128)(2,1)}, bf16[192,768]{1,0:T(8,128)(2,1)S(1)}, u32[]{:S(2)}, u32[]{:S(2)}) collective-permute-start(bf16[192,768]{1,0:T(8,128)(2,1)} %collective-permute-done.8.refs_3_), channel_id=1, source_target_pairs={{0,4},{1,5},{4,8},{5,9},{8,12},{9,13},{12,14},{13,15},{14,10},{15,... | collective-permute-start | bytes 884744 | tf_op jit(solution)/shard_map/ppermute | solution.py:384
  25.0 0.5 collective-permute-start.10
  25.5 1.9 %pad_maximum_fusion.refs_0_ = bf16[192,1280]{1,0:T(8,128)(2,1)} fusion(bf16[192,512]{1,0:T(8,128)(2,1)} %param.9, bf16[192,384]{1,0:T(8,128)(2,1)} %collective-permute-done.2, bf16[192,384]{1,0:T(8,128)(2,1)} %get-tuple-element.35), kind=kLoop, calls=%fused_computation.2 | loop fusion | flops 1474560 | bytes 983040 | tf_op jit(solution)/shard_map/concatenate | solution.py:429
  27.4 1.6 %collective-permute-start.5 = (bf16[192,1280]{1,0:T(8,128)(2,1)}, bf16[192,1280]{1,0:T(8,128)(2,1)}, u32[]{:S(2)}, u32[]{:S(2)}) collective-permute-start(bf16[192,1280]{1,0:T(8,128)(2,1)} %pad_maximum_fusion.refs_0_), channel_id=1, source_target_pairs={{0,4},{1,5},{4,8},{5,9},{8,12},{9,13},{12,14},{13,15},{14,10},{15,... | collective-permute-start | bytes 1474568 | tf_op jit(solution)/shard_map/ppermute | solution.py:384
  28.9 0.5 collective-permute-start.6
  29.5 4.1 %collective-permute-done.9.refs_5_ = bf16[192,768]{1,0:T(8,128)(2,1)S(1)} collective-permute-done((bf16[192,768]{1,0:T(8,128)(2,1)}, bf16[192,768]{1,0:T(8,128)(2,1)S(1)}, u32[]{:S(2)}, u32[]{:S(2)}) %collective-permute-start.9) | collective-permute-done | bytes 294944 | tf_op jit(solution)/shard_map/ppermute | solution.py:384
  33.6 1.7 %collective-permute-done.10.refs_6_ = bf16[192,768]{1,0:T(8,128)(2,1)} collective-permute-done((bf16[192,768]{1,0:T(8,128)(2,1)}, bf16[192,768]{1,0:T(8,128)(2,1)}, u32[]{:S(2)}, u32[]{:S(2)}) %collective-permute-start.10) | collective-permute-done | bytes 294944 | tf_op jit(solution)/shard_map/ppermute | solution.py:385
  35.3 1.6 %collective-permute-start.15 = (bf16[192,768]{1,0:T(8,128)(2,1)S(1)}, bf16[192,768]{1,0:T(8,128)(2,1)S(1)}, u32[]{:S(2)}, u32[]{:S(2)}) collective-permute-start(bf16[192,768]{1,0:T(8,128)(2,1)S(1)} %broadcast_select_fusion.1), channel_id=1, source_target_pairs={{0,4},{4,8},{8,12},{12,14},{14,10},{10,6},{6,2},{2,0},{5,1},{9,5},... | collective-permute-start | bytes 884744 | tf_op jit(solution)/shard_map/ppermute | solution.py:396
  36.9 1.0 copy-done.5
  37.9 5.8 %temporal_projection.1.most_ref = f32[1024,384]{1,0:T(8,128)S(1)} custom-call(s32[10]{0:T(128)S(1)} %pad_add_fusion.meta_ref, bf16[512,3072]{1,0:T(8,128)(2,1)S(1)} %bitcast.28, bf16[512,3072]{1,0:T(8,128)(2,1)} %collective-permute-done.1.other_ref, bf16[192,768]{1,0:T(8,128)(2,1)S(1)} %copy-done.5, bf16[192,768]{1,0:T(8,128)(2,1)} %collective-permute-done.7.refs_1_, ...), custom_call_target="tpu_custom_call" | custom-call | flops 2415919104 | bytes 8355880 | tf_op jit(solution)/shard_map/temporal_projection/pallas_call | solution.py:28
  43.7 2.0 %collective-permute-done.6.refs_2_ = bf16[192,1280]{1,0:T(8,128)(2,1)} collective-permute-done((bf16[192,1280]{1,0:T(8,128)(2,1)}, bf16[192,1280]{1,0:T(8,128)(2,1)}, u32[]{:S(2)}, u32[]{:S(2)}) %collective-permute-start.6) | collective-permute-done | bytes 491552 | tf_op jit(solution)/shard_map/ppermute | solution.py:385
  45.8 1.6 %collective-permute-start.11 = (bf16[192,1280]{1,0:T(8,128)(2,1)}, bf16[192,1280]{1,0:T(8,128)(2,1)}, u32[]{:S(2)}, u32[]{:S(2)}) collective-permute-start(bf16[192,1280]{1,0:T(8,128)(2,1)} %collective-permute-done.5.refs_1_), channel_id=1, source_target_pairs={{0,4},{1,5},{4,8},{5,9},{8,12},{9,13},{12,14},{13,15},{14,10},{15,... | collective-permute-start | bytes 1474568 | tf_op jit(solution)/shard_map/ppermute | solution.py:384
  47.4 0.4 collective-permute-start.12
  47.8 2.0 %temporal_projection_rest.1 = bf16[8,2,2,32,384]{4,3,2,1,0:T(8,128)(2,1)S(1)} custom-call(s32[10]{0:T(128)S(1)} %pad_add_fusion.meta_ref, bf16[512,3072]{1,0:T(8,128)(2,1)S(1)} %bitcast.29, bf16[512,3072]{1,0:T(8,128)(2,1)} %collective-permute-done.1.other_ref, f32[1024,384]{1,0:T(8,128)S(1)} %temporal_projection.1.most_ref, ...), custom_call_target="tpu_custom_call" | custom-call | flops 301989888 | bytes 8159272 | tf_op jit(solution)/shard_map/temporal_projection_rest/pallas_call | solution.py:28
  49.9 0.9 copy-done.3
  50.8 5.5 %all-to-all-start = ((bf16[8,2,2,32,384]{4,3,2,1,0:T(8,128)(2,1)}), bf16[8,2,2,32,384]{4,3,2,1,0:T(8,128)(2,1)}, u32[]{:S(2)}, u32[]{:S(2)}) async-start(bf16[8,2,2,32,384]{4,3,2,1,0:T(8,128)(2,1)} %copy-done.3), calls=%async_computation | async-start | bytes 1572864 | tf_op jit(solution)/shard_map/all_to_all | solution.py:494
  56.4 2.0 %collective-permute-start.13 = (bf16[192,1280]{1,0:T(8,128)(2,1)}, bf16[192,1280]{1,0:T(8,128)(2,1)}, u32[]{:S(2)}, u32[]{:S(2)}) collective-permute-start(bf16[192,1280]{1,0:T(8,128)(2,1)} %collective-permute-done.11.refs_3_.refs_0_), channel_id=1, source_target_pairs={{0,4},{1,5},{4,8},{5,9},{8,12},{9,13},{12,14},{13,15},{14,10},{15,... | collective-permute-start | bytes 1474568 | tf_op jit(solution)/shard_map/ppermute | solution.py:384
  58.4 0.2 collective-permute-start.14
  58.8 2.0 %pack_out_weight.4.refs_0_ = bf16[3,192,512]{2,1,0:T(8,128)(2,1)} custom-call(bf16[192,1280]{1,0:T(8,128)(2,1)} %pad_maximum_fusion.refs_0_, bf16[192,1280]{1,0:T(8,128)(2,1)} %collective-permute-done.5.refs_1_, bf16[192,1280]{1,0:T(8,128)(2,1)} %collective-permute-done.6.refs_2_), custom_call_target="tpu_custom_call" | custom-call | flops 1000000000 | bytes 1474560 | tf_op jit(solution)/shard_map/pack_out_weight/pallas_call | solution.py:28
  60.8 1.6 %collective-permute-start.16 = (bf16[3,192,512]{2,1,0:T(8,128)(2,1)}, bf16[3,192,512]{2,1,0:T(8,128)(2,1)}, u32[]{:S(2)}, u32[]{:S(2)}) collective-permute-start(bf16[3,192,512]{2,1,0:T(8,128)(2,1)} %pack_out_weight.4.refs_0_), channel_id=1, source_target_pairs={{0,16},{16,0},{1,17},{17,1},{2,18},{18,2},{3,19},{19,3},{4,20},{20... | collective-permute-start | bytes 1769480 | tf_op jit(solution)/shard_map/ppermute | solution.py:375
  62.4 1.8 %pack_out_weight.5.refs_1_ = bf16[2,192,512]{2,1,0:T(8,128)(2,1)} custom-call(bf16[192,1280]{1,0:T(8,128)(2,1)} %collective-permute-done.11.refs_3_.refs_0_, bf16[192,1280]{1,0:T(8,128)(2,1)} %collective-permute-done.12.refs_4_.refs_1_), custom_call_target="tpu_custom_call" | custom-call | flops 1000000000 | bytes 983040 | tf_op jit(solution)/shard_map/pack_out_weight/pallas_call | solution.py:28
  64.2 0.6 collective-permute-start.17
  64.8 7.1 %spatial_projection.1.most_ref = f32[1024,384]{1,0:T(8,128)S(1)} custom-call(s32[10]{0:T(128)S(1)} %pad_add_fusion.meta_ref, bf16[512,3072]{1,0:T(8,128)(2,1)S(1)} %bitcast.30, bf16[512,3072]{1,0:T(8,128)(2,1)} %collective-permute-done.1.other_ref, bf16[192,1280]{1,0:T(8,128)(2,1)} %pad_maximum_fusion.refs_0_, ...), custom_call_target="tpu_custom_call" | custom-call | bytes 8749096 | tf_op jit(solution)/shard_map/spatial_projection/pallas_call | solution.py:28
  71.9 1.1 copy-done.1
  73.0 4.9 %collective-permute-done.13.refs_0_ = bf16[192,1280]{1,0:T(8,128)(2,1)} collective-permute-done((bf16[192,1280]{1,0:T(8,128)(2,1)}, bf16[192,1280]{1,0:T(8,128)(2,1)}, u32[]{:S(2)}, u32[]{:S(2)}) %collective-permute-start.13) | collective-permute-done | bytes 491552 | tf_op jit(solution)/shard_map/ppermute | solution.py:384
  77.9 2.1 %collective-permute-done.14.refs_1_ = bf16[192,1280]{1,0:T(8,128)(2,1)} collective-permute-done((bf16[192,1280]{1,0:T(8,128)(2,1)}, bf16[192,1280]{1,0:T(8,128)(2,1)}, u32[]{:S(2)}, u32[]{:S(2)}) %collective-permute-start.14) | collective-permute-done | bytes 491552 | tf_op jit(solution)/shard_map/ppermute | solution.py:385
  80.0 1.9 %broadcast_select_fusion = bf16[192,1280]{1,0:T(8,128)(2,1)} fusion(bf16[192,1280]{1,0:T(8,128)(2,1)} %collective-permute-done.13.refs_0_, bf16[192,1280]{1,0:T(8,128)(2,1)} %collective-permute-done.14.refs_1_, pred[]{:T(512)S(6)} %eq.6), kind=kLoop, calls=%fused_computation.3 | loop fusion | flops 245760 | bytes 1474561 | tf_op jit(solution)/shard_map/jit(_where)/select_n | solution.py:390
  81.9 2.7 %temporal_attention.1 = bf16[2,16,32,128]{3,2,1,0:T(8,128)(2,1)} custom-call(s32[17]{0:T(128)S(1)} %pad_add_fusion.1.meta_ref, bf16[16,64,384]{2,1,0:T(8,128)(2,1)} %bitcast.9.qkv_ref), custom_call_target="tpu_custom_call" | custom-call | flops 5000000000 | bytes 786500 | tf_op jit(solution)/shard_map/temporal_attention/pallas_call | solution.py:28
  84.6 5.9 %collective-permute-start.18 = (bf16[192,1280]{1,0:T(8,128)(2,1)}, bf16[192,1280]{1,0:T(8,128)(2,1)}, u32[]{:S(2)}, u32[]{:S(2)}) collective-permute-start(bf16[192,1280]{1,0:T(8,128)(2,1)} %broadcast_select_fusion), channel_id=1, source_target_pairs={{0,4},{4,8},{8,12},{12,14},{14,10},{10,6},{6,2},{2,0},{5,1},{9,5},... | collective-permute-start | bytes 1474568 | tf_op jit(solution)/shard_map/ppermute | solution.py:396
  90.5 1.8 %pack_out_weight.6.refs_2_ = bf16[2,192,512]{2,1,0:T(8,128)(2,1)} custom-call(bf16[192,1280]{1,0:T(8,128)(2,1)} %collective-permute-done.13.refs_0_, bf16[192,1280]{1,0:T(8,128)(2,1)} %collective-permute-done.14.refs_1_), custom_call_target="tpu_custom_call" | custom-call | flops 1000000000 | bytes 983040 | tf_op jit(solution)/shard_map/pack_out_weight/pallas_call | solution.py:28
  92.3 1.6 %collective-permute-start.26 = (bf16[2,192,512]{2,1,0:T(8,128)(2,1)}, bf16[2,192,512]{2,1,0:T(8,128)(2,1)}, u32[]{:S(2)}, u32[]{:S(2)}) collective-permute-start(bf16[2,192,512]{2,1,0:T(8,128)(2,1)} %pack_out_weight.6.refs_2_), channel_id=1, source_target_pairs={{0,16},{16,0},{1,17},{17,1},{2,18},{18,2},{3,19},{19,3},{4,20},{20... | collective-permute-start | bytes 1179656 | tf_op jit(solution)/shard_map/ppermute | solution.py:375
  93.8 2.7 %all-to-all-start.1 = ((bf16[32,32,128]{2,1,0:T(8,128)(2,1)}), bf16[32,32,128]{2,1,0:T(8,128)(2,1)S(1)}, u32[]{:S(2)}, u32[]{:S(2)}) async-start(bf16[32,32,128]{2,1,0:T(8,128)(2,1)} %bitcast.14), calls=%async_computation.1 | async-start | bytes 524288 | tf_op jit(solution)/shard_map/all_to_all | solution.py:521
  96.5 0.6 collective-permute-done.18.refs_2_.refs_0_
  97.1 1.6 %pack_out_weight.7.refs_3_ = bf16[1,192,512]{2,1,0:T(8,128)(2,1)} custom-call(bf16[192,1280]{1,0:T(8,128)(2,1)} %collective-permute-done.18.refs_2_.refs_0_), custom_call_target="tpu_custom_call" | custom-call | flops 1000000000 | bytes 491520 | tf_op jit(solution)/shard_map/pack_out_weight/pallas_call | solution.py:28
  98.8 1.6 %collective-permute-start.27 = (bf16[1,192,512]{2,1,0:T(8,128)(2,1)}, bf16[1,192,512]{2,1,0:T(8,128)(2,1)}, u32[]{:S(2)}, u32[]{:S(2)}) collective-permute-start(bf16[1,192,512]{2,1,0:T(8,128)(2,1)} %pack_out_weight.7.refs_3_), channel_id=1, source_target_pairs={{0,16},{16,0},{1,17},{17,1},{2,18},{18,2},{3,19},{19,3},{4,20},{20... | collective-permute-start | bytes 589832 | tf_op jit(solution)/shard_map/ppermute | solution.py:375
  100.3 0.5 collective-permute-start.24
  100.8 1.4 %copy-done.2 = f32[1024,384]{1,0:T(8,128)S(1)} copy-done((f32[1024,384]{1,0:T(8,128)S(1)}, f32[1024,384]{1,0:T(8,128)}, u32[]{:S(2)}) %copy-start.2) | copy-done | bytes 1572888
  102.2 4.8 %spatial_heads.1 = bf16[2,2,256,128]{3,2,1,0:T(8,128)(2,1)S(1)} custom-call(s32[10]{0:T(128)S(1)} %pad_add_fusion.meta_ref, bf16[512,3072]{1,0:T(8,128)(2,1)S(1)} %bitcast.31, bf16[512,3072]{1,0:T(8,128)(2,1)} %collective-permute-done.1.other_ref, f32[1024,384]{1,0:T(8,128)S(1)} %copy-done.2, bf16[192,1280]{1,0:T(8,128)(2,1)} %collective-permute-done.13.refs_0_, ...), custom_call_target="tpu_custom_call" | custom-call | bytes 9338920 | tf_op jit(solution)/shard_map/spatial_heads/pallas_call | solution.py:28
  107.1 0.4 collective-permute-done.27.refs_11_
  107.5 0.7 slice_bitcast_fusion
  108.1 1.6 %collective-permute-start.21 = (bf16[256,128]{1,0:T(8,128)(2,1)S(1)}, bf16[256,128]{1,0:T(8,128)(2,1)S(1)}, u32[]{:S(2)}, u32[]{:S(2)}) collective-permute-start(bf16[256,128]{1,0:T(8,128)(2,1)S(1)} %get-tuple-element.39), channel_id=1, source_target_pairs={{0,17},{1,16},{2,19},{3,18},{4,21},{5,20},{6,23},{7,22},{8,25},{9,... | collective-permute-start | bytes 196616 | tf_op jit(solution)/shard_map/ppermute | solution.py:576
  109.7 0.6 collective-permute-start.19
  110.5 1.6 %collective-permute-done.21.far_ref = bf16[256,128]{1,0:T(8,128)(2,1)S(1)} collective-permute-done((bf16[256,128]{1,0:T(8,128)(2,1)S(1)}, bf16[256,128]{1,0:T(8,128)(2,1)S(1)}, u32[]{:S(2)}, u32[]{:S(2)}) %collective-permute-start.21) | collective-permute-done | bytes 65568 | tf_op jit(solution)/shard_map/ppermute | solution.py:576
  112.3 0.3 collective-permute-start.29
  112.6 1.6 %collective-permute-done.19.peer_ref = bf16[256,128]{1,0:T(8,128)(2,1)S(1)} collective-permute-done((bf16[256,128]{1,0:T(8,128)(2,1)S(1)}, bf16[256,128]{1,0:T(8,128)(2,1)S(1)}, u32[]{:S(2)}, u32[]{:S(2)}) %collective-permute-start.19) | collective-permute-done | bytes 65568 | tf_op jit(solution)/shard_map/ppermute | solution.py:375
  114.4 0.5 copy-done.19
  114.9 0.7 copy-done.6
  115.6 0.7 collective-permute-done.30.refs_14_
  116.4 0.6 copy-done.14
  117.2 6.5 %out_projection.1 = bf16[256,3072]{1,0:T(8,128)(2,1)} custom-call(s32[10]{0:T(128)} %copy-done.7, bf16[256,128]{1,0:T(8,128)(2,1)} %get-tuple-element.42.mine_ref, bf16[256,128]{1,0:T(8,128)(2,1)} %copy-done.19, bf16[256,128]{1,0:T(8,128)(2,1)} %copy-done.18, bf16[256,128]{1,0:T(8,128)(2,1)} %copy-done.17, bf16[2,256,256]{2,1,0:T(8,128)(2,1)} %copy-done.6, ...), custom_call_target="tpu_custom_call" | custom-call | flops 1610612736 | bytes 6815784 | tf_op jit(solution)/shard_map/out_projection/pallas_call | solution.py:28
  (78 shorter events, 1.5 us)
Async XLA Ops:
  0.0 3.7 %copy-start = (bf16[1,512,3072]{2,1,0:T(8,128)(2,1)S(1)}, bf16[1,512,3072]{2,1,0:T(8,128)(2,1)}, u32[]{:S(2)}) copy-start(bf16[1,512,3072]{2,1,0:T(8,128)(2,1)} %param.7) | copy-start | bytes 9437188
  0.0 6.9 %copy-start.21 = (s32[8]{0:T(128)S(1)}, s32[8]{0:T(128)}, u32[]{:S(2)}) copy-start(s32[8]{0:T(128)} %constant.67.clone) | copy-start | bytes 100
  1.3 15.9 %copy-start.8 = (s32[8]{0:T(128)S(1)}, s32[8]{0:T(128)}, u32[]{:S(2)}) copy-start(s32[8]{0:T(128)} %constant.68.clone) | copy-start | bytes 100
  2.1 1.5 %collective-permute-start = (bf16[192,384]{1,0:T(8,128)(2,1)S(1)}, bf16[192,384]{1,0:T(8,128)(2,1)S(1)}, u32[]{:S(2)}, u32[]{:S(2)}) collective-permute-start(bf16[192,384]{1,0:T(8,128)(2,1)S(1)} %get-tuple-element.38), channel_id=1, source_target_pairs={{0,1},{1,0},{2,3},{3,2},{4,5},{5,4},{6,7},{7,6},{8,9},{9,8},{10,11... | collective-permute-start | bytes 442376 | tf_op jit(solution)/shard_map/ppermute | solution.py:372
  3.7 14.2 %copy-start.4 = (bf16[192,768]{1,0:T(8,128)(2,1)}, bf16[192,768]{1,0:T(8,128)(2,1)S(1)}, u32[]{:S(2)}) copy-start(bf16[192,768]{1,0:T(8,128)(2,1)S(1)} %pad_maximum_fusion.1.refs_0_) | copy-start | bytes 884740
  3.7 33.2 %collective-permute-start.1 = (bf16[512,3072]{1,0:T(8,128)(2,1)S(1)}, bf16[512,3072]{1,0:T(8,128)(2,1)}, u32[]{:S(2)}, u32[]{:S(2)}) collective-permute-start(bf16[512,3072]{1,0:T(8,128)(2,1)S(1)} %bitcast.27), channel_id=1, source_target_pairs={{0,1},{1,0},{2,3},{3,2},{4,5},{5,4},{6,7},{7,6},{8,9},{9,8},{10,11... | collective-permute-start | bytes 9437192 | tf_op jit(solution)/shard_map/ppermute | solution.py:372
  4.1 10.3 %collective-permute-start.7 = (bf16[192,768]{1,0:T(8,128)(2,1)S(1)}, bf16[192,768]{1,0:T(8,128)(2,1)}, u32[]{:S(2)}, u32[]{:S(2)}) collective-permute-start(bf16[192,768]{1,0:T(8,128)(2,1)S(1)} %pad_maximum_fusion.1.refs_0_), channel_id=1, source_target_pairs={{0,4},{1,5},{4,8},{5,9},{8,12},{9,13},{12,14},{13,15},{14,10},{15,... | collective-permute-start | bytes 884744 | tf_op jit(solution)/shard_map/ppermute | solution.py:384
  6.9 9.4 %collective-permute-start.3 = (bf16[192,768]{1,0:T(8,128)(2,1)S(1)}, bf16[192,768]{1,0:T(8,128)(2,1)}, u32[]{:S(2)}, u32[]{:S(2)}) collective-permute-start(bf16[192,768]{1,0:T(8,128)(2,1)S(1)} %pad_maximum_fusion.1.refs_0_), channel_id=1, source_target_pairs={{4,0},{5,1},{8,4},{9,5},{12,8},{13,9},{14,12},{15,13},{10,14},{11,... | collective-permute-start | bytes 884744 | tf_op jit(solution)/shard_map/ppermute | solution.py:385
  9.3 16.2 %collective-permute-start.2 = (bf16[192,384]{1,0:T(8,128)(2,1)}, bf16[192,384]{1,0:T(8,128)(2,1)}, u32[]{:S(2)}, u32[]{:S(2)}) collective-permute-start(bf16[192,384]{1,0:T(8,128)(2,1)} %get-tuple-element.36), channel_id=1, source_target_pairs={{0,1},{1,0},{2,3},{3,2},{4,5},{5,4},{6,7},{7,6},{8,9},{9,8},{10,11... | collective-permute-start | bytes 442376 | tf_op jit(solution)/shard_map/ppermute | solution.py:372
  14.4 9.0 %collective-permute-start.8 = (bf16[192,768]{1,0:T(8,128)(2,1)}, bf16[192,768]{1,0:T(8,128)(2,1)}, u32[]{:S(2)}, u32[]{:S(2)}) collective-permute-start(bf16[192,768]{1,0:T(8,128)(2,1)} %collective-permute-done.7.refs_1_), channel_id=1, source_target_pairs={{0,4},{1,5},{4,8},{5,9},{8,12},{9,13},{12,14},{13,15},{14,10},{15,... | collective-permute-start | bytes 884744 | tf_op jit(solution)/shard_map/ppermute | solution.py:384
  16.2 8.8 %collective-permute-start.4 = (bf16[192,768]{1,0:T(8,128)(2,1)}, bf16[192,768]{1,0:T(8,128)(2,1)}, u32[]{:S(2)}, u32[]{:S(2)}) collective-permute-start(bf16[192,768]{1,0:T(8,128)(2,1)} %collective-permute-done.3.refs_2_), channel_id=1, source_target_pairs={{4,0},{5,1},{8,4},{9,5},{12,8},{13,9},{14,12},{15,13},{10,14},{11,... | collective-permute-start | bytes 884744 | tf_op jit(solution)/shard_map/ppermute | solution.py:385
  23.4 10.2 %collective-permute-start.9 = (bf16[192,768]{1,0:T(8,128)(2,1)}, bf16[192,768]{1,0:T(8,128)(2,1)S(1)}, u32[]{:S(2)}, u32[]{:S(2)}) collective-permute-start(bf16[192,768]{1,0:T(8,128)(2,1)} %collective-permute-done.8.refs_3_), channel_id=1, source_target_pairs={{0,4},{1,5},{4,8},{5,9},{8,12},{9,13},{12,14},{13,15},{14,10},{15,... | collective-permute-start | bytes 884744 | tf_op jit(solution)/shard_map/ppermute | solution.py:384
  25.0 10.3 %collective-permute-start.10 = (bf16[192,768]{1,0:T(8,128)(2,1)}, bf16[192,768]{1,0:T(8,128)(2,1)}, u32[]{:S(2)}, u32[]{:S(2)}) collective-permute-start(bf16[192,768]{1,0:T(8,128)(2,1)} %collective-permute-done.4.refs_4_), channel_id=1, source_target_pairs={{4,0},{5,1},{8,4},{9,5},{12,8},{13,9},{14,12},{15,13},{10,14},{11,... | collective-permute-start | bytes 884744 | tf_op jit(solution)/shard_map/ppermute | solution.py:385
  27.4 16.4 %collective-permute-start.5 = (bf16[192,1280]{1,0:T(8,128)(2,1)}, bf16[192,1280]{1,0:T(8,128)(2,1)}, u32[]{:S(2)}, u32[]{:S(2)}) collective-permute-start(bf16[192,1280]{1,0:T(8,128)(2,1)} %pad_maximum_fusion.refs_0_), channel_id=1, source_target_pairs={{0,4},{1,5},{4,8},{5,9},{8,12},{9,13},{12,14},{13,15},{14,10},{15,... | collective-permute-start | bytes 1474568 | tf_op jit(solution)/shard_map/ppermute | solution.py:384
  28.9 16.9 %collective-permute-start.6 = (bf16[192,1280]{1,0:T(8,128)(2,1)}, bf16[192,1280]{1,0:T(8,128)(2,1)}, u32[]{:S(2)}, u32[]{:S(2)}) collective-permute-start(bf16[192,1280]{1,0:T(8,128)(2,1)} %pad_maximum_fusion.refs_0_), channel_id=1, source_target_pairs={{4,0},{5,1},{8,4},{9,5},{12,8},{13,9},{14,12},{15,13},{10,14},{11,... | collective-permute-start | bytes 1474568 | tf_op jit(solution)/shard_map/ppermute | solution.py:385
  29.5 71.4 %copy-start.7 = (s32[10]{0:T(128)}, s32[10]{0:T(128)S(1)}, u32[]{:S(2)}) copy-start(s32[10]{0:T(128)S(1)} %pad_add_fusion.meta_ref) | copy-start | bytes 124
  35.3 12.5 %collective-permute-start.15 = (bf16[192,768]{1,0:T(8,128)(2,1)S(1)}, bf16[192,768]{1,0:T(8,128)(2,1)S(1)}, u32[]{:S(2)}, u32[]{:S(2)}) collective-permute-start(bf16[192,768]{1,0:T(8,128)(2,1)S(1)} %broadcast_select_fusion.1), channel_id=1, source_target_pairs={{0,4},{4,8},{8,12},{12,14},{14,10},{10,6},{6,2},{2,0},{5,1},{9,5},... | collective-permute-start | bytes 884744 | tf_op jit(solution)/shard_map/ppermute | solution.py:396
  36.9 1.0 copy-start.5
  45.8 10.6 %collective-permute-start.11 = (bf16[192,1280]{1,0:T(8,128)(2,1)}, bf16[192,1280]{1,0:T(8,128)(2,1)}, u32[]{:S(2)}, u32[]{:S(2)}) collective-permute-start(bf16[192,1280]{1,0:T(8,128)(2,1)} %collective-permute-done.5.refs_1_), channel_id=1, source_target_pairs={{0,4},{1,5},{4,8},{5,9},{8,12},{9,13},{12,14},{13,15},{14,10},{15,... | collective-permute-start | bytes 1474568 | tf_op jit(solution)/shard_map/ppermute | solution.py:384
  47.4 11.1 %collective-permute-start.12 = (bf16[192,1280]{1,0:T(8,128)(2,1)}, bf16[192,1280]{1,0:T(8,128)(2,1)}, u32[]{:S(2)}, u32[]{:S(2)}) collective-permute-start(bf16[192,1280]{1,0:T(8,128)(2,1)} %collective-permute-done.6.refs_2_), channel_id=1, source_target_pairs={{4,0},{5,1},{8,4},{9,5},{12,8},{13,9},{14,12},{15,13},{10,14},{11,... | collective-permute-start | bytes 1474568 | tf_op jit(solution)/shard_map/ppermute | solution.py:385
  49.9 0.9 copy-start.3
  50.8 5.5 %copy-start.20 = (s32[16]{0:T(128)S(1)}, s32[16]{0:T(128)}, u32[]{:S(2)}) copy-start(s32[16]{0:T(128)} %param.10) | copy-start | bytes 196
  50.8 31.2 %all-to-all-start = ((bf16[8,2,2,32,384]{4,3,2,1,0:T(8,128)(2,1)}), bf16[8,2,2,32,384]{4,3,2,1,0:T(8,128)(2,1)}, u32[]{:S(2)}, u32[]{:S(2)}) async-start(bf16[8,2,2,32,384]{4,3,2,1,0:T(8,128)(2,1)} %copy-done.3), calls=%async_computation | async-start | bytes 1572864 | tf_op jit(solution)/shard_map/all_to_all | solution.py:494
  56.4 21.5 %collective-permute-start.13 = (bf16[192,1280]{1,0:T(8,128)(2,1)}, bf16[192,1280]{1,0:T(8,128)(2,1)}, u32[]{:S(2)}, u32[]{:S(2)}) collective-permute-start(bf16[192,1280]{1,0:T(8,128)(2,1)} %collective-permute-done.11.refs_3_.refs_0_), channel_id=1, source_target_pairs={{0,4},{1,5},{4,8},{5,9},{8,12},{9,13},{12,14},{13,15},{14,10},{15,... | collective-permute-start | bytes 1474568 | tf_op jit(solution)/shard_map/ppermute | solution.py:384
  58.4 21.6 %collective-permute-start.14 = (bf16[192,1280]{1,0:T(8,128)(2,1)}, bf16[192,1280]{1,0:T(8,128)(2,1)}, u32[]{:S(2)}, u32[]{:S(2)}) collective-permute-start(bf16[192,1280]{1,0:T(8,128)(2,1)} %collective-permute-done.12.refs_4_.refs_1_), channel_id=1, source_target_pairs={{4,0},{5,1},{8,4},{9,5},{12,8},{13,9},{14,12},{15,13},{10,14},{11,... | collective-permute-start | bytes 1474568 | tf_op jit(solution)/shard_map/ppermute | solution.py:385
  60.8 23.8 %collective-permute-start.16 = (bf16[3,192,512]{2,1,0:T(8,128)(2,1)}, bf16[3,192,512]{2,1,0:T(8,128)(2,1)}, u32[]{:S(2)}, u32[]{:S(2)}) collective-permute-start(bf16[3,192,512]{2,1,0:T(8,128)(2,1)} %pack_out_weight.4.refs_0_), channel_id=1, source_target_pairs={{0,16},{16,0},{1,17},{17,1},{2,18},{18,2},{3,19},{19,3},{4,20},{20... | collective-permute-start | bytes 1769480 | tf_op jit(solution)/shard_map/ppermute | solution.py:375
  64.2 20.4 %collective-permute-start.17 = (bf16[2,192,512]{2,1,0:T(8,128)(2,1)}, bf16[2,192,512]{2,1,0:T(8,128)(2,1)}, u32[]{:S(2)}, u32[]{:S(2)}) collective-permute-start(bf16[2,192,512]{2,1,0:T(8,128)(2,1)} %pack_out_weight.5.refs_1_), channel_id=1, source_target_pairs={{0,16},{16,0},{1,17},{17,1},{2,18},{18,2},{3,19},{19,3},{4,20},{20... | collective-permute-start | bytes 1179656 | tf_op jit(solution)/shard_map/ppermute | solution.py:375
  71.8 1.1 copy-start.1
  84.6 12.6 %collective-permute-start.18 = (bf16[192,1280]{1,0:T(8,128)(2,1)}, bf16[192,1280]{1,0:T(8,128)(2,1)}, u32[]{:S(2)}, u32[]{:S(2)}) collective-permute-start(bf16[192,1280]{1,0:T(8,128)(2,1)} %broadcast_select_fusion), channel_id=1, source_target_pairs={{0,4},{4,8},{8,12},{12,14},{14,10},{10,6},{6,2},{2,0},{5,1},{9,5},... | collective-permute-start | bytes 1474568 | tf_op jit(solution)/shard_map/ppermute | solution.py:396
  92.3 14.8 %collective-permute-start.26 = (bf16[2,192,512]{2,1,0:T(8,128)(2,1)}, bf16[2,192,512]{2,1,0:T(8,128)(2,1)}, u32[]{:S(2)}, u32[]{:S(2)}) collective-permute-start(bf16[2,192,512]{2,1,0:T(8,128)(2,1)} %pack_out_weight.6.refs_2_), channel_id=1, source_target_pairs={{0,16},{16,0},{1,17},{17,1},{2,18},{18,2},{3,19},{19,3},{4,20},{20... | collective-permute-start | bytes 1179656 | tf_op jit(solution)/shard_map/ppermute | solution.py:375
  93.8 15.9 %collective-permute-start.22 = (bf16[3,192,512]{2,1,0:T(8,128)(2,1)}, bf16[3,192,512]{2,1,0:T(8,128)(2,1)}, u32[]{:S(2)}, u32[]{:S(2)}) collective-permute-start(bf16[3,192,512]{2,1,0:T(8,128)(2,1)} %pack_out_weight.4.refs_0_), channel_id=1, source_target_pairs={{0,1},{1,0},{2,3},{3,2},{4,5},{5,4},{6,7},{7,6},{8,9},{9,8},{10,11... | collective-permute-start | bytes 1769480 | tf_op jit(solution)/shard_map/ppermute | solution.py:372
  93.8 20.5 %all-to-all-start.1 = ((bf16[32,32,128]{2,1,0:T(8,128)(2,1)}), bf16[32,32,128]{2,1,0:T(8,128)(2,1)S(1)}, u32[]{:S(2)}, u32[]{:S(2)}) async-start(bf16[32,32,128]{2,1,0:T(8,128)(2,1)} %bitcast.14), calls=%async_computation.1 | async-start | bytes 524288 | tf_op jit(solution)/shard_map/all_to_all | solution.py:521
  96.5 3.8 %copy-start.10 = (bf16[2,192,512]{2,1,0:T(8,128)(2,1)S(1)}, bf16[2,192,512]{2,1,0:T(8,128)(2,1)}, u32[]{:S(2)}) copy-start(bf16[2,192,512]{2,1,0:T(8,128)(2,1)} %pack_out_weight.5.refs_1_) | copy-start | bytes 1179652
  98.8 8.7 %collective-permute-start.27 = (bf16[1,192,512]{2,1,0:T(8,128)(2,1)}, bf16[1,192,512]{2,1,0:T(8,128)(2,1)}, u32[]{:S(2)}, u32[]{:S(2)}) collective-permute-start(bf16[1,192,512]{2,1,0:T(8,128)(2,1)} %pack_out_weight.7.refs_3_), channel_id=1, source_target_pairs={{0,16},{16,0},{1,17},{17,1},{2,18},{18,2},{3,19},{19,3},{4,20},{20... | collective-permute-start | bytes 589832 | tf_op jit(solution)/shard_map/ppermute | solution.py:375
  100.3 9.4 %collective-permute-start.23 = (bf16[2,192,512]{2,1,0:T(8,128)(2,1)S(1)}, bf16[2,192,512]{2,1,0:T(8,128)(2,1)S(1)}, u32[]{:S(2)}, u32[]{:S(2)}) collective-permute-start(bf16[2,192,512]{2,1,0:T(8,128)(2,1)S(1)} %copy-done.10), channel_id=1, source_target_pairs={{0,1},{1,0},{2,3},{3,2},{4,5},{5,4},{6,7},{7,6},{8,9},{9,8},{10,11... | collective-permute-start | bytes 1179656 | tf_op jit(solution)/shard_map/ppermute | solution.py:372
  100.3 10.0 %collective-permute-start.24 = (bf16[2,192,512]{2,1,0:T(8,128)(2,1)}, bf16[2,192,512]{2,1,0:T(8,128)(2,1)S(1)}, u32[]{:S(2)}, u32[]{:S(2)}) collective-permute-start(bf16[2,192,512]{2,1,0:T(8,128)(2,1)} %pack_out_weight.6.refs_2_), channel_id=1, source_target_pairs={{0,1},{1,0},{2,3},{3,2},{4,5},{5,4},{6,7},{7,6},{8,9},{9,8},{10,11... | collective-permute-start | bytes 1179656 | tf_op jit(solution)/shard_map/ppermute | solution.py:372
  100.8 1.4 %copy-start.2 = (f32[1024,384]{1,0:T(8,128)S(1)}, f32[1024,384]{1,0:T(8,128)}, u32[]{:S(2)}) copy-start(f32[1024,384]{1,0:T(8,128)} %copy-done.1) | copy-start | bytes 4718596
  107.5 8.8 %collective-permute-start.28 = (bf16[3,192,512]{2,1,0:T(8,128)(2,1)}, bf16[3,192,512]{2,1,0:T(8,128)(2,1)S(1)}, u32[]{:S(2)}, u32[]{:S(2)}) collective-permute-start(bf16[3,192,512]{2,1,0:T(8,128)(2,1)} %collective-permute-done.16.refs_8_), channel_id=1, source_target_pairs={{0,1},{1,0},{2,3},{3,2},{4,5},{5,4},{6,7},{7,6},{8,9},{9,8},{10,11... | collective-permute-start | bytes 1769480 | tf_op jit(solution)/shard_map/ppermute | solution.py:372
  108.1 4.0 %collective-permute-start.21 = (bf16[256,128]{1,0:T(8,128)(2,1)S(1)}, bf16[256,128]{1,0:T(8,128)(2,1)S(1)}, u32[]{:S(2)}, u32[]{:S(2)}) collective-permute-start(bf16[256,128]{1,0:T(8,128)(2,1)S(1)} %get-tuple-element.39), channel_id=1, source_target_pairs={{0,17},{1,16},{2,19},{3,18},{4,21},{5,20},{6,23},{7,22},{8,25},{9,... | collective-permute-start | bytes 196616 | tf_op jit(solution)/shard_map/ppermute | solution.py:576
  109.7 2.6 %collective-permute-start.20 = (bf16[256,128]{1,0:T(8,128)(2,1)S(1)}, bf16[256,128]{1,0:T(8,128)(2,1)S(1)}, u32[]{:S(2)}, u32[]{:S(2)}) collective-permute-start(bf16[256,128]{1,0:T(8,128)(2,1)S(1)} %get-tuple-element.40), channel_id=1, source_target_pairs={{0,1},{1,0},{2,3},{3,2},{4,5},{5,4},{6,7},{7,6},{8,9},{9,8},{10,11... | collective-permute-start | bytes 196616 | tf_op jit(solution)/shard_map/ppermute | solution.py:372
  109.7 4.5 %copy-start.11 = (bf16[2,192,512]{2,1,0:T(8,128)(2,1)}, bf16[2,192,512]{2,1,0:T(8,128)(2,1)S(1)}, u32[]{:S(2)}) copy-start(bf16[2,192,512]{2,1,0:T(8,128)(2,1)S(1)} %collective-permute-done.23.refs_5_) | copy-start | bytes 1179652
  109.7 4.5 %collective-permute-start.19 = (bf16[256,128]{1,0:T(8,128)(2,1)S(1)}, bf16[256,128]{1,0:T(8,128)(2,1)S(1)}, u32[]{:S(2)}, u32[]{:S(2)}) collective-permute-start(bf16[256,128]{1,0:T(8,128)(2,1)S(1)} %get-tuple-element.41), channel_id=1, source_target_pairs={{0,16},{16,0},{1,17},{17,1},{2,18},{18,2},{3,19},{19,3},{4,20},{20... | collective-permute-start | bytes 196616 | tf_op jit(solution)/shard_map/ppermute | solution.py:375
  110.3 3.9 %copy-start.12 = (bf16[2,192,512]{2,1,0:T(8,128)(2,1)}, bf16[2,192,512]{2,1,0:T(8,128)(2,1)S(1)}, u32[]{:S(2)}) copy-start(bf16[2,192,512]{2,1,0:T(8,128)(2,1)S(1)} %collective-permute-done.24.refs_6_) | copy-start | bytes 1179652
  110.3 5.2 %collective-permute-start.25 = (bf16[1,192,512]{2,1,0:T(8,128)(2,1)}, bf16[1,192,512]{2,1,0:T(8,128)(2,1)S(1)}, u32[]{:S(2)}, u32[]{:S(2)}) collective-permute-start(bf16[1,192,512]{2,1,0:T(8,128)(2,1)} %pack_out_weight.7.refs_3_), channel_id=1, source_target_pairs={{0,1},{1,0},{2,3},{3,2},{4,5},{5,4},{6,7},{7,6},{8,9},{9,8},{10,11... | collective-permute-start | bytes 589832 | tf_op jit(solution)/shard_map/ppermute | solution.py:372
  112.1 2.3 %copy-start.17 = (bf16[256,128]{1,0:T(8,128)(2,1)}, bf16[256,128]{1,0:T(8,128)(2,1)S(1)}, u32[]{:S(2)}) copy-start(bf16[256,128]{1,0:T(8,128)(2,1)S(1)} %collective-permute-done.21.far_ref) | copy-start | bytes 196612
  112.1 3.4 %collective-permute-start.31 = (bf16[1,192,512]{2,1,0:T(8,128)(2,1)}, bf16[1,192,512]{2,1,0:T(8,128)(2,1)S(1)}, u32[]{:S(2)}, u32[]{:S(2)}) collective-permute-start(bf16[1,192,512]{2,1,0:T(8,128)(2,1)} %collective-permute-done.27.refs_11_), channel_id=1, source_target_pairs={{0,1},{1,0},{2,3},{3,2},{4,5},{5,4},{6,7},{7,6},{8,9},{9,8},{10,11... | collective-permute-start | bytes 589832 | tf_op jit(solution)/shard_map/ppermute | solution.py:372
  112.3 2.1 %copy-start.18 = (bf16[256,128]{1,0:T(8,128)(2,1)}, bf16[256,128]{1,0:T(8,128)(2,1)S(1)}, u32[]{:S(2)}) copy-start(bf16[256,128]{1,0:T(8,128)(2,1)S(1)} %collective-permute-done.20.core_ref) | copy-start | bytes 196612
  112.3 3.2 %collective-permute-start.29 = (bf16[2,192,512]{2,1,0:T(8,128)(2,1)}, bf16[2,192,512]{2,1,0:T(8,128)(2,1)S(1)}, u32[]{:S(2)}, u32[]{:S(2)}) collective-permute-start(bf16[2,192,512]{2,1,0:T(8,128)(2,1)} %collective-permute-done.17.refs_9_), channel_id=1, source_target_pairs={{0,1},{1,0},{2,3},{3,2},{4,5},{5,4},{6,7},{7,6},{8,9},{9,8},{10,11... | collective-permute-start | bytes 1179656 | tf_op jit(solution)/shard_map/ppermute | solution.py:372
  114.2 0.6 copy-start.19
  114.3 2.0 %collective-permute-start.30 = (bf16[2,192,512]{2,1,0:T(8,128)(2,1)}, bf16[2,192,512]{2,1,0:T(8,128)(2,1)S(1)}, u32[]{:S(2)}, u32[]{:S(2)}) collective-permute-start(bf16[2,192,512]{2,1,0:T(8,128)(2,1)} %collective-permute-done.26.refs_10_), channel_id=1, source_target_pairs={{0,1},{1,0},{2,3},{3,2},{4,5},{5,4},{6,7},{7,6},{8,9},{9,8},{10,11... | collective-permute-start | bytes 1179656 | tf_op jit(solution)/shard_map/ppermute | solution.py:372
  114.9 0.7 copy-start.6
  115.6 0.7 copy-start.15
  115.6 0.7 copy-start.16
  115.6 0.9 copy-start.13
  116.2 0.8 copy-start.14
  116.3 0.9 copy-start.9
